TPU v7x, 32 devices: a whole 2x2x4 slice. The times are simulated.
32 devices in a mesh: wide: 16 (over z, y, x), narrow: 2 (over core).
Axes of the slice: x: 2, y: 2, z: 4, core: 2. Of those that a mesh axis runs over, the one named last changes fastest.
Arguments:
- tag_inputs: bfloat16 [49152, 512], P(('wide', 'narrow')), may hold values from -7 to 7
- image_inputs: bfloat16 [75264, 512], P(('wide', 'narrow')), may hold values from -14 to 14
- tag_counts: int32 [96], P(('wide', 'narrow')), may hold values from 1 to 512, as said below
- cotangent: bfloat16 [49152, 512], P(('wide', 'narrow')), may hold values from -6 to 6
- weight_qkv: float32 [512, 1536], P(('wide', 'narrow')), may hold values from -0.25 to 0.25
- weight_out: float32 [512, 512], P(('wide', 'narrow')), may hold values from -6 to 6
- weight_up: float32 [512, 1024], P(('wide', 'narrow')), may hold values from -0.25 to 0.25
- weight_down: float32 [1024, 512], P(('wide', 'narrow')), may hold values from -0.1875 to 0.1875
- norm_params: float32 [6, 512], P(None, ('wide', 'narrow')), may hold values from -1.2 to 1.9
- first_qkv: float32 [512, 1536], P(('wide', 'narrow')), may hold values from -0.00048828125 to 0.00048828125
- first_out: float32 [512, 512], P(('wide', 'narrow')), may hold values from -3.0517578e-05 to 3.0517578e-05
- first_up: float32 [512, 1024], P(('wide', 'narrow')), may hold values from -0.00048828125 to 0.00048828125
- first_down: float32 [1024, 512], P(('wide', 'narrow')), may hold values from -0.00048828125 to 0.00048828125
- first_norm: float32 [6, 512], P(None, ('wide', 'narrow')), may hold values from -0.00048828125 to 0.00048828125
- second_qkv: float32 [512, 1536], P(('wide', 'narrow')), may hold values from 2.384186e-10 to 3.8146974e-09
- second_out: float32 [512, 512], P(('wide', 'narrow')), may hold values from 9.313226e-13 to 1.4901162e-11
- second_up: float32 [512, 1024], P(('wide', 'narrow')), may hold values from 2.384186e-10 to 3.8146974e-09
- second_down: float32 [1024, 512], P(('wide', 'narrow')), may hold values from 2.384186e-10 to 3.8146974e-09
- second_norm: float32 [6, 512], P(None, ('wide', 'narrow')), may hold values from 2.384186e-10 to 3.8146974e-09
Outputs:
- mixed: bfloat16 [49152, 512], P(('wide', 'narrow'))
- grad_tags: float32 [49152, 512], P(('wide', 'narrow'))
- grad_image: float32 [75264, 512], P(('wide', 'narrow'))
- total_norm: float32 [], replicated
- clipped_qkv: float32 [512, 1536], P(('wide', 'narrow'))
- clipped_out: float32 [512, 512], P(('wide', 'narrow'))
- clipped_up: float32 [512, 1024], P(('wide', 'narrow'))
- clipped_down: float32 [1024, 512], P(('wide', 'narrow'))
- clipped_norm: float32 [6, 512], P(None, ('wide', 'narrow'))
- moment_qkv: float32 [512, 1536], P(('wide', 'narrow'))
- moment_out: float32 [512, 512], P(('wide', 'narrow'))
- moment_up: float32 [512, 1024], P(('wide', 'narrow'))
- moment_down: float32 [1024, 512], P(('wide', 'narrow'))
- moment_norm: float32 [6, 512], P(None, ('wide', 'narrow'))
- square_qkv: float32 [512, 1536], P(('wide', 'narrow'))
- square_out: float32 [512, 512], P(('wide', 'narrow'))
- square_up: float32 [512, 1024], P(('wide', 'narrow'))
- square_down: float32 [1024, 512], P(('wide', 'narrow'))
- square_norm: float32 [6, 512], P(None, ('wide', 'narrow'))
- updated_qkv: float32 [512, 1536], P(('wide', 'narrow'))
- updated_out: float32 [512, 512], P(('wide', 'narrow'))
- updated_up: float32 [512, 1024], P(('wide', 'narrow'))
- updated_down: float32 [1024, 512], P(('wide', 'narrow'))
- updated_norm: float32 [6, 512], P(None, ('wide', 'narrow'))
- copied_qkv: bfloat16 [512, 1536], P(('wide', 'narrow'))
- copied_out: bfloat16 [512, 512], P(('wide', 'narrow'))
- copied_up: bfloat16 [512, 1024], P(('wide', 'narrow'))
- copied_down: bfloat16 [1024, 512], P(('wide', 'narrow'))
- copied_norm: bfloat16 [6, 512], P(None, ('wide', 'narrow'))
Inputs may be any that keep to these rules, and one draw needn't show every extreme that they name: `tag_counts`: at least one table has exactly 512 tags.
All inputs are finite; a program needn't handle non-finite values.
Results may differ from a plain program's by a relative error of at most 0.014.
The roundings to bfloat16 on the way count: a program that leaves them out, or rounds other values in their place, can miss the bound.
Values may be sent and summed in bfloat16 or wider, within the bound.
A program may use at most 192 MiB of HBM per device.

v0:
```python
import math

import jax
import jax.numpy as jnp
from jax import lax
from jax.sharding import PartitionSpec as P

HEADS = 8
STEP = 10


EPS_NORM = 1e-05
NEG_BIG = -1000000000.0
CLIP_AT = 1.0
BETA_FIRST = 0.9
BETA_SECOND = 0.999
ADAM_EPS = 1e-08
RATE_MATRIX = 0.05
RATE_OUTPUT = 1.0
RATE_NORMS = 0.5
DECAY_RATE = 0.1


def gelu_tanh(values):
    return jax.nn.gelu(values, approximate=True)


def row_norm(values, gain, shift):
    centred = values - jnp.mean(values, -1, keepdims=True)
    inverse = lax.rsqrt(jnp.mean(centred * centred, -1, keepdims=True) + EPS_NORM)
    normed = centred * inverse
    return (normed * gain + shift, normed, inverse)


def row_norm_back(gradient, normed, inverse, gain):
    scaled = gradient * gain
    return inverse * (
        scaled
        - jnp.mean(scaled, -1, keepdims=True)
        - normed * jnp.mean(scaled * normed, -1, keepdims=True)
    )


def table_scores(queries, key_rows, tag_count, score_scale):
    tag_len = queries.shape[0]
    img_len = key_rows.shape[0] - tag_len
    raw_scores = (
        jnp.einsum("qhd,khd->hqk", queries, key_rows, preferred_element_type=jnp.float32)
        * score_scale
    )
    row_ids = lax.broadcasted_iota(jnp.int32, (tag_len, img_len + tag_len), 0)
    col_ids = lax.broadcasted_iota(jnp.int32, (tag_len, img_len + tag_len), 1) - img_len
    allowed = (col_ids < 0) | (col_ids <= row_ids) & (col_ids < tag_count)
    return jnp.where(allowed[None], raw_scores, NEG_BIG)


def table_forward(queries, key_rows, value_rows, tag_count, score_scale):
    scores = table_scores(queries, key_rows, tag_count, score_scale)
    row_top = jnp.max(scores, -1, keepdims=True)
    exp_total = jnp.sum(jnp.exp(scores - row_top), -1, keepdims=True)
    log_total = row_top + jnp.log(exp_total)
    soft_low = jnp.exp(scores - log_total).astype(jnp.bfloat16)
    mixed_heads = jnp.einsum(
        "hqk,khd->qhd", soft_low, value_rows, preferred_element_type=jnp.float32
    )
    return (mixed_heads.astype(jnp.bfloat16), log_total[..., 0])


def table_backward(queries, key_rows, value_rows, tag_count, log_total, grad_heads, score_scale):
    scores = table_scores(queries, key_rows, tag_count, score_scale)
    soft_weights = jnp.exp(scores - log_total[..., None])
    grad_values = jnp.einsum(
        "hqk,qhd->khd",
        soft_weights.astype(jnp.bfloat16),
        grad_heads,
        preferred_element_type=jnp.float32,
    )
    grad_soft = jnp.einsum(
        "qhd,khd->hqk", grad_heads, value_rows, preferred_element_type=jnp.float32
    )
    delta_rows = jnp.sum(soft_weights * grad_soft, -1, keepdims=True)
    grad_scores = (soft_weights * (grad_soft - delta_rows)).astype(jnp.bfloat16)
    grad_queries = (
        jnp.einsum("hqk,khd->qhd", grad_scores, key_rows, preferred_element_type=jnp.float32)
        * score_scale
    )
    grad_keys = (
        jnp.einsum("hqk,qhd->khd", grad_scores, queries, preferred_element_type=jnp.float32)
        * score_scale
    )
    return (
        grad_queries.astype(jnp.bfloat16),
        grad_keys.astype(jnp.bfloat16),
        grad_values.astype(jnp.bfloat16),
    )


def shards(
    tag_inputs,
    image_inputs,
    tag_counts,
    cotangent,
    weight_qkv,
    weight_out,
    weight_up,
    weight_down,
    norm_params,
    first_qkv,
    first_out,
    first_up,
    first_down,
    first_norm,
    second_qkv,
    second_out,
    second_up,
    second_down,
    second_norm,
):
    model_width = tag_inputs.shape[1]
    head_size = model_width // HEADS
    score_scale = 1.0 / math.sqrt(head_size)
    tables = tag_counts.shape[0]
    tag_rows = tag_inputs.shape[0]
    image_rows = image_inputs.shape[0]
    tag_len = tag_rows // tables
    img_len = image_rows // tables
    devices = lax.axis_size(("wide", "narrow"))
    total_rows = image_rows * devices
    masters = (weight_qkv, weight_out, weight_up, weight_down, norm_params)
    firsts = (first_qkv, first_out, first_up, first_down, first_norm)
    seconds = (second_qkv, second_out, second_up, second_down, second_norm)
    rates = (RATE_MATRIX, RATE_OUTPUT, RATE_MATRIX, RATE_MATRIX)
    copies = tuple((master.astype(jnp.bfloat16) for master in masters))
    gathered = (
        lax.all_gather(copies[0], ("wide", "narrow"), axis=0, tiled=True),
        lax.all_gather(copies[1], ("wide", "narrow"), axis=0, tiled=True),
        lax.all_gather(copies[2], ("wide", "narrow"), axis=0, tiled=True),
        lax.all_gather(copies[3], ("wide", "narrow"), axis=0, tiled=True),
        lax.all_gather(copies[4], ("wide", "narrow"), axis=1, tiled=True),
    )
    w_qkv, w_out, w_up, w_down = (gathered[0], gathered[1], gathered[2], gathered[3])
    gain_rows = gathered[4].astype(jnp.float32)
    image_values = image_inputs.astype(jnp.float32)
    bn_mean = lax.psum(jnp.sum(image_values, 0), ("wide", "narrow")) / total_rows
    centred = image_values - bn_mean
    bn_spread = lax.psum(jnp.sum(centred * centred, 0), ("wide", "narrow")) / total_rows
    bn_inverse = lax.rsqrt(bn_spread + EPS_NORM)
    img_normed = centred * bn_inverse
    img_low = (img_normed * gain_rows[4] + gain_rows[5]).astype(jnp.bfloat16)
    kv_image = jnp.dot(img_low, w_qkv[:, model_width:], preferred_element_type=jnp.float32).astype(
        jnp.bfloat16
    )
    qkv_tags = jnp.dot(tag_inputs, w_qkv, preferred_element_type=jnp.float32).astype(jnp.bfloat16)
    queries = qkv_tags[:, :model_width].reshape(tables, tag_len, HEADS, head_size)
    key_rows = jnp.concatenate(
        [
            kv_image[:, :model_width].reshape(tables, img_len, model_width),
            qkv_tags[:, model_width : 2 * model_width].reshape(tables, tag_len, model_width),
        ],
        1,
    ).reshape(tables, img_len + tag_len, HEADS, head_size)
    value_rows = jnp.concatenate(
        [
            kv_image[:, model_width:].reshape(tables, img_len, model_width),
            qkv_tags[:, 2 * model_width :].reshape(tables, tag_len, model_width),
        ],
        1,
    ).reshape(tables, img_len + tag_len, HEADS, head_size)
    attended, log_totals = lax.map(
        lambda table_item: table_forward(
            table_item[0], table_item[1], table_item[2], table_item[3], score_scale
        ),
        (queries, key_rows, value_rows, tag_counts),
    )
    attended_low = attended.reshape(tag_rows, model_width)
    hidden_pre = tag_inputs.astype(jnp.float32) + jnp.dot(
        attended_low, w_out, preferred_element_type=jnp.float32
    )
    hidden, hidden_hat, hidden_inverse = row_norm(hidden_pre, gain_rows[0], gain_rows[1])
    hidden_low = hidden.astype(jnp.bfloat16)
    pre_act = jnp.dot(hidden_low, w_up, preferred_element_type=jnp.float32)
    activated = gelu_tanh(pre_act).astype(jnp.bfloat16)
    resid = hidden + jnp.dot(activated, w_down, preferred_element_type=jnp.float32)
    output, resid_hat, resid_inverse = row_norm(resid, gain_rows[2], gain_rows[3])
    mixed = output.astype(jnp.bfloat16)
    regathered = (
        lax.all_gather(copies[0], ("wide", "narrow"), axis=0, tiled=True),
        lax.all_gather(copies[1], ("wide", "narrow"), axis=0, tiled=True),
        lax.all_gather(copies[2], ("wide", "narrow"), axis=0, tiled=True),
        lax.all_gather(copies[3], ("wide", "narrow"), axis=0, tiled=True),
        lax.all_gather(copies[4], ("wide", "narrow"), axis=1, tiled=True),
    )
    b_qkv, b_out, b_up, b_down = (regathered[0], regathered[1], regathered[2], regathered[3])
    back_gains = regathered[4].astype(jnp.float32)
    valid = (lax.broadcasted_iota(jnp.int32, (tables, tag_len), 1) < tag_counts[:, None]).reshape(
        tag_rows, 1
    )
    grad_out = jnp.where(valid, cotangent.astype(jnp.float32), 0.0)
    second_gain = jnp.sum(grad_out * resid_hat, 0)
    second_bias = jnp.sum(grad_out, 0)
    grad_resid = row_norm_back(grad_out, resid_hat, resid_inverse, back_gains[2])
    resid_low = grad_resid.astype(jnp.bfloat16)
    grad_down = jnp.einsum("rf,rd->fd", activated, resid_low, preferred_element_type=jnp.float32)
    grad_act = jnp.einsum("rd,fd->rf", resid_low, b_down, preferred_element_type=jnp.float32)
    act_pull = jax.vjp(gelu_tanh, pre_act)[1]
    pre_low = act_pull(grad_act)[0].astype(jnp.bfloat16)
    grad_up = jnp.einsum("rd,rf->df", hidden_low, pre_low, preferred_element_type=jnp.float32)
    grad_hidden = grad_resid + jnp.einsum(
        "rf,df->rd", pre_low, b_up, preferred_element_type=jnp.float32
    )
    first_gain = jnp.sum(grad_hidden * hidden_hat, 0)
    first_bias = jnp.sum(grad_hidden, 0)
    grad_hpre = row_norm_back(grad_hidden, hidden_hat, hidden_inverse, back_gains[0])
    hpre_low = grad_hpre.astype(jnp.bfloat16)
    grad_outw = jnp.einsum("rd,re->de", attended_low, hpre_low, preferred_element_type=jnp.float32)
    layer_terms = jnp.stack([first_gain, first_bias, second_gain, second_bias])
    grad_attended = jnp.einsum(
        "re,de->rd", hpre_low, b_out, preferred_element_type=jnp.float32
    ).astype(jnp.bfloat16)
    grad_heads = grad_attended.reshape(tables, tag_len, HEADS, head_size)
    grad_queries, grad_keys, grad_values = lax.map(
        lambda table_item: table_backward(
            table_item[0],
            table_item[1],
            table_item[2],
            table_item[3],
            table_item[4],
            table_item[5],
            score_scale,
        ),
        (queries, key_rows, value_rows, tag_counts, log_totals, grad_heads),
    )
    grad_keys = grad_keys.reshape(tables, img_len + tag_len, model_width)
    grad_values = grad_values.reshape(tables, img_len + tag_len, model_width)
    grad_qkv_tags = jnp.concatenate(
        [
            grad_queries.reshape(tag_rows, model_width),
            grad_keys[:, img_len:].reshape(tag_rows, model_width),
            grad_values[:, img_len:].reshape(tag_rows, model_width),
        ],
        1,
    )
    grad_kv_image = jnp.concatenate(
        [
            grad_keys[:, :img_len].reshape(image_rows, model_width),
            grad_values[:, :img_len].reshape(image_rows, model_width),
        ],
        1,
    )
    tag_part = jnp.einsum(
        "rd,re->de", tag_inputs, grad_qkv_tags, preferred_element_type=jnp.float32
    )
    image_part = jnp.einsum("rd,re->de", img_low, grad_kv_image, preferred_element_type=jnp.float32)
    grad_qkv = jnp.concatenate(
        [tag_part[:, :model_width], tag_part[:, model_width:] + image_part], 1
    )
    grad_tags = grad_hpre + jnp.einsum(
        "re,de->rd", grad_qkv_tags, b_qkv, preferred_element_type=jnp.float32
    )
    grad_z = jnp.einsum(
        "re,de->rd", grad_kv_image, b_qkv[:, model_width:], preferred_element_type=jnp.float32
    )
    bn_gain_sum, bn_bias_sum = lax.psum(
        (jnp.sum(grad_z * img_normed, 0), jnp.sum(grad_z, 0)), ("wide", "narrow")
    )
    bn_gain = back_gains[4]
    grad_image = bn_inverse * (
        grad_z * bn_gain
        - bn_gain * bn_bias_sum / total_rows
        - img_normed * bn_gain * bn_gain_sum / total_rows
    )
    owned_grads = (
        lax.psum_scatter(grad_qkv, ("wide", "narrow"), scatter_dimension=0, tiled=True),
        lax.psum_scatter(grad_outw, ("wide", "narrow"), scatter_dimension=0, tiled=True),
        lax.psum_scatter(grad_up, ("wide", "narrow"), scatter_dimension=0, tiled=True),
        lax.psum_scatter(grad_down, ("wide", "narrow"), scatter_dimension=0, tiled=True),
        lax.psum_scatter(layer_terms, ("wide", "narrow"), scatter_dimension=1, tiled=True),
    )
    owned_qkv, owned_outw, owned_up, owned_down, owned_layer = (
        owned_grads[0],
        owned_grads[1],
        owned_grads[2],
        owned_grads[3],
        owned_grads[4],
    )
    own_cols = model_width // devices
    own_start = lax.axis_index(("wide", "narrow")) * own_cols
    bn_owned = jnp.stack(
        [
            lax.dynamic_slice_in_dim(bn_gain_sum, own_start, own_cols),
            lax.dynamic_slice_in_dim(bn_bias_sum, own_start, own_cols),
        ]
    )
    gradients = (
        owned_qkv,
        owned_outw,
        owned_up,
        owned_down,
        jnp.concatenate([owned_layer, bn_owned], 0),
    )
    local_squares = jnp.sum(gradients[0] * gradients[0])
    for gradient in gradients[1:]:
        local_squares = local_squares + jnp.sum(gradient * gradient)
    total_norm = jnp.sqrt(lax.psum(local_squares, ("wide", "narrow")))
    factor = CLIP_AT / jnp.maximum(total_norm, CLIP_AT)
    clipped, moments, squares, updated, copied = ([], [], [], [], [])
    for position in range(5):
        master = masters[position]
        clip_grad = factor * gradients[position]
        moment = BETA_FIRST * firsts[position] + (1.0 - BETA_FIRST) * clip_grad
        square = BETA_SECOND * seconds[position] + (1.0 - BETA_SECOND) * clip_grad * clip_grad
        direction = (
            moment
            / (1.0 - BETA_FIRST**STEP)
            / (jnp.sqrt(square / (1.0 - BETA_SECOND**STEP)) + ADAM_EPS)
        )
        if position < 4:
            new_weight = master - rates[position] * (direction + DECAY_RATE * master)
        else:
            new_weight = master - RATE_NORMS * direction
        clipped.append(clip_grad)
        moments.append(moment)
        squares.append(square)
        updated.append(new_weight)
        copied.append(new_weight.astype(jnp.bfloat16))
    return (
        mixed,
        grad_tags,
        grad_image,
        total_norm,
        clipped[0],
        clipped[1],
        clipped[2],
        clipped[3],
        clipped[4],
        moments[0],
        moments[1],
        moments[2],
        moments[3],
        moments[4],
        squares[0],
        squares[1],
        squares[2],
        squares[3],
        squares[4],
        updated[0],
        updated[1],
        updated[2],
        updated[3],
        updated[4],
        copied[0],
        copied[1],
        copied[2],
        copied[3],
        copied[4],
    )


def solution(mesh):
    return jax.shard_map(
        shards,
        mesh=mesh,
        in_specs=(
            P(("wide", "narrow"), None),
            P(("wide", "narrow"), None),
            P(("wide", "narrow")),
            P(("wide", "narrow"), None),
            P(("wide", "narrow"), None),
            P(("wide", "narrow"), None),
            P(("wide", "narrow"), None),
            P(("wide", "narrow"), None),
            P(None, ("wide", "narrow")),
            P(("wide", "narrow"), None),
            P(("wide", "narrow"), None),
            P(("wide", "narrow"), None),
            P(("wide", "narrow"), None),
            P(None, ("wide", "narrow")),
            P(("wide", "narrow"), None),
            P(("wide", "narrow"), None),
            P(("wide", "narrow"), None),
            P(("wide", "narrow"), None),
            P(None, ("wide", "narrow")),
        ),
        out_specs=(
            P(("wide", "narrow"), None),
            P(("wide", "narrow"), None),
            P(("wide", "narrow"), None),
            P(),
            P(("wide", "narrow"), None),
            P(("wide", "narrow"), None),
            P(("wide", "narrow"), None),
            P(("wide", "narrow"), None),
            P(None, ("wide", "narrow")),
            P(("wide", "narrow"), None),
            P(("wide", "narrow"), None),
            P(("wide", "narrow"), None),
            P(("wide", "narrow"), None),
            P(None, ("wide", "narrow")),
            P(("wide", "narrow"), None),
            P(("wide", "narrow"), None),
            P(("wide", "narrow"), None),
            P(("wide", "narrow"), None),
            P(None, ("wide", "narrow")),
            P(("wide", "narrow"), None),
            P(("wide", "narrow"), None),
            P(("wide", "narrow"), None),
            P(("wide", "narrow"), None),
            P(None, ("wide", "narrow")),
            P(("wide", "narrow"), None),
            P(("wide", "narrow"), None),
            P(("wide", "narrow"), None),
            P(("wide", "narrow"), None),
            P(None, ("wide", "narrow")),
        ),
        check_vma=False,
    )
```

profile of v0, /device:TPU:0, one launch (start us, length us, event | category | flops | bytes accessed | tf_op | source)
XLA Modules:
  0.0 1092.3 jit_solution(142911219150433259)
XLA Ops:
  16.2 42.1 %psum.35 = f32[512]{0:T(512)S(1)} all-reduce(f32[512]{0:T(512)S(1)} %convert_reduce_fusion), channel_id=1, replica_groups=mesh['wide'=16,'narrow'=2] {'wide','narrow'}, use_global_device_ids=true, to_apply=%region_1.0 | all-reduce | flops 512 | bytes 4096 | tf_op jit(solution)/shard_map/psum | solution.py:144
  59.0 40.4 %psum.36 = f32[512]{0:T(512)S(1)} all-reduce(f32[512]{0:T(512)S(1)} %fusion.92), channel_id=1, replica_groups=mesh['wide'=16,'narrow'=2] {'wide','narrow'}, use_global_device_ids=true, to_apply=%region_3.0 | all-reduce | flops 512 | bytes 4096 | tf_op jit(solution)/shard_map/psum | solution.py:146
  99.4 41.3 %all-gather = bf16[32,16,6]{1,2,0:T(8,128)(2,1)S(1)} all-gather(bf16[1,16,6]{1,2,0:T(8,128)(2,1)S(1)} %convert_bitcast_fusion), channel_id=1, replica_groups=mesh['wide'=16,'narrow'=2] {'wide','narrow'}, dimensions={0}, use_global_device_ids=true | all-gather | bytes 6336 | tf_op jit(solution)/shard_map/all_gather | solution.py:139
  141.6 41.2 %all_gather.22 = bf16[512,512]{1,0:T(8,128)(2,1)} all-gather(bf16[16,512]{1,0:T(8,128)(2,1)S(1)} %convert_element_type.135), channel_id=1, replica_groups=mesh['wide'=16,'narrow'=2] {'wide','narrow'}, dimensions={0}, use_global_device_ids=true | all-gather | bytes 540672 | tf_op jit(solution)/shard_map/all_gather | solution.py:136
  187.5 4.2 convolution_convert_fusion
  195.8 5.6 concatenate.32
  203.0 5.6 concatenate.29
  211.5 3.8 copy.204
  215.4 4.6 convolution_convert_fusion.1
  222.6 4.3 copy.201
  226.9 8.8 concatenate.31
  235.7 8.8 pad_maximum_fusion.1
  244.5 5.5 copy.205
  249.9 4.5 copy.198
  254.4 8.8 concatenate.28
  263.2 8.8 pad_maximum_fusion
  272.0 5.5 copy.203
  277.6 76.4 %while.30 = (s32[]{:T(128)}, bf16[3,512,8,64]{1,3,2,0:T(8,128)(2,1)S(1)}, f32[3,8,512]{2,1,0:T(8,128)S(1)}, bf16[3,1296,8,64]{1,3,2,0:T(8,128)(2,1)}, s32[3]{0:T...) while((s32[]{:T(128)}, ...), condition=%wide.region_7.8_spmd, body=%wide.region_4.7_spmd.sunk | while | flops 1398367232 | bytes 154043728 | solution.py:169
  280.1 4.9 fusion.179
  288.3 3.8 copy-done
  292.1 10.9 fusion.180
  305.5 4.9 fusion.179
  313.7 3.8 copy-done
  317.5 10.9 fusion.180
  330.9 4.9 fusion.179
  339.1 3.8 copy-done
  342.9 10.9 fusion.180
  359.2 6.9 fusion.121
  366.1 7.3 fusion.140
  378.7 6.6 fusion.80
  385.3 3.4 multiply_reduce_fusion.2
  400.4 4.7 copy.212
  406.5 216.2 %while.31 = (s32[]{:T(128)}, bf16[3,512,8,64]{1,3,2,0:T(8,128)(2,1)}, bf16[3,1296,8,64]{1,3,2,0:T(8,128)(2,1)}, bf16[3,1296,8,64]{1,3,2,0:T(8,128)(2,1)}, bf16[3...) while((s32[]{:T(128)}, ...), condition=%wide.region_18.19_spmd, body=%wide.region_16.18_spmd.sunk | while | flops 3449668608 | bytes 202363312 | solution.py:221
  409.1 11.6 %fusion.189 = f32[8,512,1296]{1,2,0:T(8,128)} fusion(bf16[3,1296,8,64]{1,3,2,0:T(8,128)(2,1)} %get-tuple-element.761, s32[]{:T(128)S(6)} %copy.257, bf16[3,512,8,64]{1,3,2,0:T(8,128)(2,1)} %get-tuple-element.760), kind=kOutput, calls=%fused_computation.39.clone.1 | convolution fusion | flops 679477248 | bytes 23200768 | tf_op jit(solution)/shard_map/while/body/eval_jaxpr/qhd,khd->hqk/dot_general | solution.py:78
  420.7 15.2 %multiply_reduce_fusion.14 = (f32[8,512]{1,0:T(8,128)S(1)}, f32[8,512,1296]{1,2,0:T(8,128)}) fusion(f32[8,512,1296]{1,2,0:T(8,128)} %fusion.189, f32[8,512]{1,0:T(8,128)S(1)} %dynamic-slice_bitcast_fusion.4, bf16[3,1296,8,64]{1,3,2,0:T(8,128)(2,1)} %get-tuple-element.756, s32[]{:T(128)S(6)} %copy.257, ...), kind=kOutput, calls=%fused_computation.25.clone.1 | convolution fusion | flops 706015232 | bytes 45130752 | tf_op jit(solution)/shard_map/while/body/eval_jaxpr/qhd,khd->hqk/dot_general | solution.py:48
  435.9 19.0 %multiply_convert_fusion.5 = bf16[8,512,1296]{1,2,0:T(8,128)(2,1)} fusion(f32[8,512,1296]{1,2,0:T(8,128)} %get-tuple-element.704, f32[8,512,1296]{1,2,0:T(8,128)} %fusion.189, f32[8,512]{1,0:T(8,128)S(1)} %get-tuple-element.705), kind=kLoop, calls=%fused_computation.24.clone.1 | loop fusion | flops 15925248 | bytes 53100544 | tf_op jit(solution)/shard_map/while/body/eval_jaxpr/convert_element_type | solution.py:82
  454.9 11.8 %fusion.194 = bf16[3,1296,8,64]{1,3,2,0:T(8,128)(2,1)} fusion(bf16[3,1296,8,64]{1,3,2,0:T(8,128)(2,1)} %get-tuple-element.744, s32[]{:T(128)S(6)} %copy.257, f32[8,512,1296]{1,2,0:T(8,128)} %get-tuple-element.704, bf16[3,512,8,64]{1,3,2,0:T(8,128)(2,1)} %get-tuple-element.760), kind=kOutput, calls=%fused_computation.33.clone.1 | convolution fusion | flops 685449216 | bytes 23200768 | tf_op jit(solution)/shard_map/while/body/eval_jaxpr/hqk,qhd->khd/dot_general | solution.py:72
  466.7 7.5 fusion.192
  474.2 4.4 fusion.193
  481.1 11.6 %fusion.189 = f32[8,512,1296]{1,2,0:T(8,128)} fusion(bf16[3,1296,8,64]{1,3,2,0:T(8,128)(2,1)} %get-tuple-element.761, s32[]{:T(128)S(6)} %copy.257, bf16[3,512,8,64]{1,3,2,0:T(8,128)(2,1)} %get-tuple-element.760), kind=kOutput, calls=%fused_computation.39.clone.1 | convolution fusion | flops 679477248 | bytes 23200768 | tf_op jit(solution)/shard_map/while/body/eval_jaxpr/qhd,khd->hqk/dot_general | solution.py:78
  492.7 15.2 %multiply_reduce_fusion.14 = (f32[8,512]{1,0:T(8,128)S(1)}, f32[8,512,1296]{1,2,0:T(8,128)}) fusion(f32[8,512,1296]{1,2,0:T(8,128)} %fusion.189, f32[8,512]{1,0:T(8,128)S(1)} %dynamic-slice_bitcast_fusion.4, bf16[3,1296,8,64]{1,3,2,0:T(8,128)(2,1)} %get-tuple-element.756, s32[]{:T(128)S(6)} %copy.257, ...), kind=kOutput, calls=%fused_computation.25.clone.1 | convolution fusion | flops 706015232 | bytes 45130752 | tf_op jit(solution)/shard_map/while/body/eval_jaxpr/qhd,khd->hqk/dot_general | solution.py:48
  507.9 19.0 %multiply_convert_fusion.5 = bf16[8,512,1296]{1,2,0:T(8,128)(2,1)} fusion(f32[8,512,1296]{1,2,0:T(8,128)} %get-tuple-element.704, f32[8,512,1296]{1,2,0:T(8,128)} %fusion.189, f32[8,512]{1,0:T(8,128)S(1)} %get-tuple-element.705), kind=kLoop, calls=%fused_computation.24.clone.1 | loop fusion | flops 15925248 | bytes 53100544 | tf_op jit(solution)/shard_map/while/body/eval_jaxpr/convert_element_type | solution.py:82
  526.9 11.8 %fusion.194 = bf16[3,1296,8,64]{1,3,2,0:T(8,128)(2,1)} fusion(bf16[3,1296,8,64]{1,3,2,0:T(8,128)(2,1)} %get-tuple-element.744, s32[]{:T(128)S(6)} %copy.257, f32[8,512,1296]{1,2,0:T(8,128)} %get-tuple-element.704, bf16[3,512,8,64]{1,3,2,0:T(8,128)(2,1)} %get-tuple-element.760), kind=kOutput, calls=%fused_computation.33.clone.1 | convolution fusion | flops 685449216 | bytes 23200768 | tf_op jit(solution)/shard_map/while/body/eval_jaxpr/hqk,qhd->khd/dot_general | solution.py:72
  538.7 7.4 fusion.192
  546.1 4.4 fusion.193
  553.0 11.6 %fusion.189 = f32[8,512,1296]{1,2,0:T(8,128)} fusion(bf16[3,1296,8,64]{1,3,2,0:T(8,128)(2,1)} %get-tuple-element.761, s32[]{:T(128)S(6)} %copy.257, bf16[3,512,8,64]{1,3,2,0:T(8,128)(2,1)} %get-tuple-element.760), kind=kOutput, calls=%fused_computation.39.clone.1 | convolution fusion | flops 679477248 | bytes 23200768 | tf_op jit(solution)/shard_map/while/body/eval_jaxpr/qhd,khd->hqk/dot_general | solution.py:78
  564.6 15.2 %multiply_reduce_fusion.14 = (f32[8,512]{1,0:T(8,128)S(1)}, f32[8,512,1296]{1,2,0:T(8,128)}) fusion(f32[8,512,1296]{1,2,0:T(8,128)} %fusion.189, f32[8,512]{1,0:T(8,128)S(1)} %dynamic-slice_bitcast_fusion.4, bf16[3,1296,8,64]{1,3,2,0:T(8,128)(2,1)} %get-tuple-element.756, s32[]{:T(128)S(6)} %copy.257, ...), kind=kOutput, calls=%fused_computation.25.clone.1 | convolution fusion | flops 706015232 | bytes 45130752 | tf_op jit(solution)/shard_map/while/body/eval_jaxpr/qhd,khd->hqk/dot_general | solution.py:48
  579.8 19.0 %multiply_convert_fusion.5 = bf16[8,512,1296]{1,2,0:T(8,128)(2,1)} fusion(f32[8,512,1296]{1,2,0:T(8,128)} %get-tuple-element.704, f32[8,512,1296]{1,2,0:T(8,128)} %fusion.189, f32[8,512]{1,0:T(8,128)S(1)} %get-tuple-element.705), kind=kLoop, calls=%fused_computation.24.clone.1 | loop fusion | flops 15925248 | bytes 53100544 | tf_op jit(solution)/shard_map/while/body/eval_jaxpr/convert_element_type | solution.py:82
  598.8 11.8 %fusion.194 = bf16[3,1296,8,64]{1,3,2,0:T(8,128)(2,1)} fusion(bf16[3,1296,8,64]{1,3,2,0:T(8,128)(2,1)} %get-tuple-element.744, s32[]{:T(128)S(6)} %copy.257, f32[8,512,1296]{1,2,0:T(8,128)} %get-tuple-element.704, bf16[3,512,8,64]{1,3,2,0:T(8,128)(2,1)} %get-tuple-element.760), kind=kOutput, calls=%fused_computation.33.clone.1 | convolution fusion | flops 685449216 | bytes 23200768 | tf_op jit(solution)/shard_map/while/body/eval_jaxpr/hqk,qhd->khd/dot_general | solution.py:72
  610.6 7.4 fusion.192
  618.1 4.4 fusion.193
  622.7 3.4 slice.89
  626.1 3.7 slice.91
  632.0 4.5 copy.221
  661.0 5.1 fusion.119
  666.2 9.3 fusion.106
  678.5 9.1 fusion.123
  687.6 37.3 %all-reduce = (f32[512]{0:T(512)S(1)}, f32[512]{0:T(512)S(1)}) all-reduce(f32[512]{0:T(512)S(1)} %get-tuple-element.484, f32[512]{0:T(512)S(1)} %get-tuple-element.483), channel_id=1, replica_groups=mesh['wide'=16,'narrow'=2] {'wide','narrow'}, use_global_device_ids=true, to_apply=%region_22.23 | all-reduce | flops 1024 | bytes 8192 | tf_op jit(solution)/shard_map/psum | solution.py:263
  725.1 7.2 convolution_add_fusion.1
  732.3 3.8 fusion.90
  738.9 21.8 %reduce-scatter.16.cloned.1.call-done = f32[16,1536]{1,0:T(8,128)} async-done(((f32[512,1536]{1,0:T(8,128)}), f32[16,1536]{1,0:T(8,128)}) %reduce-scatter.16.cloned.1.call-update) | async-done | bytes 98320 | tf_op jit(solution)/shard_map/reduce_scatter | solution.py:273
  765.9 132.7 %reduce-scatter.12.cloned.1.call-done = f32[16,1024]{1,0:T(8,128)} async-done(((f32[512,1024]{1,0:T(8,128)}), f32[16,1024]{1,0:T(8,128)}) %reduce-scatter.12.cloned.1.call-update) | async-done | bytes 65552 | tf_op jit(solution)/shard_map/reduce_scatter | solution.py:275
  900.7 132.9 %reduce-scatter.14.cloned.1.call-done = f32[32,512]{1,0:T(8,128)} async-done(((f32[1024,512]{1,0:T(8,128)}), f32[32,512]{1,0:T(8,128)}) %reduce-scatter.14.cloned.1.call-update) | async-done | bytes 65552 | tf_op jit(solution)/shard_map/reduce_scatter | solution.py:276
  1038.9 36.8 %psum.39 = f32[]{:T(128)} all-reduce(f32[]{:T(128)S(6)} %add.258), channel_id=1, replica_groups=mesh['wide'=16,'narrow'=2] {'wide','narrow'}, use_global_device_ids=true, to_apply=%region_37.38 | all-reduce | flops 1 | bytes 8 | tf_op jit(solution)/shard_map/psum | solution.py:304
  (295 shorter events, 123.8 us)
Async XLA Ops:
  7.2 51.1 %copy-start.6 = (bf16[2352,512]{1,0:T(8,128)(2,1)S(1)}, bf16[2352,512]{1,0:T(8,128)(2,1)}, u32[]{:S(2)}) copy-start(bf16[2352,512]{1,0:T(8,128)(2,1)} %param.24) | copy-start | bytes 7225348
  7.2 92.1 %copy-start.30 = (f32[16,512]{1,0:T(8,128)S(1)}, f32[16,512]{1,0:T(8,128)}, u32[]{:S(2)}) copy-start(f32[16,512]{1,0:T(8,128)} %param.28) | copy-start | bytes 98308
  7.2 180.3 %all-gather.5.cloned.1.call-start = ((), (), s32[]{:S(2)}) async-start(), calls=%async_computation.5 | async-start | bytes 1622016 | tf_op jit(solution)/shard_map/all_gather | solution.py:135
  9.0 350.2 %all-gather.7.cloned.1.call-start = ((), (), s32[]{:S(2)}) async-start(), calls=%async_computation.6 | async-start | bytes 1081344 | tf_op jit(solution)/shard_map/all_gather | solution.py:137
  10.5 355.5 %all-gather.9.cloned.1.call-start = ((), (), s32[]{:S(2)}) async-start(), calls=%async_computation.7 | async-start | bytes 1081344 | tf_op jit(solution)/shard_map/all_gather | solution.py:138
  12.0 724.1 %reduce-scatter.18.cloned.1.call-start = ((), (), s32[]{:S(2)}) async-start(), calls=%async_computation.12 | async-start | bytes 270336
  58.3 157.1 %copy-start.39 = (f32[512]{0:T(512)}, f32[512]{0:T(512)S(1)}, u32[]{:S(2)}) copy-start(f32[512]{0:T(512)S(1)} %broadcast_multiply_fusion.10) | copy-start | bytes 6148
  59.0 127.0 %copy-start.21 = (bf16[1536,512]{1,0:T(8,128)(2,1)S(1)}, bf16[1536,512]{1,0:T(8,128)(2,1)}, u32[]{:S(2)}) copy-start(bf16[1536,512]{1,0:T(8,128)(2,1)} %param.23) | copy-start | bytes 4718596
  99.4 116.0 %copy-start.55 = (f32[512]{0:T(512)}, f32[512]{0:T(512)S(1)}, u32[]{:S(2)}) copy-start(f32[512]{0:T(512)S(1)} %add_rsqrt_fusion.2) | copy-start | bytes 6148
  141.6 73.8 %copy-start.41 = (f32[1,512]{1,0:T(1,128)}, f32[1,512]{1,0:T(1,128)S(1)}, u32[]{:S(2)}) copy-start(f32[1,512]{1,0:T(1,128)S(1)} %get-tuple-element.573) | copy-start | bytes 6148
  141.6 73.8 %copy-start.63 = (f32[1,512]{1,0:T(1,128)}, f32[1,512]{1,0:T(1,128)S(1)}, u32[]{:S(2)}) copy-start(f32[1,512]{1,0:T(1,128)S(1)} %get-tuple-element.572) | copy-start | bytes 6148
  211.5 3.9 copy-start.66
  272.0 5.6 copy-start.65
  285.0 7.1 copy-start
  310.4 7.1 copy-start
  335.8 7.1 copy-start
  357.1 31.7 %copy-start.33 = (f32[1536]{0:T(1024)}, f32[1536]{0:T(1024)S(1)}, u32[]{:S(2)}) copy-start(f32[1536]{0:T(1024)S(1)} %broadcast_multiply_fusion.9) | copy-start | bytes 18436
  359.1 29.6 %copy-start.37 = (f32[1536]{0:T(1024)}, f32[1536]{0:T(1024)S(1)}, u32[]{:S(2)}) copy-start(f32[1536]{0:T(1024)S(1)} %add_rsqrt_fusion.1) | copy-start | bytes 18436
  373.4 11.9 %copy-start.9 = (f32[1536,512]{0,1:T(8,128)}, f32[1536,512]{0,1:T(8,128)S(1)}, u32[]{:S(2)}) copy-start(f32[1536,512]{0,1:T(8,128)S(1)} %get-tuple-element.577) | copy-start | bytes 9437188
  373.4 11.8 %copy-start.31 = (f32[1536]{0:T(1024)}, f32[1536]{0:T(1024)S(1)}, u32[]{:S(2)}) copy-start(f32[1536]{0:T(1024)S(1)} %broadcast_multiply_fusion.8) | copy-start | bytes 18436
  373.4 5.2 copy-start.69
  373.9 11.4 %copy-start.35 = (f32[1536]{0:T(1024)}, f32[1536]{0:T(1024)S(1)}, u32[]{:S(2)}) copy-start(f32[1536]{0:T(1024)S(1)} %add_rsqrt_fusion) | copy-start | bytes 18436
  378.6 6.6 copy-start.49
  378.6 6.7 copy-start.51
  378.6 6.6 copy-start.2
  378.7 6.6 copy-start.67
  385.3 3.4 copy-start.70
  394.2 343.3 %reduce-scatter.10.cloned.1.call-start = ((), (), s32[]{:S(2)}) async-start(), calls=%async_computation.8 | async-start | bytes 1081344 | tf_op jit(solution)/shard_map/reduce_scatter | solution.py:274
  405.1 355.6 %reduce-scatter.16.cloned.1.call-start = ((), (), s32[]{:S(2)}) async-start(), calls=%async_computation.11 | async-start | bytes 3244032 | tf_op jit(solution)/shard_map/reduce_scatter | solution.py:273
  454.9 19.3 %slice-start = ((s8[10616832]{0:T(1024)(128)(4,1)}), s8[2228224]{0:T(1024)(128)(4,1)S(1)}, s32[]{:S(2)}) async-start(s8[10616832]{0:T(1024)(128)(4,1)} %bitcast.185), calls=%async_computation.13 | async-start | bytes 4456448 | tf_op jit(solution)/shard_map/while
  454.9 19.3 %slice-start.1 = ((s8[10616832]{0:T(1024)(128)(4,1)}), s8[4194304]{0:T(1024)(128)(4,1)S(1)}, s32[]{:S(2)}) async-start(s8[10616832]{0:T(1024)(128)(4,1)} %bitcast.185), calls=%async_computation.14 | async-start | bytes 8388608 | tf_op jit(solution)/shard_map/while
  466.7 7.5 slice-start.2
  526.9 19.2 %slice-start = ((s8[10616832]{0:T(1024)(128)(4,1)}), s8[2228224]{0:T(1024)(128)(4,1)S(1)}, s32[]{:S(2)}) async-start(s8[10616832]{0:T(1024)(128)(4,1)} %bitcast.185), calls=%async_computation.13 | async-start | bytes 4456448 | tf_op jit(solution)/shard_map/while
  526.9 19.2 %slice-start.1 = ((s8[10616832]{0:T(1024)(128)(4,1)}), s8[4194304]{0:T(1024)(128)(4,1)S(1)}, s32[]{:S(2)}) async-start(s8[10616832]{0:T(1024)(128)(4,1)} %bitcast.185), calls=%async_computation.14 | async-start | bytes 8388608 | tf_op jit(solution)/shard_map/while
  538.7 7.4 slice-start.2
  598.8 19.2 %slice-start = ((s8[10616832]{0:T(1024)(128)(4,1)}), s8[2228224]{0:T(1024)(128)(4,1)S(1)}, s32[]{:S(2)}) async-start(s8[10616832]{0:T(1024)(128)(4,1)} %bitcast.185), calls=%async_computation.13 | async-start | bytes 4456448 | tf_op jit(solution)/shard_map/while
  598.8 19.2 %slice-start.1 = ((s8[10616832]{0:T(1024)(128)(4,1)}), s8[4194304]{0:T(1024)(128)(4,1)S(1)}, s32[]{:S(2)}) async-start(s8[10616832]{0:T(1024)(128)(4,1)} %bitcast.185), calls=%async_computation.14 | async-start | bytes 8388608 | tf_op jit(solution)/shard_map/while
  610.6 7.4 slice-start.2
  626.1 3.7 copy-start.16
  644.3 3.4 copy-start.11
  650.1 3.2 copy-start.19
  650.2 3.2 copy-start.40
  659.1 7.0 copy-start.32
  659.1 7.0 copy-start.36
  659.1 7.0 copy-start.45
  659.1 7.0 copy-start.48
  659.1 7.0 copy-start.50
  659.2 7.0 copy-start.52
  659.2 239.4 %reduce-scatter.12.cloned.1.call-start = ((), (), s32[]{:S(2)}) async-start(), calls=%async_computation.9 | async-start | bytes 2162688 | tf_op jit(solution)/shard_map/reduce_scatter | solution.py:275
  666.1 367.5 %reduce-scatter.14.cloned.1.call-start = ((), (), s32[]{:S(2)}) async-start(), calls=%async_computation.10 | async-start | bytes 2162688 | tf_op jit(solution)/shard_map/reduce_scatter | solution.py:276
  678.5 46.6 %copy-start.5 = (f32[1536,512]{0,1:T(8,128)S(1)}, f32[1536,512]{0,1:T(8,128)}, u32[]{:S(2)}) copy-start(f32[1536,512]{0,1:T(8,128)} %copy-done.4) | copy-start | bytes 9437188
  725.0 11.9 %copy-start.59 = (f32[1,16]{1,0:T(1,128)}, f32[1,16]{1,0:T(1,128)S(1)}, u32[]{:S(2)}) copy-start(f32[1,16]{1,0:T(1,128)S(1)} %dynamic-slice_bitcast_fusion.2) | copy-start | bytes 196
  725.0 11.9 %copy-start.60 = (f32[1,16]{1,0:T(1,128)}, f32[1,16]{1,0:T(1,128)S(1)}, u32[]{:S(2)}) copy-start(f32[1,16]{1,0:T(1,128)S(1)} %dynamic-slice_bitcast_fusion.1) | copy-start | bytes 196
  725.0 7.3 copy-start.8
  725.0 7.3 copy-start.14
  732.3 304.1 %copy-start.17 = (f32[1536,512]{0,1:T(8,128)S(1)}, f32[1536,512]{0,1:T(8,128)}, u32[]{:S(2)}) copy-start(f32[1536,512]{0,1:T(8,128)} %convolution_add_fusion.1) | copy-start | bytes 9437188
  1036.4 40.0 %copy-start.43 = (f32[6,16]{1,0:T(8,128)S(1)}, f32[6,16]{1,0:T(8,128)}, u32[]{:S(2)}) copy-start(f32[6,16]{1,0:T(8,128)} %param.31) | copy-start | bytes 1156
  1036.4 40.0 %copy-start.57 = (f32[6,16]{1,0:T(8,128)S(1)}, f32[6,16]{1,0:T(8,128)}, u32[]{:S(2)}) copy-start(f32[6,16]{1,0:T(8,128)} %param.41) | copy-start | bytes 1156
  1036.4 40.0 %copy-start.58 = (f32[6,16]{1,0:T(8,128)S(1)}, f32[6,16]{1,0:T(8,128)}, u32[]{:S(2)}) copy-start(f32[6,16]{1,0:T(8,128)} %param.36) | copy-start | bytes 1156
  1036.4 42.8 %copy-start.27 = (f32[32,512]{1,0:T(8,128)S(1)}, f32[32,512]{1,0:T(8,128)}, u32[]{:S(2)}) copy-start(f32[32,512]{1,0:T(8,128)} %param.30) | copy-start | bytes 196612
  1036.5 44.4 %copy-start.28 = (f32[16,1024]{1,0:T(8,128)S(1)}, f32[16,1024]{1,0:T(8,128)}, u32[]{:S(2)}) copy-start(f32[16,1024]{1,0:T(8,128)} %param.29) | copy-start | bytes 196612
  1036.5 44.4 %copy-start.29 = (f32[16,1024]{1,0:T(8,128)S(1)}, f32[16,1024]{1,0:T(8,128)}, u32[]{:S(2)}) copy-start(f32[16,1024]{1,0:T(8,128)} %reduce-scatter.12.cloned.1.call-done) | copy-start | bytes 196612
  1036.5 46.0 %copy-start.25 = (f32[16,1536]{1,0:T(8,128)S(1)}, f32[16,1536]{1,0:T(8,128)}, u32[]{:S(2)}) copy-start(f32[16,1536]{1,0:T(8,128)} %reduce-scatter.16.cloned.1.call-done) | copy-start | bytes 294916
  1036.5 45.9 %copy-start.26 = (f32[16,1536]{1,0:T(8,128)S(1)}, f32[16,1536]{1,0:T(8,128)}, u32[]{:S(2)}) copy-start(f32[16,1536]{1,0:T(8,128)} %param.27) | copy-start | bytes 294916
  (26 other events, 62.7 us)
Sparse Core Ops, SparseCore 0:
  11.5 57.6 all-gather.4
  72.6 52.8 all-gather.6
  129.0 52.6 all-gather.8
  394.4 130.4 reduce-scatter.17
  527.0 130.6 reduce-scatter.9
  663.0 97.5 reduce-scatter.15
  762.9 135.6 reduce-scatter.11
  901.0 132.6 reduce-scatter.13
where the time goes:
time: 1100 us; the launch traced here: 1090 us
  waiting for transfers between devices  288 us (26%)
  matrix products  274 us (25%)
  blocking collectives  239 us (22%)
  local copies, waits for them, and re-layouts  142 us (13%)
  other arithmetic  127 us (12%)
  between operations  20.5 us (2%)
    reduce_scatter x1, waiting for transfers between devices, shards(): lax.psum_scatter(grad_down, ('wide', 'narrow'), scatter_dimension=0, tile...  133 us
    reduce_scatter x1, waiting for transfers between devices, shards(): lax.psum_scatter(grad_up, ('wide', 'narrow'), scatter_dimension=0, tiled=...  133 us
    dot_general x6, matrix products, table_scores(): jnp.einsum('qhd,khd->hqk', queries, key_rows, preferred_element_type=jnp....  60.3 us
    convert_element_type x3, other arithmetic, table_backward(): grad_scores = (soft_weights * (grad_soft - delta_rows)).astype(jnp.bfloat16)  56.9 us
    psum x1, blocking collectives, shards(): lax.psum(jnp.sum(image_values, 0), ('wide', 'narrow')) / total_rows  42.1 us
    all_gather x1, blocking collectives, shards(): lax.all_gather(copies[4], ('wide', 'narrow'), axis=1, tiled=True)  41.3 us
    all_gather x1, blocking collectives, shards(): lax.all_gather(copies[1], ('wide', 'narrow'), axis=0, tiled=True)  41.2 us
    psum x1, blocking collectives, shards(): lax.psum(jnp.sum(centred * centred, 0), ('wide', 'narrow')) / total_rows  40.4 us
  transfers between devices with their start and end apart: 8, of which 3 were waited for; matrix products, arithmetic and copies ran while one was open for 44% of the time, Pallas kernels for 0%

commit v1 on v0

v1 whole, which is shorter than its diff:
```python
import functools
import math

import jax
import jax.numpy as jnp
from jax import lax
from jax.experimental import pallas as pl
from jax.experimental.pallas import tpu as pltpu
from jax.sharding import PartitionSpec as P

f32 = jnp.float32
bf = jnp.bfloat16
MESH = pl.DeviceIdType.MESH
HEADS = 8
STEP = 10
EPS = 1e-05
NEG = -1000000000.0
CLIP_AT = 1.0
BETA_FIRST = 0.9
BETA_SECOND = 0.999
ADAM_EPS = 1e-08
RATE_MATRIX = 0.05
RATE_OUTPUT = 1.0
RATE_NORMS = 0.5
DECAY_RATE = 0.1
GC = math.sqrt(2 / math.pi)
GA = 0.044715
AXES = ("wide", "narrow")
VM = pl.BlockSpec(memory_space=pltpu.VMEM)


def dg(a, b, ca, cb):
    return lax.dot_general(a, b, (((ca,), (cb,)), ((), ())), preferred_element_type=f32)


class Place:
    def __init__(self):
        self.w = lax.axis_index("wide")
        self.c = lax.axis_index("narrow")
        self.x = lax.rem(self.w, 2)
        self.y = lax.rem(self.w // 2, 2)
        self.z = self.w // 4
        self.d = self.w * 2 + self.c
        self.to_x = (self.w + 1 - 2 * self.x, self.c)
        self.to_y = (self.w + 2 - 4 * self.y, self.c)
        self.sib = (self.w, 1 - self.c)

    def to_z(self, k):
        return (lax.rem(self.w + 4 * k, 16), self.c)

    def peer(self, k):
        d = lax.rem(self.d + k, 32)
        return (d // 2, lax.rem(d, 2))


def greet_all(me):
    bar = pltpu.get_barrier_semaphore()
    for k in range(1, 32):
        pl.semaphore_signal(bar, inc=1, device_id=me.peer(k), device_id_type=MESH)
    pl.semaphore_wait(bar, 31)


def remote(src, dst, ss, rs, dev):
    return pltpu.make_async_remote_copy(
        src_ref=src, dst_ref=dst, send_sem=ss, recv_sem=rs, device_id=dev, device_id_type=MESH
    )


def push_all(me, src, dst, ss, rs):
    cps = []
    for k in range(1, 32):
        cp = remote(src, dst.at[me.d], ss.at[k], rs.at[k], me.peer(k))
        cp.start()
        cps.append(cp)
    return cps


class Gather:
    SLOTS = 35

    def __init__(self, me, g, ss, rs, split):
        self.me, self.g, self.ss, self.rs = me, g, ss, rs
        n = g.shape[-1]
        self.h = n // 2 if split else n
        self.split = split
        self.sent = []

    def blk(self, kz, pos):
        me = self.me
        z = lax.rem(me.z + 4 - kz, 4)
        y = me.y if pos in (0, 1) else 1 - me.y
        x = me.x if pos in (0, 2) else 1 - me.x
        return z, y, x

    def ref(self, kz, pos, lanes=None, c=None):
        z, y, x = self.blk(kz, pos)
        c = self.me.c if c is None else c
        if lanes is None:
            return self.g.at[z, y, x, c]
        return self.g.at[z, y, x, c, :, lanes]

    def go(self, ref, slot, dev):
        cp = remote(ref, ref, self.ss.at[slot], self.rs.at[slot], dev)
        cp.start()
        self.sent.append(cp)

    def got(self, ref, slot):
        remote(ref, ref, self.ss.at[slot], self.rs.at[slot], self.me.sib).wait_recv()

    def start(self):
        me = self.me
        own = self.ref(0, 0)
        for k in (1, 2, 3):
            self.go(own, k - 1, me.to_z(k))
        self.go(own, 3, me.to_x)
        self.go(own, 7, me.to_y)
        self.go(own, 19, me.sib)

    def column(self):
        me = self.me
        for k in (1, 3, 2):
            r = self.ref(k, 0)
            self.got(r, k - 1)
            self.go(r, 3 + k, me.to_x)
            self.go(r, 7 + k, me.to_y)
            self.go(r, 19 + k, me.sib)

    def plane(self):
        me = self.me
        for k in (0, 1, 3, 2):
            r = self.ref(k, 1)
            self.got(r, 3 + k)
            self.go(self.ref(k, 1, pl.ds(0, self.h)), 11 + k, me.to_y)
            self.go(r, 23 + k, me.sib)
            r = self.ref(k, 2)
            self.got(r, 7 + k)
            if self.split:
                self.go(self.ref(k, 2, pl.ds(self.h, self.h)), 15 + k, me.to_x)
            self.go(r, 27 + k, me.sib)

    def corner(self):
        me = self.me
        for k in (0, 1, 3, 2):
            self.got(self.ref(k, 3, pl.ds(0, self.h)), 11 + k)
            if self.split:
                self.got(self.ref(k, 3, pl.ds(self.h, self.h)), 15 + k)
            self.go(self.ref(k, 3), 31 + k, me.sib)

    def finish(self):
        for pos in range(4):
            for k in range(4):
                self.got(self.ref(k, pos, c=1 - self.me.c), 19 + 4 * pos + k)
        for cp in self.sent:
            cp.wait_send()


def gather_kernel(
    img_ref, wqkv_ref, wout_ref, wup_ref, wdn_ref, norm_ref,
    gq, gr, gd, stats_ref, gains_ref,
    gn, st, sq_s, sq_r, sr_s, sr_r, sd_s, sd_r, sn_s, sn_r, st_s, st_r,
):
    me = Place()
    D = wqkv_ref.shape[1] // 3
    F = wup_ref.shape[1]
    own = (me.z, me.y, me.x, me.c)
    gq[own] = wqkv_ref[...].astype(bf)
    gr[own + (slice(None), pl.ds(0, D))] = wout_ref[...].astype(bf)
    gr[own + (slice(None), pl.ds(D, F))] = wup_ref[...].astype(bf)
    gd[own] = wdn_ref[...].astype(bf)
    lane = lax.broadcasted_iota(jnp.int32, (16, 128), 1)
    unit = lax.broadcasted_iota(jnp.int32, (16, 128), 0)
    at = (lane == unit + 16 * lax.rem(me.d, 8)).astype(bf)
    tile = dg(norm_ref[...].astype(bf), at, 1, 0)
    gn[own] = jnp.concatenate([tile, jnp.zeros((10, 128), f32)], 0).astype(bf)
    greet_all(me)
    q = Gather(me, gq, sq_s, sq_r, True)
    n = Gather(me, gn, sn_s, sn_r, False)
    r = Gather(me, gr, sr_s, sr_r, True)
    dn = Gather(me, gd, sd_s, sd_r, True)
    q.start()
    n.start()
    rows = img_ref.shape[0]
    step = rows // 3
    total = jnp.zeros((1, D), f32)
    for i in range(3):
        total += jnp.sum(img_ref[i * step : (i + 1) * step, :].astype(f32), 0, keepdims=True)
    mean_d = total / rows
    m2 = jnp.zeros((1, D), f32)
    for i in range(3):
        cen = img_ref[i * step : (i + 1) * step, :].astype(f32) - mean_d
        m2 += jnp.sum(cen * cen, 0, keepdims=True)
    mine = jnp.concatenate(
        [mean_d[:, g * 128 : (g + 1) * 128] for g in range(4)] + [m2[:, g * 128 : (g + 1) * 128] for g in range(4)], 0
    )
    st[me.d] = mine
    cps = push_all(me, st.at[me.d], st, st_s, st_r)
    q.column()
    n.column()
    r.start()
    dn.start()
    q.plane()
    n.plane()
    q.corner()
    n.corner()
    r.column()
    dn.column()
    r.plane()
    dn.plane()
    r.corner()
    dn.corner()
    for k in range(1, 32):
        cps[k - 1].wait_send()
        src = lax.rem(me.d + 32 - k, 32)
        remote(st.at[src], st.at[src], st_s.at[k], st_r.at[k], me.sib).wait_recv()
    mean = jnp.sum(st[:, 0:4, :], 0) / 32
    off = st[:, 0:4, :] - mean[None]
    spread = (jnp.sum(st[:, 4:8, :], 0) + rows * jnp.sum(off * off, 0)) / (rows * 32)
    inv = lax.rsqrt(spread + EPS)
    for g in range(4):
        stats_ref[0:1, g * 128 : (g + 1) * 128] = mean[g : g + 1, :]
        stats_ref[1:2, g * 128 : (g + 1) * 128] = inv[g : g + 1, :]
    for part in (q, n, r, dn):
        part.finish()
    for z in range(4):
        acc = jnp.zeros((16, 128), f32)
        for y in range(2):
            for x in range(2):
                for c in range(2):
                    acc += gn[z, y, x, c].astype(f32)
        gains_ref[:, z * 128 : (z + 1) * 128] = acc[0:8, :]


def gather(img, wqkv, wout, wup, wdn, norm):
    D = img.shape[1]
    F = wup.shape[1]
    R, RD = wqkv.shape[0], wdn.shape[0]
    dims = (4, 2, 2, 2)
    dma = pltpu.SemaphoreType.DMA
    S = Gather.SLOTS
    outs = pl.pallas_call(
        gather_kernel,
        out_shape=[
            jax.ShapeDtypeStruct(dims + (R, 3 * D), bf),
            jax.ShapeDtypeStruct(dims + (R, D + F), bf),
            jax.ShapeDtypeStruct(dims + (RD, D), bf),
            jax.ShapeDtypeStruct((2, D), f32),
            jax.ShapeDtypeStruct((8, D), f32),
        ],
        in_specs=[VM] * 6,
        out_specs=[VM] * 5,
        scratch_shapes=[pltpu.VMEM(dims + (16, 128), bf), pltpu.VMEM((32, 8, 128), f32)]
        + [dma((S,))] * 8
        + [dma((32,))] * 2,
        compiler_params=pltpu.CompilerParams(collective_id=0, has_side_effects=True, vmem_limit_bytes=40 * 2**20),
        name="gather",
    )(img, wqkv, wout, wup, wdn, norm)
    gq, gr, gd, stats, gains = outs
    return gq.reshape(D, 3 * D), gr.reshape(D, D + F), gd.reshape(F, D), stats, gains


class Scatter:
    SLOTS = 8

    def __init__(self, me, g, out, bufs, ss, rs):
        self.me, self.g, self.out, self.ss, self.rs = me, g, out, ss, rs
        self.r0, self.s0, self.r1a, self.r1b, self.s1a, self.s1b, self.r2a, self.r2b, self.s2, self.r3 = bufs
        self.h = g.shape[-1] // 2
        self.sent = []

    @staticmethod
    def bufs(R, N):
        h = N // 2
        v = lambda *s: pltpu.VMEM(s, bf)
        return [
            v(4, 2, 2, R, N), v(4, 2, 2, R, N), v(4, 2, R, h), v(4, 2, R, h), v(4, 2, R, h), v(4, 2, R, h),
            v(4, R, h), v(4, R, h), v(4, R, N), v(3, R, N),
        ]

    def go(self, src, dst, slot, dev):
        cp = remote(src, dst, self.ss.at[slot], self.rs.at[slot], dev)
        cp.start()
        self.sent.append(cp)

    def got(self, dst, slot):
        remote(dst, dst, self.ss.at[slot], self.rs.at[slot], self.me.sib).wait_recv()

    def core(self):
        me = self.me
        self.go(self.g.at[:, :, :, 1 - me.c], self.r0, 0, me.sib)

    def plane1(self):
        me, h = self.me, self.h
        self.got(self.r0, 0)

        def add(i, _):
            k = (i // 4, lax.rem(i // 2, 2), lax.rem(i, 2))
            self.s0[k] = (self.g[k + (me.c,)].astype(f32) + self.r0[k].astype(f32)).astype(bf)
            return 0

        lax.fori_loop(0, 16, add, 0)
        self.go(self.s0.at[:, :, 1 - me.x, :, pl.ds(0, h)], self.r1a, 1, me.to_x)
        self.go(self.s0.at[:, 1 - me.y, :, :, pl.ds(h, h)], self.r1b, 2, me.to_y)

    def plane2(self):
        me, h = self.me, self.h
        self.got(self.r1a, 1)
        self.got(self.r1b, 2)

        def add(i, _):
            z, k = i // 2, lax.rem(i, 2)
            a = self.s0[z, k, me.x, :, pl.ds(0, h)].astype(f32) + self.r1a[z, k].astype(f32)
            self.s1a[z, k] = a.astype(bf)
            b = self.s0[z, me.y, k, :, pl.ds(h, h)].astype(f32) + self.r1b[z, k].astype(f32)
            self.s1b[z, k] = b.astype(bf)
            return 0

        lax.fori_loop(0, 8, add, 0)
        self.go(self.s1a.at[:, 1 - me.y], self.r2a, 3, me.to_y)
        self.go(self.s1b.at[:, 1 - me.x], self.r2b, 4, me.to_x)

    def column(self):
        me, h = self.me, self.h
        self.got(self.r2a, 3)
        self.got(self.r2b, 4)
        for z in range(4):
            self.s2[z, :, 0:h] = (self.s1a[z, me.y].astype(f32) + self.r2a[z].astype(f32)).astype(bf)
            self.s2[z, :, h:] = (self.s1b[z, me.x].astype(f32) + self.r2b[z].astype(f32)).astype(bf)
        for k in (2, 1, 3):
            self.go(self.s2.at[lax.rem(me.z + k, 4)], self.r3.at[k - 1], 4 + k, me.to_z(k))

    def finish(self):
        me = self.me
        acc = self.s2[me.z].astype(f32)
        for k in (1, 2, 3):
            self.got(self.r3.at[k - 1], 4 + k)
            acc += self.r3[k - 1].astype(f32)
        self.out[...] = acc
        for cp in self.sent:
            cp.wait_send()
        return jnp.sum(acc * acc)


def scatter_kernel(gq, gr, gd, terms, bnsum, oq, orr, od, small, nsq, *rest):
    bq, br, bd = rest[0:10], rest[10:20], rest[20:30]
    tb, nb, q_s, q_r, r_s, r_r, d_s, d_r, t_s, t_r, n_s, n_r = rest[30:]
    me = Place()
    D = terms.shape[1]
    tb[0, 0:4, :] = terms[...]
    tb[0, 4:6, :] = bnsum[...]
    tb[0, 6:8, :] = jnp.zeros((2, D), f32)
    greet_all(me)
    d = Scatter(me, gd, od, bd, d_s, d_r)
    r = Scatter(me, gr, orr, br, r_s, r_r)
    q = Scatter(me, gq, oq, bq, q_s, q_r)
    tsent = []

    def tgo(src, dst, slot, dev):
        cp = remote(tb.at[src], tb.at[dst], t_s.at[slot], t_r.at[slot], dev)
        cp.start()
        tsent.append(cp)

    def tgot(dst, slot):
        remote(tb.at[dst], tb.at[dst], t_s.at[slot], t_r.at[slot], me.sib).wait_recv()

    tgo(0, 1, 0, me.sib)
    for a in (d, r, q):
        a.core()
    tgot(1, 0)
    tb[2] = tb[0] + tb[1]
    tgo(2, 3, 1, me.to_x)
    d.plane1()
    r.plane1()
    tgot(3, 1)
    tb[4] = tb[2] + tb[3]
    tgo(4, 5, 2, me.to_y)
    d.plane2()
    q.plane1()
    tgot(5, 2)
    tb[6 + me.z] = tb[4] + tb[5]
    for k in (1, 2, 3):
        tgo(6 + me.z, 6 + me.z, 2 + k, me.to_z(k))
    d.column()
    r.plane2()
    q.plane2()
    r.column()
    q.column()
    sq = d.finish()
    for k in (1, 2, 3):
        tgot(6 + lax.rem(me.z + 4 - k, 4), 2 + k)
    tot = (tb[6] + tb[7]) + (tb[8] + tb[9])
    small[...] = tot
    sq += r.finish()
    sq += q.finish()
    for cp in tsent:
        cp.wait_send()
    nb[me.d] = jnp.full((8, 128), sq, f32)
    cps = push_all(me, nb.at[me.d], nb, n_s, n_r)
    for k in range(1, 32):
        cps[k - 1].wait_send()
        src = lax.rem(me.d + 32 - k, 32)
        remote(nb.at[src], nb.at[src], n_s.at[k], n_r.at[k], me.sib).wait_recv()
    nsq[...] = jnp.sum(nb[...], 0) + jnp.sum(tot * tot)


def scatter(gq, gr, gd, terms, bnsum):
    D, F = terms.shape[1], gd.shape[0]
    R, RD = D // 32, F // 32
    dims = (4, 2, 2, 2)
    dma = pltpu.SemaphoreType.DMA
    return pl.pallas_call(
        scatter_kernel,
        out_shape=[
            jax.ShapeDtypeStruct((R, 3 * D), f32),
            jax.ShapeDtypeStruct((R, D + F), f32),
            jax.ShapeDtypeStruct((RD, D), f32),
            jax.ShapeDtypeStruct((8, D), f32),
            jax.ShapeDtypeStruct((8, 128), f32),
        ],
        in_specs=[VM] * 5,
        out_specs=[VM] * 5,
        scratch_shapes=Scatter.bufs(R, 3 * D)
        + Scatter.bufs(R, D + F)
        + Scatter.bufs(RD, D)
        + [pltpu.VMEM((10, 8, D), f32), pltpu.VMEM((32, 8, 128), f32)]
        + [dma((Scatter.SLOTS,))] * 6
        + [dma((6,))] * 2
        + [dma((32,))] * 2,
        compiler_params=pltpu.CompilerParams(collective_id=1, has_side_effects=True, vmem_limit_bytes=40 * 2**20),
        name="scatter",
    )(
        gq.reshape(dims + (R, 3 * D)), gr.reshape(dims + (R, D + F)), gd.reshape(dims + (RD, D)), terms, bnsum
    )


def k2_body(counts, tag_ref, img_ref, cot_ref, stats_ref, wqkv_ref, wr_ref, wdn_ref, gains_ref,
            mixed_ref, gtags_ref, gz_ref, gqkv_ref, gr_ref, gdn_ref, terms_ref, bnsum_ref,
            imglow_s, kall, vall, kT, vT, q_s, qT, bias_s, s_s, e_s, attT, oT_s, rl_s,
            hidlow_s, act_s, rlow_s, plow_s, hplow_s, ghp_s, dqkv_s, dkvi_s, dqT_s, dO_s, dOT_s, del_s,
            aqkv, aout, aup, adn):
    t = pl.program_id(0)
    T, D = tag_ref.shape
    I = img_ref.shape[0]
    NK = T + I
    hd = D // HEADS
    F = wdn_ref.shape[0]
    wout_ref = wr_ref.at[:, 0:D]
    wup_ref = wr_ref.at[:, D:D + F]
    count = counts[t]

    @pl.when(t == 0)
    def _():
        aqkv[...] = jnp.zeros_like(aqkv); aout[...] = jnp.zeros_like(aout)
        aup[...] = jnp.zeros_like(aup); adn[...] = jnp.zeros_like(adn)
        terms_ref[...] = jnp.zeros_like(terms_ref); bnsum_ref[...] = jnp.zeros_like(bnsum_ref)

    mean = stats_ref[0:1, :]; inv = stats_ref[1:2, :]
    g1 = gains_ref[0:1, :]; b1 = gains_ref[1:2, :]; g2 = gains_ref[2:3, :]; b2 = gains_ref[3:4, :]
    gb = gains_ref[4:5, :]; bb = gains_ref[5:6, :]

    x = tag_ref[...]
    for r0, rl in ((0, 256), (256, 256), (512, I - 512)):
        img_hat = (img_ref[r0:r0 + rl, :].astype(f32) - mean) * inv
        imglow_s[r0:r0 + rl, :] = (img_hat * gb + bb).astype(bf)
    for r0 in range(0, T, 256):
        q = dg(tag_ref[r0:r0 + 256, :], wqkv_ref[:, 0:D], 1, 0).astype(bf) * bf(1.0 / math.sqrt(hd))
        q_s[r0:r0 + 256, :] = q
        qT[:, r0:r0 + 256] = q.T
    for j,(dst, dstT) in enumerate(((kall, kT), (vall, vT))):
        w = wqkv_ref[:, (j + 1) * D:(j + 2) * D]
        for r0 in range(0, T, 256):
            a = dg(tag_ref[r0:r0 + 256, :], w, 1, 0).astype(bf)
            dst[r0:r0 + 256, :] = a
            dstT[:, r0:r0 + 256] = a.T
        for r0, rl in ((0, 256), (256, 256), (512, I - 512)):
            a = dg(imglow_s[r0:r0 + rl, :], w, 1, 0).astype(bf)
            dst[T + r0:T + r0 + rl, :] = a
            dstT[:, T + r0:T + r0 + rl] = a.T
    ji = lax.broadcasted_iota(jnp.int32, (T, T), 0); ii = lax.broadcasted_iota(jnp.int32, (T, T), 1)
    bias_s[...] = jnp.where((ji <= ii) & (ji < count), 3e38, NEG)

    chunks = [(0, 256, 0), (256, 256, 256), (512, 256, 0), (768, 256, 0), (1024, NK - 1024, 0)]
    row64 = lax.broadcasted_iota(jnp.int32, (2 * hd, 1), 0)
    lane64 = lax.broadcasted_iota(jnp.int32, (1, 2 * hd), 1)
    def own_rows(a, h):
        keep = (row64 < hd) if h % 2 == 0 else (row64 >= hd)
        return jnp.where(keep, a, jnp.zeros_like(a))
    def own_lanes(a, h):
        keep = (lane64 < hd) if h % 2 == 0 else (lane64 >= hd)
        return jnp.where(keep, a, jnp.zeros_like(a))
    def pr(h): return slice(h // 2 * 2 * hd, (h // 2 + 1) * 2 * hd)

    def fullq(a, q0, fill):
        if q0 == 0: return a
        return jnp.concatenate([jnp.full((a.shape[0], q0), fill, a.dtype), a], 1)

    def A(h, c, qz):
        k0, kl, q0 = chunks[c]
        s = dg(kall[k0:k0 + kl, pr(h)], qz[:, q0:], 1, 0)
        if k0 < T:
            s = jnp.minimum(s, bias_s[k0:k0 + kl, q0:])
        s_s[h % 2, k0:k0 + kl, q0:] = s
        return fullq(jnp.max(s, 0, keepdims=True), q0, NEG)
    def B(h, c, m):
        k0, kl, q0 = chunks[c]
        e = jnp.exp(s_s[h % 2, k0:k0 + kl, q0:] - m[:, q0:])
        l = jnp.sum(e, 0, keepdims=True)
        e = e.astype(bf)
        e_s[h, k0:k0 + kl, q0:] = e
        o = dg(vT[h * hd:(h + 1) * hd, k0:k0 + kl], e, 1, 0)
        return fullq(o, q0, 0.0), fullq(l, q0, 0.0)
    nc = len(chunks)
    def fwd_pair(p, _):
        ps = pl.ds(pl.multiple_of(p * 2 * hd, 2 * hd), 2 * hd)
        qzs = [own_rows(qT[ps, :], b) for b in range(2)]
        def A(b, c):
            k0, kl, q0 = chunks[c]
            s = dg(kall[k0:k0 + kl, ps], qzs[b][:, q0:], 1, 0)
            if k0 < T:
                s = jnp.minimum(s, bias_s[k0:k0 + kl, q0:])
            s_s[b, k0:k0 + kl, q0:] = s
            return fullq(jnp.max(s, 0, keepdims=True), q0, NEG)
        def B(b, c, m):
            k0, kl, q0 = chunks[c]
            e = jnp.exp(s_s[b, k0:k0 + kl, q0:] - m[:, q0:])
            l = jnp.sum(e, 0, keepdims=True)
            e = e.astype(bf)
            e_s[2 * p + b, k0:k0 + kl, q0:] = e
            o = dg(vT[pl.ds(pl.multiple_of(p * 2 * hd + b * hd, hd), hd), k0:k0 + kl], e, 1, 0)
            return fullq(o, q0, 0.0), fullq(l, q0, 0.0)
        def done(b, o, l):
            rl = 1.0 / l
            o = o * rl
            hs = pl.ds(pl.multiple_of(p * 2 * hd + b * hd, hd), hd)
            oT_s[hs, :] = o
            attT[hs, :] = o.astype(bf)
            rl_s[2 * p + b] = rl
        m0 = None
        for c in range(nc):
            mc = A(0, c); m0 = mc if m0 is None else jnp.maximum(m0, mc)
        m1 = None; o = None
        for c in range(nc):
            mc = A(1, c); m1 = mc if m1 is None else jnp.maximum(m1, mc)
            oc, lc = B(0, c, m0)
            o, l = (oc, lc) if o is None else (o + oc, l + lc)
        done(0, o, l)
        o = None
        for c in range(nc):
            oc, lc = B(1, c, m1)
            o, l = (oc, lc) if o is None else (o + oc, l + lc)
        done(1, o, l)
        return 0
    lax.fori_loop(0, HEADS // 2, fwd_pair, 0)

    tg2 = jnp.zeros((1, D), f32); tb2 = tg2; tg1 = tg2; tb1 = tg2
    RC = 128
    def rows_part(i, tg):
        tg1, tb1, tg2, tb2 = tg
        r0 = pl.multiple_of(i * RC, RC)
        rs = pl.ds(r0, RC)
        hp = tag_ref[rs, :].astype(f32) + dg(attT[:, rs], wout_ref[...], 0, 0)
        c = hp - jnp.mean(hp, -1, keepdims=True)
        inv1 = lax.rsqrt(jnp.mean(c * c, -1, keepdims=True) + EPS)
        hat1 = c * inv1
        hidden = hat1 * g1 + b1
        hl = hidden.astype(bf)
        hidlow_s[rs, :] = hl
        pre = dg(hl, wup_ref[...], 1, 0)
        p2 = pre * pre
        th = jnp.tanh(GC * (pre + GA * (p2 * pre)))
        act = (0.5 * pre * (1.0 + th)).astype(bf)
        act_s[rs, :] = act
        gp = 0.5 * (1.0 + th) + 0.5 * pre * (1.0 - th * th) * (GC * (1.0 + 3 * GA * p2))
        resid = hidden + dg(act, wdn_ref[...], 1, 0)
        c = resid - jnp.mean(resid, -1, keepdims=True)
        inv2 = lax.rsqrt(jnp.mean(c * c, -1, keepdims=True) + EPS)
        hat2 = c * inv2
        mixed_ref[rs, :] = (hat2 * g2 + b2).astype(bf)
        rows = r0 + lax.broadcasted_iota(jnp.int32, (RC, 1), 0)
        go = jnp.where(rows < count, cot_ref[rs, :].astype(f32), 0.0)
        tg2 += jnp.sum(go * hat2, 0, keepdims=True); tb2 += jnp.sum(go, 0, keepdims=True)
        s = go * g2
        gr = inv2 * (s - jnp.mean(s, -1, keepdims=True) - hat2 * jnp.mean(s * hat2, -1, keepdims=True))
        rlow = gr.astype(bf)
        rlow_s[rs, :] = rlow
        plow = (dg(rlow, wdn_ref[...], 1, 1) * gp).astype(bf)
        plow_s[rs, :] = plow
        gh = gr + dg(plow, wup_ref[...], 1, 1)
        tg1 += jnp.sum(gh * hat1, 0, keepdims=True); tb1 += jnp.sum(gh, 0, keepdims=True)
        s = gh * g1
        ghp = inv1 * (s - jnp.mean(s, -1, keepdims=True) - hat1 * jnp.mean(s * hat1, -1, keepdims=True))
        ghp_s[rs, :] = ghp
        hpl = ghp.astype(bf)
        hplow_s[rs, :] = hpl
        dO = dg(hpl, wout_ref[...], 1, 1).astype(bf)
        dOT_s[:, rs] = dO.T
        return tg1, tb1, tg2, tb2
    tg1, tb1, tg2, tb2 = lax.fori_loop(0, T // RC, rows_part, (tg1, tb1, tg2, tb2))
    terms_ref[0:1, :] += tg1; terms_ref[1:2, :] += tb1; terms_ref[2:3, :] += tg2; terms_ref[3:4, :] += tb2
    for h in range(HEADS):
        hs = slice(h * hd, (h + 1) * hd)
        d = dOT_s[hs, :].astype(f32) * rl_s[h]
        dOT_s[hs, :] = d.astype(bf)
        del_s[h] = jnp.sum(d * oT_s[hs, :], 0, keepdims=True)
    dO_s[...] = dOT_s[...].T

    for r0 in range(0, D, 256):
        aout[r0:r0 + 256, :] += dg(attT[r0:r0 + 256, :], hplow_s[...], 1, 0)
        for c0 in range(0, F, 512):
            aup[r0:r0 + 256, c0:c0 + 512] += dg(hidlow_s[:, r0:r0 + 256], plow_s[:, c0:c0 + 512], 0, 0)
    for r0 in range(0, F, 256):
        adn[r0:r0 + 256, :] += dg(act_s[:, r0:r0 + 256], rlow_s[...], 0, 0)

    def bwd_pair(p, _):
        p128 = pl.multiple_of(p * 2 * hd, 2 * hd)
        ps = pl.ds(p128, 2 * hd)
        dq = [None, None]
        ops = []
        for b in range(2):
            ops.append((own_rows(dOT_s[ps, :], b), own_lanes(dO_s[:, ps], b), own_lanes(q_s[:, ps], b)))
        for c in range(nc):
            k0, kl, q0 = chunks[c]
            ks = slice(k0, k0 + kl)
            dk = None
            for b in range(2):
                h = 2 * p + b
                hs = pl.ds(pl.multiple_of(p * 2 * hd + b * hd, hd), hd)
                dOz, dOl, ql = ops[b]
                dp = dg(vall[ks, ps], dOz[:, q0:], 1, 0)
                e = e_s[h, ks, q0:]
                ds = (e.astype(f32) * (dp - del_s[h][:, q0:])).astype(bf)
                dvc = dg(e, dOl[q0:, :], 1, 0)
                dkc = dg(ds, ql[q0:, :], 1, 0)
                dqc = fullq(dg(kT[hs, ks], ds, 1, 0), q0, 0.0)
                dk, dv = (dkc, dvc) if dk is None else (dk + dkc, dv + dvc)
                dq[b] = dqc if dq[b] is None else dq[b] + dqc
            kc = pl.ds(pl.multiple_of(D + p128, 128), 2 * hd); vc = pl.ds(pl.multiple_of(2 * D + p128, 128), 2 * hd)
            if k0 < T:
                dqkv_s[ks, kc] = dk.astype(bf)
                dqkv_s[ks, vc] = dv.astype(bf)
            else:
                si = slice(k0 - T, k0 - T + kl)
                dkvi_s[si, ps] = dk.astype(bf)
                dkvi_s[si, kc] = dv.astype(bf)
        for b in range(2):
            hs = pl.ds(pl.multiple_of(p * 2 * hd + b * hd, hd), hd)
            dqT_s[hs, :] = (dq[b] * (1.0 / math.sqrt(hd))).astype(bf)
        return 0
    lax.fori_loop(0, HEADS // 2, bwd_pair, 0)
    dqkv_s[:, 0:D] = dqT_s[...].T

    for r0 in range(0, T, 256):
        gtags_ref[r0:r0 + 256, :] = ghp_s[r0:r0 + 256, :] + dg(dqkv_s[r0:r0 + 256, :], wqkv_ref[...], 1, 1)
    sg = jnp.zeros((1, D), f32); sb = sg
    for r0, rl in ((0, 256), (256, 256), (512, I - 512)):
        rs = slice(r0, r0 + rl)
        gz = dg(dkvi_s[rs, :], wqkv_ref[:, D:], 1, 1)
        gz_ref[rs, :] = gz
        hat = (img_ref[rs, :].astype(f32) - mean) * inv
        sg += jnp.sum(gz * hat, 0, keepdims=True); sb += jnp.sum(gz, 0, keepdims=True)
    bnsum_ref[0:1, :] += sg; bnsum_ref[1:2, :] += sb
    for r0 in range(0, D, 256):
        rs = slice(r0, r0 + 256)
        aqkv[rs, 0:D] += dg(tag_ref[:, rs], dqkv_s[:, 0:D], 0, 0)
        for c0 in range(D, 3 * D, 512):
            aqkv[rs, c0:c0 + 512] += dg(tag_ref[:, rs], dqkv_s[:, c0:c0 + 512], 0, 0) + dg(imglow_s[:, rs], dkvi_s[:, c0 - D:c0 - D + 512], 0, 0)

    @pl.when(t == pl.num_programs(0) - 1)
    def _():
        gqkv_ref[...] = aqkv[...].astype(bf); gr_ref[:, 0:D] = aout[...].astype(bf)
        gr_ref[:, D:D + F] = aup[...].astype(bf); gdn_ref[...] = adn[...].astype(bf)

def tables_call(counts, tag, img, cot, stats, wqkv, wr, wdn, gains):
    n = counts.shape[0]
    T = tag.shape[0] // n; I = img.shape[0] // n; D = tag.shape[1]; F = wdn.shape[0]; NK = T + I
    V = lambda *s, d=bf: pltpu.VMEM(s, d)
    def row(r, c): return pl.BlockSpec((r, c), lambda t, *_: (t, 0))
    def whole(a): return pl.BlockSpec(a.shape, lambda t, *_: (0, 0), pipeline_mode=pl.Buffered(1))
    def wholeo(r, c): return pl.BlockSpec((r, c), lambda t, *_: (0, 0))
    outs = [((n * T, D), bf, row(T, D)), ((n * T, D), f32, row(T, D)), ((n * I, D), f32, row(I, D)),
            ((D, 3 * D), bf, wholeo(D, 3 * D)), ((D, D + F), bf, wholeo(D, D + F)), ((F, D), bf, wholeo(F, D)),
            ((4, D), f32, wholeo(4, D)), ((2, D), f32, wholeo(2, D))]
    return pl.pallas_call(
        k2_body,
        out_shape=[jax.ShapeDtypeStruct(s, d) for s, d, _ in outs],
        grid_spec=pltpu.PrefetchScalarGridSpec(
            num_scalar_prefetch=1, grid=(n,),
            in_specs=[row(T, D), row(I, D), row(T, D)] + [whole(a) for a in (stats, wqkv, wr, wdn, gains)],
            out_specs=[s for _, _, s in outs],
            scratch_shapes=[V(I, D), V(NK, D), V(NK, D), V(D, NK), V(D, NK), V(T, D), V(D, T), V(T, T, d=f32),
                V(2, NK, T, d=f32), V(HEADS, NK, T), V(D, T), V(D, T, d=f32), V(HEADS, 1, T, d=f32),
                V(T, D), V(T, F), V(T, D), V(T, F), V(T, D), V(T, D, d=f32), V(T, 3 * D), V(I, 2 * D), V(D, T), V(T, D), V(D, T),
                V(HEADS, 1, T, d=f32),
                V(D, 3 * D, d=f32), V(D, D, d=f32), V(D, F, d=f32), V(F, D, d=f32)]),
        compiler_params=pltpu.CompilerParams(vmem_limit_bytes=62 * 2**20),
        name="tables",
    )(counts, tag, img, cot, stats, wqkv, wr, wdn, gains)


def update_kernel(
    place, gz_ref, img_ref, stats_ref, gains_ref, small_ref, nsq_ref, oq, orr, od,
    w0, w1, w2, w3, w4, f0, f1, f2, f3, f4, v0, v1, v2, v3, v4,
    gimg_ref, norm_ref, *outs
):
    D = gz_ref.shape[1]
    total_rows = place[1].astype(f32)
    gb = gains_ref[4:5, :]
    k = stats_ref[1:2, :] * gb
    gsum = small_ref[4:5, :]
    bsum = small_ref[5:6, :]
    hat = (img_ref[...].astype(f32) - stats_ref[0:1, :]) * stats_ref[1:2, :]
    gimg_ref[...] = k * (gz_ref[...] - bsum / total_rows - hat * (gsum / total_rows))

    @pl.when(pl.program_id(0) == 0)
    def _():
        total_norm = jnp.sqrt(nsq_ref[0:1, 0:1])
        norm_ref[...] = total_norm
        factor = CLIP_AT / jnp.maximum(total_norm, CLIP_AT)
        cols = w4.shape[1]
        row = lax.broadcasted_iota(jnp.int32, (D, cols), 0)
        col = lax.broadcasted_iota(jnp.int32, (D, cols), 1)
        pick = (row == col + place[0] * cols).astype(f32)
        own = lax.dot_general(
            small_ref[...], pick, (((1,), (0,)), ((), ())), precision=lax.Precision.HIGHEST, preferred_element_type=f32
        )[0:6]
        grads = (oq[...], orr[:, 0:D], orr[:, D:], od[...], own)
        rates = (RATE_MATRIX, RATE_OUTPUT, RATE_MATRIX, RATE_MATRIX, RATE_NORMS)
        for i, (g, w, f, v) in enumerate(zip(grads, (w0, w1, w2, w3, w4), (f0, f1, f2, f3, f4), (v0, v1, v2, v3, v4))):
            clip = g * factor
            moment = BETA_FIRST * f[...] + (1.0 - BETA_FIRST) * clip
            square = BETA_SECOND * v[...] + (1.0 - BETA_SECOND) * clip * clip
            u = (moment / (1.0 - BETA_FIRST**STEP)) / (jnp.sqrt(square / (1.0 - BETA_SECOND**STEP)) + ADAM_EPS)
            if i < 4:
                new = w[...] - rates[i] * (u + DECAY_RATE * w[...])
            else:
                new = w[...] - rates[i] * u
            outs[i][...] = clip
            outs[5 + i][...] = moment
            outs[10 + i][...] = square
            outs[15 + i][...] = new
            outs[20 + i][...] = new.astype(bf)


def update(place, gz, img, stats, gains, small, nsq, owned, masters, firsts, seconds, steps):
    rows, D = gz.shape
    block = rows // steps

    def whole(a):
        return pl.BlockSpec(a.shape, lambda t, *_: (0, 0))

    tile = pl.BlockSpec((block, D), lambda t, *_: (t, 0))
    small_in = (stats, gains, small, nsq) + tuple(owned) + tuple(masters) + tuple(firsts) + tuple(seconds)
    shapes = [jax.ShapeDtypeStruct(m.shape, f32) for m in masters] * 4 + [jax.ShapeDtypeStruct(m.shape, bf) for m in masters]
    one = jax.ShapeDtypeStruct((1, 1), f32)
    return pl.pallas_call(
        update_kernel,
        out_shape=[jax.ShapeDtypeStruct((rows, D), f32), one] + shapes,
        grid_spec=pltpu.PrefetchScalarGridSpec(
            num_scalar_prefetch=1,
            grid=(steps,),
            in_specs=[tile, tile] + [whole(a) for a in small_in],
            out_specs=[tile, whole(one)] + [whole(a) for a in shapes],
        ),
        compiler_params=pltpu.CompilerParams(vmem_limit_bytes=40 * 2**20),
        name="update",
    )(place, gz, img, *small_in)


def gather_any(img, wqkv, wout, wup, wdn, norm):
    full = lambda a, axis: lax.all_gather(a.astype(bf), AXES, axis=axis, tiled=True)
    gr = jnp.concatenate([full(wout, 0), full(wup, 0)], 1)
    gains = jnp.concatenate([full(norm, 1).astype(f32), jnp.zeros((2, img.shape[1]), f32)], 0)
    values = img.astype(f32)
    total = img.shape[0] * lax.axis_size(AXES)
    mean = lax.psum(jnp.sum(values, 0), AXES) / total
    centred = values - mean
    spread = lax.psum(jnp.sum(centred * centred, 0), AXES) / total
    return full(wqkv, 0), gr, full(wdn, 0), jnp.stack([mean, lax.rsqrt(spread + EPS)]), gains


def scatter_any(gq, gr, gd, terms, bnsum):
    part = lambda a: lax.psum_scatter(a.astype(f32), AXES, scatter_dimension=0, tiled=True)
    oq, orr, od = part(gq), part(gr), part(gd)
    small = lax.psum(jnp.concatenate([terms, bnsum, jnp.zeros_like(bnsum)], 0), AXES)
    local = jnp.sum(oq * oq) + jnp.sum(orr * orr) + jnp.sum(od * od)
    nsq = lax.psum(local, AXES) + jnp.sum(small * small)
    return oq, orr, od, small, jnp.full((8, 128), nsq, f32)


def shards(direct, tag_inputs, image_inputs, tag_counts, cotangent, *params):
    masters, firsts, seconds = params[0:5], params[5:10], params[10:15]
    tables = tag_counts.shape[0]
    devices = lax.axis_size(AXES)
    total_rows = image_inputs.shape[0] * devices
    wq, wr, wd, stats, gains = (gather if direct else gather_any)(image_inputs, *masters)
    mixed, gtags, gz, gq, gr, gd, terms, bnsum = tables_call(
        tag_counts, tag_inputs, image_inputs, cotangent, stats, wq, wr, wd, gains
    )
    oq, orr, od, small, nsq = (scatter if direct else scatter_any)(gq, gr, gd, terms, bnsum)
    place = jnp.stack([lax.axis_index(AXES), jnp.int32(total_rows)])
    gimg, norm, *rest = update(
        place, gz, image_inputs, stats, gains, small, nsq, (oq, orr, od), masters, firsts, seconds, tables
    )
    return (mixed, gtags, gimg, norm.reshape(()), *rest)


def solution(mesh):
    rows = P(AXES, None)
    state = (rows, rows, rows, rows, P(None, AXES))
    direct = dict(mesh.shape) == {"wide": 16, "narrow": 2}
    return jax.shard_map(
        functools.partial(shards, direct),
        mesh=mesh,
        in_specs=(rows, rows, P(AXES), rows) + state * 3,
        out_specs=(rows, rows, rows, P()) + state * 5,
        check_vma=False,
    )
```

time: 1100 us -> 220 us (0.20)
  waiting for transfers between devices: 288 us -> 0 us
  matrix products: 274 us -> 0 us
  blocking collectives: 239 us -> 0 us
  Pallas kernels: 0 us -> 200 us
  other arithmetic: 127 us -> 0.08 us
  local copies, waits for them, and re-layouts: 142 us -> 18.1 us
  between operations: 20.5 us -> 1.16 us
    reduce_scatter x4 -> x0, waiting for transfers between devices: 287 us -> none  [the longest x1 133 us: shards(): lax.psum_scatter(grad_down, ('wide', 'narrow'), scatter_dimension=0, tile...]
    dot_general x36 -> x0, matrix products: 274 us -> none  [the longest x6 60.3 us: table_scores(): jnp.einsum('qhd,khd->hqk', queries, key_rows, preferred_element_type=jnp....]
    pallas_call x0 -> x4, Pallas kernels: none -> 200 us  [the longest x1 121 us: tables_call(): pl.pallas_call(k2_body, out_shape=[jax.ShapeDtypeStruct(s, d) for s, d, _...]
    psum x4 -> x0, blocking collectives: 157 us -> none  [the longest x1 42.1 us: shards(): lax.psum(jnp.sum(image_values, 0), ('wide', 'narrow')) / total_rows]
    all_gather x2 -> x0, blocking collectives: 82.6 us -> none  [the longest x1 41.3 us: shards(): lax.all_gather(copies[4], ('wide', 'narrow'), axis=1, tiled=True)]
    convert_element_type x12 -> x0, other arithmetic: 69.2 us -> none  [the longest x3 56.9 us: table_backward(): grad_scores = (soft_weights * (grad_soft - delta_rows)).astype(jnp.bfloat16)]
    slice x16 -> x0, local copies, waits for them, and re-layouts: 38.6 us -> none  [the longest x2 8.18 us: shards(): grad_values[:, :img_len].reshape(image_rows, model_width)]
    while x30 -> x0, local copies, waits for them, and re-layouts: 33.6 us -> none  [the longest x4 16.1 us: shards(): lax.map(lambda table_item: table_forward(table_item[0], table_item[1], ta...]
  transfers between devices with their start and end apart: 8 -> 0, of which waited for: 3 -> 0; matrix products, arithmetic and copies ran while one was open for 44% -> 0% of each run, Pallas kernels for 0% -> 0%
where the time goes in v1:
time: 220 us; the launch traced here: 219 us
  Pallas kernels  200 us (91%)
  local copies, waits for them, and re-layouts  18.1 us (8%)
    pallas_call x1, Pallas kernels, tables_call(): pl.pallas_call(k2_body, out_shape=[jax.ShapeDtypeStruct(s, d) for s, d, _...  121 us
    pallas_call x1, Pallas kernels, scatter(): pl.pallas_call(scatter_kernel, out_shape=[jax.ShapeDtypeStruct((R, 3 * D)...  39.3 us
    pallas_call x1, Pallas kernels, gather(): pl.pallas_call(gather_kernel, out_shape=[jax.ShapeDtypeStruct(dims + (R,...  35.1 us
    unnamed x70, local copies, waits for them, and re-layouts  18.1 us
    pallas_call x1, Pallas kernels, update(): pl.pallas_call(update_kernel, out_shape=[jax.ShapeDtypeStruct((rows, D),...  4.48 us

profile of v1, /device:TPU:0, one launch (start us, length us, event | category | flops | bytes accessed | tf_op | source)
XLA Modules:
  0.0 219.3 jit_solution(9165689194326440880)
XLA Ops:
  0.7 0.0 copy-start
  0.7 1.7 copy-done
  2.4 0.0 copy-start.9
  2.4 0.9 copy-done.9
  3.2 0.0 copy-start.11
  3.2 0.8 copy-done.11
  4.1 0.0 copy-start.13
  4.1 0.8 copy-done.13
  4.9 0.0 copy-start.15
  4.9 0.8 copy-done.15
  5.7 0.0 copy-start.27
  5.7 0.7 copy-done.27
  6.4 35.1 %gather.1 = (bf16[4,2,2,2,16,1536]{5,4,3,2,1,0:T(8,128)(2,1)S(1)}, bf16[4,2,2,2,16,1536]{5,4,3,2,1,0:T(8,128)(2,1)S(1)}, bf16[4,2,2,2,32,512]{5,4,3,2,1,0:T(8,12...) custom-call(bf16[2352,512]{1,0:T(8,128)(2,1)S(1)} %copy-done, f32[16,1536]{1,0:T(8,128)S(1)} %copy-done.9, ...), custom_call_target="tpu_custom_call" | custom-call | tf_op jit(solution)/shard_map/gather/pallas_call | solution.py:240
  41.5 0.0 copy-start.3
  41.5 1.2 copy-done.3
  42.7 0.0 copy-start.4
  42.7 1.1 copy-done.4
  43.8 1.0 copy-done.8
  44.8 0.6 copy-done.23
  45.4 0.6 copy-done.29
  46.0 121.1 %tables.1 = (bf16[1536,512]{1,0:T(8,128)(2,1)}, f32[1536,512]{1,0:T(8,128)}, f32[2352,512]{1,0:T(8,128)}, bf16[512,1536]{1,0:T(8,128)(2,1)}, bf16[512,1536]{1,0:...) custom-call(s32[3]{0:T(128)} %counts.1, bf16[1536,512]{1,0:T(8,128)(2,1)} %tag_ref.1, ...), custom_call_target="tpu_custom_call" | custom-call | tf_op jit(solution)/shard_map/tables/pallas_call | solution.py:682
  167.1 0.0 copy-start.5
  167.1 1.4 copy-done.5
  168.5 1.4 copy-done.6
  169.9 1.2 copy-done.7
  171.2 0.7 copy-done.31
  171.9 0.7 copy-done.34
  172.5 0.0 copy-start.16
  172.6 0.0 copy-start.17
  172.6 0.0 copy-start.18
  172.6 0.0 copy-start.19
  172.6 0.0 copy-start.20
  172.6 0.0 copy-start.21
  172.6 0.0 copy-start.22
  172.6 0.0 copy-start.24
  172.6 0.0 copy-start.25
  172.7 0.0 copy-start.26
  172.7 0.0 copy-start.28
  172.7 0.0 copy-start.30
  172.7 0.0 copy-start.32
  172.7 0.0 copy-start.33
  172.7 39.3 %scatter.1 = (f32[16,1536]{1,0:T(8,128)S(1)}, f32[16,1536]{1,0:T(8,128)S(1)}, f32[32,512]{1,0:T(8,128)S(1)}, f32[8,512]{1,0:T(8,128)S(1)}, f32[8,128]{1,0:T(8,128)S(1)}) custom-call(bf16[4,2,2,2,16,1536]{5,4,3,2,1,0:T(8,128)(2,1)S(1)} %bitcast.10, bf16[4,2,2,2,16,1536]{5,4,3,2,1,0:T(8,128)(2,1)S(1)} %bitcast.11, ...), custom_call_target="tpu_custom_call" | custom-call | tf_op jit(solution)/shard_map/scatter/pallas_call | solution.py:410
  212.0 0.1 pad_add_fusion.place
  212.1 0.0 copy-done.1
  212.1 0.0 copy-done.10
  212.1 0.0 copy-done.12
  212.1 0.0 copy-done.14
  212.1 0.0 copy-done.16
  212.1 0.0 copy-done.17
  212.2 0.0 copy-done.18
  212.2 0.0 copy-done.19
  212.2 0.0 copy-done.20
  212.2 0.0 copy-done.21
  212.2 0.0 copy-done.22
  212.2 0.0 copy-done.24
  212.2 0.0 copy-done.25
  212.2 0.0 copy-done.26
  212.2 0.0 copy-done.28
  212.2 0.0 copy-done.30
  212.3 0.0 copy-done.32
  212.3 0.0 copy-done.33
  212.3 0.0 copy-start.2
  212.3 2.4 %copy-done.2 = f32[2352,512]{1,0:T(8,128)S(1)} copy-done((f32[2352,512]{1,0:T(8,128)S(1)}, f32[2352,512]{1,0:T(8,128)}, u32[]{:S(2)}) %copy-start.2) | copy-done | bytes 4816920
  214.6 4.5 %update.1 = (f32[2352,512]{1,0:T(8,128)}, f32[1,1]{1,0:T(1,128)}, f32[16,1536]{1,0:T(8,128)}, f32[16,512]{1,0:T(8,128)}, f32[16,1024]{1,0:T(8,128)}, /*index=5*/...) custom-call(s32[2]{0:T(128)S(1)} %pad_add_fusion.place, ...), custom_call_target="tpu_custom_call" | custom-call | tf_op jit(solution)/shard_map/update/pallas_call | solution.py:754
  (11 shorter events, 0.0 us)
Async XLA Ops:
  0.7 1.7 copy-start
  2.4 0.9 copy-start.9
  3.2 0.8 copy-start.11
  4.1 0.8 copy-start.13
  4.9 0.8 copy-start.15
  5.7 0.7 copy-start.27
  41.5 1.2 copy-start.3
  42.7 1.2 copy-start.4
  43.8 1.0 copy-start.8
  44.8 0.6 copy-start.23
  45.4 0.6 copy-start.29
  167.1 1.4 copy-start.5
  168.5 1.4 copy-start.6
  169.9 1.2 copy-start.7
  171.2 0.7 copy-start.31
  171.8 0.7 copy-start.34
  172.5 39.6 %copy-start.1 = (bf16[2352,512]{1,0:T(8,128)(2,1)S(1)}, bf16[2352,512]{1,0:T(8,128)(2,1)}, u32[]{:S(2)}) copy-start(bf16[2352,512]{1,0:T(8,128)(2,1)} %img_ref.5) | copy-start | bytes 7225348
  172.5 39.6 %copy-start.10 = (f32[16,1536]{1,0:T(8,128)S(1)}, f32[16,1536]{1,0:T(8,128)}, u32[]{:S(2)}) copy-start(f32[16,1536]{1,0:T(8,128)} %w0.1) | copy-start | bytes 294916
  172.5 39.6 %copy-start.12 = (f32[16,1024]{1,0:T(8,128)S(1)}, f32[16,1024]{1,0:T(8,128)}, u32[]{:S(2)}) copy-start(f32[16,1024]{1,0:T(8,128)} %w2.1) | copy-start | bytes 196612
  172.5 39.6 %copy-start.14 = (f32[32,512]{1,0:T(8,128)S(1)}, f32[32,512]{1,0:T(8,128)}, u32[]{:S(2)}) copy-start(f32[32,512]{1,0:T(8,128)} %w3.1) | copy-start | bytes 196612
  172.5 39.6 %copy-start.16 = (f32[16,512]{1,0:T(8,128)S(1)}, f32[16,512]{1,0:T(8,128)}, u32[]{:S(2)}) copy-start(f32[16,512]{1,0:T(8,128)} %w1.1) | copy-start | bytes 98308
  172.6 39.6 %copy-start.17 = (f32[16,1536]{1,0:T(8,128)S(1)}, f32[16,1536]{1,0:T(8,128)}, u32[]{:S(2)}) copy-start(f32[16,1536]{1,0:T(8,128)} %f0.1) | copy-start | bytes 294916
  172.6 39.6 %copy-start.18 = (f32[16,1536]{1,0:T(8,128)S(1)}, f32[16,1536]{1,0:T(8,128)}, u32[]{:S(2)}) copy-start(f32[16,1536]{1,0:T(8,128)} %v0.1) | copy-start | bytes 294916
  172.6 39.6 %copy-start.19 = (f32[16,1024]{1,0:T(8,128)S(1)}, f32[16,1024]{1,0:T(8,128)}, u32[]{:S(2)}) copy-start(f32[16,1024]{1,0:T(8,128)} %f2.1) | copy-start | bytes 196612
  172.6 39.6 %copy-start.20 = (f32[32,512]{1,0:T(8,128)S(1)}, f32[32,512]{1,0:T(8,128)}, u32[]{:S(2)}) copy-start(f32[32,512]{1,0:T(8,128)} %f3.1) | copy-start | bytes 196612
  172.6 39.6 %copy-start.21 = (f32[16,1024]{1,0:T(8,128)S(1)}, f32[16,1024]{1,0:T(8,128)}, u32[]{:S(2)}) copy-start(f32[16,1024]{1,0:T(8,128)} %v2.1) | copy-start | bytes 196612
  172.6 39.6 %copy-start.22 = (f32[32,512]{1,0:T(8,128)S(1)}, f32[32,512]{1,0:T(8,128)}, u32[]{:S(2)}) copy-start(f32[32,512]{1,0:T(8,128)} %v3.1) | copy-start | bytes 196612
  172.6 39.6 %copy-start.24 = (f32[8,512]{1,0:T(8,128)S(1)}, f32[8,512]{1,0:T(8,128)}, u32[]{:S(2)}) copy-start(f32[8,512]{1,0:T(8,128)} %copy-done.23) | copy-start | bytes 49156
  172.6 39.6 %copy-start.25 = (f32[16,512]{1,0:T(8,128)S(1)}, f32[16,512]{1,0:T(8,128)}, u32[]{:S(2)}) copy-start(f32[16,512]{1,0:T(8,128)} %f1.1) | copy-start | bytes 98308
  172.7 39.6 %copy-start.26 = (f32[16,512]{1,0:T(8,128)S(1)}, f32[16,512]{1,0:T(8,128)}, u32[]{:S(2)}) copy-start(f32[16,512]{1,0:T(8,128)} %v1.1) | copy-start | bytes 98308
  172.7 39.6 %copy-start.28 = (f32[6,16]{1,0:T(8,128)S(1)}, f32[6,16]{1,0:T(8,128)}, u32[]{:S(2)}) copy-start(f32[6,16]{1,0:T(8,128)} %w4.1) | copy-start | bytes 1156
  172.7 39.6 %copy-start.30 = (f32[2,512]{1,0:T(2,128)S(1)}, f32[2,512]{1,0:T(2,128)}, u32[]{:S(2)}) copy-start(f32[2,512]{1,0:T(2,128)} %copy-done.29) | copy-start | bytes 12292
  172.7 39.6 %copy-start.32 = (f32[6,16]{1,0:T(8,128)S(1)}, f32[6,16]{1,0:T(8,128)}, u32[]{:S(2)}) copy-start(f32[6,16]{1,0:T(8,128)} %f4.1) | copy-start | bytes 1156
  172.7 39.6 %copy-start.33 = (f32[6,16]{1,0:T(8,128)S(1)}, f32[6,16]{1,0:T(8,128)}, u32[]{:S(2)}) copy-start(f32[6,16]{1,0:T(8,128)} %v4.1) | copy-start | bytes 1156
  212.3 2.4 %copy-start.2 = (f32[2352,512]{1,0:T(8,128)S(1)}, f32[2352,512]{1,0:T(8,128)}, u32[]{:S(2)}) copy-start(f32[2352,512]{1,0:T(8,128)} %get-tuple-element.81.gz_ref) | copy-start | bytes 14450692

commit v2 on v1

v2 whole, which is shorter than its diff:
```python
import functools
import math

import jax
import jax.numpy as jnp
from jax import lax
from jax.experimental import pallas as pl
from jax.experimental.pallas import tpu as pltpu
from jax.sharding import PartitionSpec as P

f32 = jnp.float32
bf = jnp.bfloat16
MESH = pl.DeviceIdType.MESH
HEADS = 8
STEP = 10
EPS = 1e-05
NEG = -1000000000.0
CLIP_AT = 1.0
BETA_FIRST = 0.9
BETA_SECOND = 0.999
ADAM_EPS = 1e-08
RATE_MATRIX = 0.05
RATE_OUTPUT = 1.0
RATE_NORMS = 0.5
DECAY_RATE = 0.1
GC = math.sqrt(2 / math.pi)
GA = 0.044715
AXES = ("wide", "narrow")
VM = pl.BlockSpec(memory_space=pltpu.VMEM)


def dg(a, b, ca, cb):
    return lax.dot_general(a, b, (((ca,), (cb,)), ((), ())), preferred_element_type=f32)


class Place:
    def __init__(self):
        self.w = lax.axis_index("wide")
        self.c = lax.axis_index("narrow")
        self.x = lax.rem(self.w, 2)
        self.y = lax.rem(self.w // 2, 2)
        self.z = self.w // 4
        self.d = self.w * 2 + self.c
        self.to_x = (self.w + 1 - 2 * self.x, self.c)
        self.to_y = (self.w + 2 - 4 * self.y, self.c)
        self.sib = (self.w, 1 - self.c)

    def to_z(self, k):
        return (lax.rem(self.w + 4 * k, 16), self.c)

    def peer(self, k):
        d = lax.rem(self.d + k, 32)
        return (d // 2, lax.rem(d, 2))


def greet_all(me):
    bar = pltpu.get_barrier_semaphore()
    for k in range(1, 32):
        pl.semaphore_signal(bar, inc=1, device_id=me.peer(k), device_id_type=MESH)
    pl.semaphore_wait(bar, 31)


def remote(src, dst, ss, rs, dev):
    return pltpu.make_async_remote_copy(
        src_ref=src, dst_ref=dst, send_sem=ss, recv_sem=rs, device_id=dev, device_id_type=MESH
    )


def mo(a, n):
    return pl.multiple_of(a, n)


class Gather:
    SLOTS = 35

    def __init__(self, me, g, ss, rs, split):
        self.me, self.g, self.ss, self.rs = me, g, ss, rs
        self.rows = g.shape[0] // 32
        n = g.shape[1]
        self.h = n // 2 if split else n
        self.split = split
        self.sent = []

    def ref(self, kz, pos, part=None, c=None):
        me = self.me
        z = lax.rem(me.z + 4 - kz, 4)
        y = me.y if pos in (0, 1) else 1 - me.y
        x = me.x if pos in (0, 2) else 1 - me.x
        d = z * 8 + y * 4 + x * 2 + (me.c if c is None else c)
        rows = pl.ds(mo(d * self.rows, self.rows), self.rows)
        if part is None:
            return self.g.at[rows]
        return self.g.at[rows, pl.ds(part * self.h, self.h)]

    def go(self, kz, pos, part, slot, dev):
        ref = self.ref(kz, pos, part)
        remote(ref, ref, self.ss.at[slot], self.rs.at[slot], dev).start()
        self.sent.append((kz, pos, part, slot))

    def got(self, slot, *key, **kw):
        ref = self.ref(*key, **kw)
        remote(ref, ref, self.ss.at[slot], self.rs.at[slot], self.me.sib).wait_recv()

    def start(self):
        me = self.me
        for k in (2, 1, 3):
            self.go(0, 0, None, k - 1, me.to_z(k))
        self.go(0, 0, None, 3, me.to_x)
        self.go(0, 0, None, 7, me.to_y)
        self.go(0, 0, None, 19, me.sib)

    def column(self):
        me = self.me
        for k in (1, 3, 2):
            self.got(k - 1, k, 0)
            self.go(k, 0, None, 3 + k, me.to_x)
            self.go(k, 0, None, 7 + k, me.to_y)
            self.go(k, 0, None, 19 + k, me.sib)

    def plane(self):
        me = self.me
        for k in (0, 1, 3, 2):
            self.got(3 + k, k, 1)
            self.go(k, 1, 0, 11 + k, me.to_y)
            self.go(k, 1, None, 23 + k, me.sib)
            self.got(7 + k, k, 2)
            if self.split:
                self.go(k, 2, 1, 15 + k, me.to_x)
            self.go(k, 2, None, 27 + k, me.sib)

    def corner(self):
        me = self.me
        for k in (0, 1, 3, 2):
            self.got(11 + k, k, 3, 0)
            if self.split:
                self.got(15 + k, k, 3, 1)
            self.go(k, 3, None, 31 + k, me.sib)

    def finish(self):
        for pos in range(4):
            for k in range(4):
                self.got(19 + 4 * pos + k, k, pos, c=1 - self.me.c)
        for kz, pos, part, slot in self.sent:
            ref = self.ref(kz, pos, part)
            remote(ref, ref, self.ss.at[slot], self.rs.at[slot], self.me.sib).wait_send()


def push_all(me, g, ss, rs):
    for k in range(1, 32):
        remote(g.at[me.d], g.at[me.d], ss.at[k], rs.at[k], me.peer(k)).start()


def push_done(me, g, ss, rs):
    for k in range(1, 32):
        remote(g.at[me.d], g.at[me.d], ss.at[k], rs.at[k], me.sib).wait_send()
        src = lax.rem(me.d + 32 - k, 32)
        remote(g.at[src], g.at[src], ss.at[k], rs.at[k], me.sib).wait_recv()


class Scatter:
    SLOTS = 8

    def __init__(self, me, g, out, bufs, ss, rs):
        self.me, self.g, self.out, self.ss, self.rs = me, g, out, ss, rs
        self.r0, self.r1a, self.r1b, self.r2a, self.r2b, self.s2, self.r3 = bufs
        self.s0, self.s1a, self.s1b = self.r0, self.r1a, self.r1b
        self.h = g.shape[-1] // 2

    @staticmethod
    def bufs(R, N):
        h = N // 2
        v = lambda *s: pltpu.VMEM(s, bf)
        return [
            v(4, 2, 2, R, N), v(4, 2, R, h), v(4, 2, R, h), v(4, R, h), v(4, R, h), v(4, R, N), v(3, R, N),
        ]

    def hop(self, slot):
        me, h = self.me, self.h
        if slot == 0:
            src, dst, dev = self.g.at[:, :, :, 1 - me.c], self.r0, me.sib
        elif slot == 1:
            src, dst, dev = self.s0.at[:, :, 1 - me.x, :, pl.ds(0, h)], self.r1a, me.to_x
        elif slot == 2:
            src, dst, dev = self.s0.at[:, 1 - me.y, :, :, pl.ds(h, h)], self.r1b, me.to_y
        elif slot == 3:
            src, dst, dev = self.s1a.at[:, 1 - me.y], self.r2a, me.to_y
        elif slot == 4:
            src, dst, dev = self.s1b.at[:, 1 - me.x], self.r2b, me.to_x
        else:
            k = slot - 4
            src, dst, dev = self.s2.at[lax.rem(me.z + k, 4)], self.r3.at[k - 1], me.to_z(k)
        return remote(src, dst, self.ss.at[slot], self.rs.at[slot], dev)

    def core(self):
        self.hop(0).start()

    def plane1(self):
        me = self.me
        self.hop(0).wait_recv()

        def add(i, _):
            k = (i // 4, lax.rem(i // 2, 2), lax.rem(i, 2))
            self.s0[k] = (self.g[k + (me.c,)].astype(f32) + self.r0[k].astype(f32)).astype(bf)
            return 0

        lax.fori_loop(0, 16, add, 0)
        self.hop(1).start()
        self.hop(2).start()

    def plane2(self):
        me, h = self.me, self.h
        self.hop(1).wait_recv()
        self.hop(2).wait_recv()

        def add(i, _):
            z, k = i // 2, lax.rem(i, 2)
            a = self.s0[z, k, me.x, :, pl.ds(0, h)].astype(f32) + self.r1a[z, k].astype(f32)
            self.s1a[z, k] = a.astype(bf)
            b = self.s0[z, me.y, k, :, pl.ds(h, h)].astype(f32) + self.r1b[z, k].astype(f32)
            self.s1b[z, k] = b.astype(bf)
            return 0

        lax.fori_loop(0, 8, add, 0)
        self.hop(3).start()
        self.hop(4).start()

    def column(self):
        me, h = self.me, self.h
        self.hop(3).wait_recv()
        self.hop(4).wait_recv()
        for z in range(4):
            self.s2[z, :, 0:h] = (self.s1a[z, me.y].astype(f32) + self.r2a[z].astype(f32)).astype(bf)
            self.s2[z, :, h:] = (self.s1b[z, me.x].astype(f32) + self.r2b[z].astype(f32)).astype(bf)
        for k in (2, 1, 3):
            self.hop(4 + k).start()

    def finish(self):
        acc = self.s2[self.me.z].astype(f32)
        for k in (1, 2, 3):
            self.hop(4 + k).wait_recv()
            acc += self.r3[k - 1].astype(f32)
        self.out[...] = acc
        for slot in range(8):
            self.hop(slot).wait_send()
        return jnp.sum(acc * acc)


class Sums:
    def __init__(self, me, tb, ss, rs):
        self.me, self.tb, self.ss, self.rs = me, tb, ss, rs

    def hop(self, slot):
        me = self.me
        src, dst, dev = ((0, 1, me.sib), (2, 3, me.to_x), (4, 5, me.to_y))[slot] if slot < 3 else (
            6 + me.z, 6 + me.z, me.to_z(slot - 2)
        )
        return remote(self.tb.at[src], self.tb.at[dst], self.ss.at[slot], self.rs.at[slot], dev)

    def step(self, i):
        tb = self.tb
        if i > 0:
            self.hop(i - 1).wait_recv()
            at = 2 * i if i < 3 else 6 + self.me.z
            tb[at] = tb[2 * i - 2] + tb[2 * i - 1]
        for slot in (i,) if i < 3 else (3, 4, 5):
            self.hop(slot).start()

    def finish(self):
        tb = self.tb
        for k in (1, 2, 3):
            at = tb.at[6 + lax.rem(self.me.z + 4 - k, 4)]
            remote(at, at, self.ss.at[2 + k], self.rs.at[2 + k], self.me.sib).wait_recv()
        for slot in range(6):
            self.hop(slot).wait_send()
        return (tb[6] + tb[7]) + (tb[8] + tb[9])


class Refs:
    pass


def tables_kernel(direct, names, *refs):
    r = Refs()
    for name, ref in zip(names, refs, strict=True):
        setattr(r, name, ref)
    t = pl.program_id(0)
    first = t == 0
    last = t == pl.num_programs(0) - 1
    T, D = r.tag.shape
    I = r.imglow.shape[0]
    NK = T + I
    hd = D // HEADS
    F = r.act.shape[1]
    count = r.counts[t]
    half = HEADS // 4
    HC = D // 2
    if direct:
        me = Place()
        gat = [
            Gather(me, r.wq, r.gs.at[0], r.gs.at[1], True),
            Gather(me, r.wn, r.gs.at[2], r.gs.at[3], False),
            Gather(me, r.wr, r.gs.at[4], r.gs.at[5], True),
            Gather(me, r.wd, r.gs.at[6], r.gs.at[7], True),
        ]
        sq0 = Scatter(me, r.gq0, r.oq0, r.bq0, r.cs.at[0], r.cs.at[1])
        sq1 = Scatter(me, r.gq1, r.oq1, r.bq1, r.cs.at[2], r.cs.at[3])
        sr = Scatter(me, r.gr, r.orr, r.br, r.cs.at[4], r.cs.at[5])
        sd = Scatter(me, r.gd, r.od, r.bd, r.cs.at[6], r.cs.at[7])
        sm = Sums(me, r.tb, r.cs.at[8], r.cs.at[9])
    wout_ref = r.wr.at[:, 0:D]
    wup_ref = r.wr.at[:, D : D + F]

    @pl.when(first)
    def _():
        r.aqkv[...] = jnp.zeros_like(r.aqkv)
        r.aout[...] = jnp.zeros_like(r.aout)
        r.aup[...] = jnp.zeros_like(r.aup)
        r.adn[...] = jnp.zeros_like(r.adn)
        r.terms[...] = jnp.zeros_like(r.terms)

    if direct:

        @pl.when(first)
        def _():
            img_in = pltpu.make_async_copy(r.img_hbm, r.img, r.isem)
            img_in.start()
            R, RD = r.pqkv.shape[0], r.pdn.shape[0]
            own = pl.ds(mo(me.d * R, R), R)
            r.wq[own, :] = r.pqkv[...].astype(bf)
            r.wr[own, pl.ds(0, D)] = r.pout[...].astype(bf)
            r.wr[own, pl.ds(D, F)] = r.pup[...].astype(bf)
            r.wd[pl.ds(mo(me.d * RD, RD), RD), :] = r.pdn[...].astype(bf)
            lane = lax.broadcasted_iota(jnp.int32, (16, 128), 1)
            unit = lax.broadcasted_iota(jnp.int32, (16, 128), 0)
            at = (lane == unit + 16 * lax.rem(me.d, 8)).astype(bf)
            tile = dg(r.pnorm[...].astype(bf), at, 1, 0)
            r.wn[pl.ds(mo(me.d * 16, 16), 16), :] = jnp.concatenate([tile, jnp.zeros((10, 128), f32)], 0).astype(bf)
            greet_all(me)
            gat[0].start()
            gat[1].start()
            img_in.wait()
            rows = r.img.shape[0]
            step = rows // 3
            total = jnp.zeros((1, D), f32)
            for i in range(3):
                total += jnp.sum(r.img[i * step : (i + 1) * step, :].astype(f32), 0, keepdims=True)
            mean_d = total / rows
            m2 = jnp.zeros((1, D), f32)
            for i in range(3):
                cen = r.img[i * step : (i + 1) * step, :].astype(f32) - mean_d
                m2 += jnp.sum(cen * cen, 0, keepdims=True)
            for g in range(4):
                r.st[me.d, g : g + 1, :] = mean_d[:, g * 128 : (g + 1) * 128]
                r.st[me.d, g + 4 : g + 5, :] = m2[:, g * 128 : (g + 1) * 128]
            push_all(me, r.st, r.ps.at[0], r.ps.at[1])
            gat[0].column()
            gat[1].column()
            gat[2].start()
            gat[3].start()
            gat[0].plane()
            gat[1].plane()
            gat[0].corner()
            gat[1].corner()
            push_done(me, r.st, r.ps.at[0], r.ps.at[1])
            mean = jnp.sum(r.st[:, 0:4, :], 0) / 32
            off = r.st[:, 0:4, :] - mean[None]
            spread = (jnp.sum(r.st[:, 4:8, :], 0) + rows * jnp.sum(off * off, 0)) / (rows * 32)
            inv = lax.rsqrt(spread + EPS)
            for g in range(4):
                r.stats[0:1, g * 128 : (g + 1) * 128] = mean[g : g + 1, :]
                r.stats[1:2, g * 128 : (g + 1) * 128] = inv[g : g + 1, :]
            gat[1].finish()
            for z in range(4):
                acc = jnp.zeros((8, 128), f32)
                for k in range(8):
                    acc += r.wn[(z * 8 + k) * 16 : (z * 8 + k) * 16 + 16, :].astype(f32)[0:8]
                r.gains[:, z * 128 : (z + 1) * 128] = acc
            gat[0].finish()

    img_ref = r.img.at[pl.ds(mo(t * I, 16), I)] if direct else r.img
    mean = r.stats[0:1, :]
    inv = r.stats[1:2, :]
    g1, b1, g2 = r.gains[0:1, :], r.gains[1:2, :], r.gains[2:3, :]
    b2, gb, bb = r.gains[3:4, :], r.gains[4:5, :], r.gains[5:6, :]
    img_parts = ((0, 256), (256, 256), (512, I - 512))

    for r0, rl in img_parts:
        img_hat = (img_ref[r0 : r0 + rl, :].astype(f32) - mean) * inv
        r.imglow[r0 : r0 + rl, :] = (img_hat * gb + bb).astype(bf)
    for r0 in range(0, T, 256):
        q = dg(r.tag[r0 : r0 + 256, :], r.wq[:, 0:D], 1, 0).astype(bf) * bf(1.0 / math.sqrt(hd))
        r.q[r0 : r0 + 256, :] = q
        r.qT[:, r0 : r0 + 256] = q.T
    for j, (dst, dstT) in enumerate(((r.kall, r.kT), (r.vall, r.vT))):
        w = r.wq[:, (j + 1) * D : (j + 2) * D]
        for r0 in range(0, T, 256):
            a = dg(r.tag[r0 : r0 + 256, :], w, 1, 0).astype(bf)
            dst[r0 : r0 + 256, :] = a
            dstT[:, r0 : r0 + 256] = a.T
        for r0, rl in img_parts:
            a = dg(r.imglow[r0 : r0 + rl, :], w, 1, 0).astype(bf)
            dst[T + r0 : T + r0 + rl, :] = a
            dstT[:, T + r0 : T + r0 + rl] = a.T
    ji = lax.broadcasted_iota(jnp.int32, (T, T), 0)
    ii = lax.broadcasted_iota(jnp.int32, (T, T), 1)
    r.bias[...] = jnp.where((ji <= ii) & (ji < count), 3e38, NEG)

    chunks = [(0, 256, 0), (256, 256, 256), (512, 256, 0), (768, 256, 0), (1024, NK - 1024, 0)]
    nc = len(chunks)
    row64 = lax.broadcasted_iota(jnp.int32, (2 * hd, 1), 0)
    lane64 = lax.broadcasted_iota(jnp.int32, (1, 2 * hd), 1)

    def own_rows(a, b):
        return jnp.where((row64 < hd) if b == 0 else (row64 >= hd), a, jnp.zeros_like(a))

    def own_lanes(a, b):
        return jnp.where((lane64 < hd) if b == 0 else (lane64 >= hd), a, jnp.zeros_like(a))

    def fullq(a, q0, fill):
        if q0 == 0:
            return a
        return jnp.concatenate([jnp.full((a.shape[0], q0), fill, a.dtype), a], 1)

    def e_at(h, c):
        k0, kl, q0 = chunks[c]
        if q0:
            return r.e1.at[h]
        return r.e.at[h, 0:kl] if k0 == 0 else r.e.at[h, k0 - 256 : k0 - 256 + kl]

    def fwd_pair(p, _):
        ps = pl.ds(mo(p * 2 * hd, 2 * hd), 2 * hd)
        qzs = [own_rows(r.qT[ps, :], b) for b in range(2)]

        def A(b, c):
            k0, kl, q0 = chunks[c]
            s = dg(r.kall[k0 : k0 + kl, ps], qzs[b][:, q0:], 1, 0)
            if k0 < T:
                s = jnp.minimum(s, r.bias[k0 : k0 + kl, q0:])
            r.s[k0 : k0 + kl, q0:] = s
            return fullq(jnp.max(s, 0, keepdims=True), q0, NEG)

        def B(b, c, m):
            k0, kl, q0 = chunks[c]
            e = jnp.exp(r.s[k0 : k0 + kl, q0:] - m[:, q0:])
            l = jnp.sum(e, 0, keepdims=True)
            e = e.astype(bf)
            e_at(2 * p + b, c)[...] = e
            o = dg(r.vT[pl.ds(mo(p * 2 * hd + b * hd, hd), hd), k0 : k0 + kl], e, 1, 0)
            return fullq(o, q0, 0.0), fullq(l, q0, 0.0)

        def done(b, o, l):
            rl = 1.0 / l
            o = o * rl
            hs = pl.ds(mo(p * 2 * hd + b * hd, hd), hd)
            r.oT[hs, :] = o
            r.attT[hs, :] = o.astype(bf)
            r.rl[2 * p + b] = rl

        m0 = None
        for c in range(nc):
            mc = A(0, c)
            m0 = mc if m0 is None else jnp.maximum(m0, mc)
        m1 = None
        o = None
        for c in range(nc):
            oc, lc = B(0, c, m0)
            o, l = (oc, lc) if o is None else (o + oc, l + lc)
            mc = A(1, c)
            m1 = mc if m1 is None else jnp.maximum(m1, mc)
        done(0, o, l)
        o = None
        for c in range(nc):
            oc, lc = B(1, c, m1)
            o, l = (oc, lc) if o is None else (o + oc, l + lc)
        done(1, o, l)
        if direct:

            @pl.when(first & (p == 0))
            def _():
                gat[2].column()
                gat[3].column()

            @pl.when(first & (p == 1))
            def _():
                gat[2].plane()
                gat[3].plane()

            @pl.when(first & (p == 2))
            def _():
                gat[2].corner()
                gat[3].corner()

            @pl.when(first & (p == 3))
            def _():
                gat[2].finish()
                gat[3].finish()

        return 0

    lax.fori_loop(0, HEADS // 2, fwd_pair, 0)

    RC = 128
    zero = jnp.zeros((1, D), f32)

    def rows_part(i, tg):
        tg1, tb1, tg2, tb2 = tg
        r0 = mo(i * RC, RC)
        rs = pl.ds(r0, RC)
        hp = r.tag[rs, :].astype(f32) + dg(r.attT[:, rs], wout_ref[...], 0, 0)
        c = hp - jnp.mean(hp, -1, keepdims=True)
        inv1 = lax.rsqrt(jnp.mean(c * c, -1, keepdims=True) + EPS)
        hat1 = c * inv1
        hidden = hat1 * g1 + b1
        hl = hidden.astype(bf)
        r.hidlow[rs, :] = hl
        pre = dg(hl, wup_ref[...], 1, 0)
        p2 = pre * pre
        th = jnp.tanh(GC * (pre + GA * (p2 * pre)))
        act = (0.5 * pre * (1.0 + th)).astype(bf)
        r.act[rs, :] = act
        gp = 0.5 * (1.0 + th) + 0.5 * pre * (1.0 - th * th) * (GC * (1.0 + 3 * GA * p2))
        resid = hidden + dg(act, r.wd[...], 1, 0)
        c = resid - jnp.mean(resid, -1, keepdims=True)
        inv2 = lax.rsqrt(jnp.mean(c * c, -1, keepdims=True) + EPS)
        hat2 = c * inv2
        r.mixed[rs, :] = (hat2 * g2 + b2).astype(bf)
        rows = r0 + lax.broadcasted_iota(jnp.int32, (RC, 1), 0)
        go = jnp.where(rows < count, r.cot[rs, :].astype(f32), 0.0)
        tg2 += jnp.sum(go * hat2, 0, keepdims=True)
        tb2 += jnp.sum(go, 0, keepdims=True)
        s = go * g2
        gr = inv2 * (s - jnp.mean(s, -1, keepdims=True) - hat2 * jnp.mean(s * hat2, -1, keepdims=True))
        rlow = gr.astype(bf)
        r.rlow[rs, :] = rlow
        plow = (dg(rlow, r.wd[...], 1, 1) * gp).astype(bf)
        r.plow[rs, :] = plow
        gh = gr + dg(plow, wup_ref[...], 1, 1)
        tg1 += jnp.sum(gh * hat1, 0, keepdims=True)
        tb1 += jnp.sum(gh, 0, keepdims=True)
        s = gh * g1
        ghp = inv1 * (s - jnp.mean(s, -1, keepdims=True) - hat1 * jnp.mean(s * hat1, -1, keepdims=True))
        r.gtags[rs, :] = ghp
        hpl = ghp.astype(bf)
        r.hplow[rs, :] = hpl
        r.dOT[:, rs] = dg(hpl, wout_ref[...], 1, 1).astype(bf).T
        return tg1, tb1, tg2, tb2

    tg1, tb1, tg2, tb2 = lax.fori_loop(0, T // RC, rows_part, (zero,) * 4)
    r.terms[0:1, :] += tg1
    r.terms[1:2, :] += tb1
    r.terms[2:3, :] += tg2
    r.terms[3:4, :] += tb2
    for h in range(HEADS):
        hs = slice(h * hd, (h + 1) * hd)
        d = r.dOT[hs, :].astype(f32) * r.rl[h]
        r.dOT[hs, :] = d.astype(bf)
        r.delta[h] = jnp.sum(d * r.oT[hs, :], 0, keepdims=True)
    r.dO[...] = r.dOT[...].T

    def put(dst, acc, r0, rn, c0, cn, add, col=None):
        new = acc[r0 : r0 + rn, c0 : c0 + cn] + add
        acc[r0 : r0 + rn, c0 : c0 + cn] = new
        col = c0 if col is None else col
        low = new.astype(bf)
        if direct:
            R = dst.shape[4]
            nz = rn // (8 * R)
            z0 = r0 // (8 * R)
            dst[z0 : z0 + nz, :, :, :, :, col : col + cn] = low.reshape(nz, 2, 2, 2, R, cn)
        else:
            dst[r0 : r0 + rn, col : col + cn] = low

    for r0 in range(0, D, 256):
        put(r.gr, r.aout, r0, 256, 0, D, dg(r.attT[r0 : r0 + 256, :], r.hplow[...], 1, 0))
        for c0 in range(0, F, 512):
            put(r.gr, r.aup, r0, 256, c0, 512, dg(r.hidlow[:, r0 : r0 + 256], r.plow[:, c0 : c0 + 512], 0, 0), D + c0)
    for r0 in range(0, F, 256):
        put(r.gd, r.adn, r0, 256, 0, D, dg(r.act[:, r0 : r0 + 256], r.rlow[...], 0, 0))
    if direct:

        @pl.when(last)
        def _():
            sd.core()
            sr.core()

    def bwd_pair(p, _):
        p128 = mo(p * 2 * hd, 2 * hd)
        ps = pl.ds(p128, 2 * hd)
        dq = [None, None]
        ops = [(own_rows(r.dOT[ps, :], b), own_lanes(r.dO[:, ps], b), own_lanes(r.q[:, ps], b)) for b in range(2)]
        kc = pl.ds(mo(D + p128, 128), 2 * hd)
        vc = pl.ds(mo(2 * D + p128, 128), 2 * hd)
        for c in range(nc):
            k0, kl, q0 = chunks[c]
            ks = slice(k0, k0 + kl)
            dk = None
            for b in range(2):
                h = 2 * p + b
                hs = pl.ds(mo(p * 2 * hd + b * hd, hd), hd)
                dOz, dOl, ql = ops[b]
                dp = dg(r.vall[ks, ps], dOz[:, q0:], 1, 0)
                e = e_at(h, c)[...]
                ds = (e.astype(f32) * (dp - r.delta[h][:, q0:])).astype(bf)
                dvc = dg(e, dOl[q0:, :], 1, 0)
                dkc = dg(ds, ql[q0:, :], 1, 0)
                dqc = fullq(dg(r.kT[hs, ks], ds, 1, 0), q0, 0.0)
                dk, dv = (dkc, dvc) if dk is None else (dk + dkc, dv + dvc)
                dq[b] = dqc if dq[b] is None else dq[b] + dqc
            if k0 < T:
                r.dqkv[ks, kc] = dk.astype(bf)
                r.dqkv[ks, vc] = dv.astype(bf)
            else:
                si = slice(k0 - T, k0 - T + kl)
                r.dkvi[si, ps] = dk.astype(bf)
                r.dkvi[si, kc] = dv.astype(bf)
        for b in range(2):
            hs = pl.ds(mo(p * 2 * hd + b * hd, hd), hd)
            r.dqT[hs, :] = (dq[b] * (1.0 / math.sqrt(hd))).astype(bf)
        if direct:

            @pl.when(last & (p == 0))
            def _():
                sd.plane1()
                sr.plane1()

            @pl.when(last & (p == 1))
            def _():
                sd.plane2()

            @pl.when(last & (p == 2))
            def _():
                sd.column()
                sq0.plane1()

            @pl.when(last & (p == 3))
            def _():
                sr.column()
                sq0.plane2()

        return 0

    for i, gq in enumerate((r.gq0, r.gq1)):
        lax.fori_loop(i * half, (i + 1) * half, bwd_pair, 0)
        hc = slice(i * HC, (i + 1) * HC)
        r.dqkv[:, hc] = r.dqT[hc, :].T
        if i == 1:
            sg = jnp.zeros((1, D), f32)
            sb = sg
            for r0, rl in img_parts:
                rs = slice(r0, r0 + rl)
                gz = dg(r.dkvi[rs, :], r.wq[:, D:], 1, 1)
                r.gz[rs, :] = gz.astype(bf)
                hat = (img_ref[rs, :].astype(f32) - mean) * inv
                sg += jnp.sum(gz * hat, 0, keepdims=True)
                sb += jnp.sum(gz, 0, keepdims=True)
            r.terms[4:5, :] += sg
            r.terms[5:6, :] += sb
            if direct:

                @pl.when(last)
                def _():
                    r.tb[0] = r.terms[...]
                    sm.step(0)

        for r0 in range(0, D, 256):
            rs = slice(r0, r0 + 256)
            x = r.tag[:, rs]
            put(gq, r.aqkv, r0, 256, i * HC, HC, dg(x, r.dqkv[:, hc], 0, 0), 0)
            for j in (1, 2):
                cs = slice(j * D + i * HC, j * D + (i + 1) * HC)
                ci = slice(cs.start - D, cs.stop - D)
                add = dg(x, r.dqkv[:, cs], 0, 0) + dg(r.imglow[:, rs], r.dkvi[:, ci], 0, 0)
                put(gq, r.aqkv, r0, 256, cs.start, HC, add, j * HC)
        if direct and i == 0:

            @pl.when(last)
            def _():
                sq0.core()
                sr.plane2()

    if direct:

        @pl.when(last)
        def _():
            sq1.core()

    for r0 in range(0, T, 256):
        r.gtags[r0 : r0 + 256, :] += dg(r.dqkv[r0 : r0 + 256, :], r.wq[...], 1, 1)

    if direct:

        @pl.when(last)
        def _():
            sm.step(1)
            sq1.plane1()
            sq0.column()
            sq = sd.finish()
            sm.step(2)
            sq1.plane2()
            sq += sr.finish()
            sm.step(3)
            sq1.column()
            sq += sq0.finish()
            tot = sm.finish()
            r.small[...] = tot
            sq += sq1.finish()
            r.st[me.d] = jnp.full((8, 128), sq, f32)
            push_all(me, r.st, r.ps.at[2], r.ps.at[3])
            push_done(me, r.st, r.ps.at[2], r.ps.at[3])
            r.nsq[...] = jnp.sum(r.st[...], 0) + jnp.sum(tot * tot)


def tables_call(direct, counts, tag, img, cot, params):
    n = counts.shape[0]
    T, I, D = tag.shape[0] // n, img.shape[0] // n, tag.shape[1]
    NK = T + I
    HC = D // 2
    V = lambda *s, d=bf: pltpu.VMEM(s, d)
    S = jax.ShapeDtypeStruct

    def row(a, b):
        return pl.BlockSpec((a, b), lambda t, *_: (t, 0))

    def whole(shape, **kw):
        return pl.BlockSpec(shape, lambda t, *_: (0,) * len(shape), **kw)

    one = dict(pipeline_mode=pl.Buffered(1))
    if direct:
        F = params[2].shape[1]
        R, RD = params[0].shape[0], params[3].shape[0]
        ins = [("tag", row(T, D)), ("img_hbm", pl.BlockSpec(memory_space=pl.ANY)), ("cot", row(T, D))]
        ins += [(k, whole(a.shape, **one)) for k, a in zip(("pqkv", "pout", "pup", "pdn", "pnorm"), params)]
    else:
        F = params[4].shape[0]
        ins = [("tag", row(T, D)), ("img", row(I, D)), ("cot", row(T, D))]
        ins += [(k, whole(a.shape, **one)) for k, a in zip(("stats", "gains", "wq", "wr", "wd"), params)]
    outs = [
        ("mixed", S((n * T, D), bf), row(T, D)),
        ("gtags", S((n * T, D), f32), row(T, D)),
        ("gz", S((n * I, D), bf), row(I, D)),
    ]
    scratch = [
        ("imglow", V(I, D)), ("kall", V(NK, D)), ("vall", V(NK, D)), ("kT", V(D, NK)), ("vT", V(D, NK)),
        ("q", V(T, D)), ("qT", V(D, T)), ("bias", V(T, T, d=f32)), ("s", V(NK, T, d=f32)),
        ("e", V(HEADS, NK - 256, T)), ("e1", V(HEADS, 256, T - 256)), ("attT", V(D, T)), ("oT", V(D, T, d=f32)),
        ("rl", V(HEADS, 1, T, d=f32)), ("hidlow", V(T, D)), ("act", V(T, F)), ("rlow", V(T, D)), ("plow", V(T, F)),
        ("hplow", V(T, D)), ("dqkv", V(T, 3 * D)), ("dkvi", V(I, 2 * D)), ("dqT", V(D, T)), ("dO", V(T, D)),
        ("dOT", V(D, T)), ("delta", V(HEADS, 1, T, d=f32)), ("aqkv", V(D, 3 * D, d=f32)), ("aout", V(D, D, d=f32)),
        ("aup", V(D, F, d=f32)), ("adn", V(F, D, d=f32)),
    ]
    if direct:
        outs += [
            ("oq0", S((R, 3 * HC), f32), None), ("oq1", S((R, 3 * HC), f32), None), ("orr", S((R, D + F), f32), None),
            ("od", S((RD, D), f32), None), ("small", S((8, D), f32), None), ("nsq", S((8, 128), f32), None),
            ("stats", S((2, D), f32), None), ("gains", S((8, D), f32), None),
        ]
        dims = (4, 2, 2, 2)
        dma = pltpu.SemaphoreType.DMA
        scratch += [
            ("img", V(n * I, D)), ("wq", V(D, 3 * D)), ("wr", V(D, D + F)), ("wd", V(F, D)), ("wn", V(32 * 16, 128)),
            ("st", V(32, 8, 128, d=f32)), ("terms", V(8, D, d=f32)), ("tb", V(10, 8, D, d=f32)),
            ("gq0", V(*dims, R, 3 * HC)), ("gq1", V(*dims, R, 3 * HC)), ("gr", V(*dims, R, D + F)), ("gd", V(*dims, RD, D)),
            ("bq0", Scatter.bufs(R, 3 * HC)), ("bq1", Scatter.bufs(R, 3 * HC)), ("br", Scatter.bufs(R, D + F)),
            ("bd", Scatter.bufs(RD, D)),
            ("isem", dma), ("gs", dma((8, Gather.SLOTS))), ("cs", dma((10, Scatter.SLOTS))), ("ps", dma((4, 32))),
        ]
        extra = dict(collective_id=0, has_side_effects=True)
    else:
        outs += [
            ("gq0", S((D, 3 * HC), bf), None), ("gq1", S((D, 3 * HC), bf), None), ("gr", S((D, D + F), bf), None),
            ("gd", S((F, D), bf), None), ("terms", S((8, D), f32), None),
        ]
        extra = {}
    names = ("counts",) + tuple(k for k, _ in ins) + tuple(k for k, _, _ in outs) + tuple(k for k, _ in scratch)
    return pl.pallas_call(
        functools.partial(tables_kernel, direct, names),
        out_shape=[s for _, s, _ in outs],
        grid_spec=pltpu.PrefetchScalarGridSpec(
            num_scalar_prefetch=1,
            grid=(n,),
            in_specs=[b for _, b in ins],
            out_specs=[whole(s.shape) if b is None else b for _, s, b in outs],
            scratch_shapes=[a for _, a in scratch],
        ),
        compiler_params=pltpu.CompilerParams(vmem_limit_bytes=63 * 2**20, **extra),
        name="tables",
    )(counts, tag, img, cot, *params)


def update_kernel(
    place, gz_ref, img_ref, stats_ref, gains_ref, small_ref, nsq_ref, oq0, oq1, orr, od,
    w0, w1, w2, w3, w4, f0, f1, f2, f3, f4, v0, v1, v2, v3, v4,
    gimg_ref, norm_ref, *outs
):
    D = gz_ref.shape[1]
    total_rows = place[1].astype(f32)
    gb = gains_ref[4:5, :]
    k = stats_ref[1:2, :] * gb
    gsum = small_ref[4:5, :]
    bsum = small_ref[5:6, :]
    hat = (img_ref[...].astype(f32) - stats_ref[0:1, :]) * stats_ref[1:2, :]
    gimg_ref[...] = k * (gz_ref[...].astype(f32) - bsum / total_rows - hat * (gsum / total_rows))

    @pl.when(pl.program_id(0) == 0)
    def _():
        total_norm = jnp.sqrt(nsq_ref[0:1, 0:1])
        norm_ref[...] = total_norm
        factor = CLIP_AT / jnp.maximum(total_norm, CLIP_AT)
        cols = w4.shape[1]
        row = lax.broadcasted_iota(jnp.int32, (D, cols), 0)
        col = lax.broadcasted_iota(jnp.int32, (D, cols), 1)
        pick = (row == col + place[0] * cols).astype(f32)
        own = lax.dot_general(
            small_ref[...], pick, (((1,), (0,)), ((), ())), precision=lax.Precision.HIGHEST, preferred_element_type=f32
        )[0:6]
        hc = D // 2
        oq = [o[:, j * hc : (j + 1) * hc] for j in range(3) for o in (oq0, oq1)]
        grads = (jnp.concatenate(oq, 1), orr[:, 0:D], orr[:, D:], od[...], own)
        rates = (RATE_MATRIX, RATE_OUTPUT, RATE_MATRIX, RATE_MATRIX, RATE_NORMS)
        for i, (g, w, f, v) in enumerate(zip(grads, (w0, w1, w2, w3, w4), (f0, f1, f2, f3, f4), (v0, v1, v2, v3, v4))):
            clip = g * factor
            moment = BETA_FIRST * f[...] + (1.0 - BETA_FIRST) * clip
            square = BETA_SECOND * v[...] + (1.0 - BETA_SECOND) * clip * clip
            u = (moment / (1.0 - BETA_FIRST**STEP)) / (jnp.sqrt(square / (1.0 - BETA_SECOND**STEP)) + ADAM_EPS)
            if i < 4:
                new = w[...] - rates[i] * (u + DECAY_RATE * w[...])
            else:
                new = w[...] - rates[i] * u
            outs[i][...] = clip
            outs[5 + i][...] = moment
            outs[10 + i][...] = square
            outs[15 + i][...] = new
            outs[20 + i][...] = new.astype(bf)


def update(place, gz, img, stats, gains, small, nsq, owned, masters, firsts, seconds, steps):
    rows, D = gz.shape
    block = rows // steps

    def whole(a):
        return pl.BlockSpec(a.shape, lambda t, *_: (0, 0))

    tile = pl.BlockSpec((block, D), lambda t, *_: (t, 0))
    small_in = (stats, gains, small, nsq) + tuple(owned) + tuple(masters) + tuple(firsts) + tuple(seconds)
    shapes = [jax.ShapeDtypeStruct(m.shape, f32) for m in masters] * 4 + [jax.ShapeDtypeStruct(m.shape, bf) for m in masters]
    one = jax.ShapeDtypeStruct((1, 1), f32)
    return pl.pallas_call(
        update_kernel,
        out_shape=[jax.ShapeDtypeStruct((rows, D), f32), one] + shapes,
        grid_spec=pltpu.PrefetchScalarGridSpec(
            num_scalar_prefetch=1,
            grid=(steps,),
            in_specs=[tile, tile] + [whole(a) for a in small_in],
            out_specs=[tile, whole(one)] + [whole(a) for a in shapes],
        ),
        compiler_params=pltpu.CompilerParams(vmem_limit_bytes=40 * 2**20),
        name="update",
    )(place, gz, img, *small_in)


def gather_any(img, wqkv, wout, wup, wdn, norm):
    full = lambda a, axis: lax.all_gather(a.astype(bf), AXES, axis=axis, tiled=True)
    gr = jnp.concatenate([full(wout, 0), full(wup, 0)], 1)
    gains = jnp.concatenate([full(norm, 1).astype(f32), jnp.zeros((2, img.shape[1]), f32)], 0)
    values = img.astype(f32)
    total = img.shape[0] * lax.axis_size(AXES)
    mean = lax.psum(jnp.sum(values, 0), AXES) / total
    centred = values - mean
    spread = lax.psum(jnp.sum(centred * centred, 0), AXES) / total
    return full(wqkv, 0), gr, full(wdn, 0), jnp.stack([mean, lax.rsqrt(spread + EPS)]), gains


def scatter_any(gq0, gq1, gr, gd, terms):
    part = lambda a: lax.psum_scatter(a.astype(f32), AXES, scatter_dimension=0, tiled=True)
    owned = [part(a) for a in (gq0, gq1, gr, gd)]
    small = lax.psum(terms, AXES)
    local = sum(jnp.sum(a * a) for a in owned)
    nsq = lax.psum(local, AXES) + jnp.sum(small * small)
    return *owned, small, jnp.full((8, 128), nsq, f32)


def shards(direct, tag_inputs, image_inputs, tag_counts, cotangent, *params):
    masters, firsts, seconds = params[0:5], params[5:10], params[10:15]
    tables = tag_counts.shape[0]
    devices = lax.axis_size(AXES)
    total_rows = image_inputs.shape[0] * devices
    if direct:
        mixed, gtags, gz, *owned, small, nsq, stats, gains = tables_call(
            True, tag_counts, tag_inputs, image_inputs, cotangent, masters
        )
    else:
        wq, wr, wd, stats, gains = gather_any(image_inputs, *masters)
        mixed, gtags, gz, *sums = tables_call(
            False, tag_counts, tag_inputs, image_inputs, cotangent, (stats, gains, wq, wr, wd)
        )
        *owned, small, nsq = scatter_any(*sums)
    place = jnp.stack([lax.axis_index(AXES), jnp.int32(total_rows)])
    gimg, norm, *rest = update(
        place, gz, image_inputs, stats, gains, small, nsq, owned, masters, firsts, seconds, tables
    )
    return (mixed, gtags, gimg, norm.reshape(()), *rest)


def solution(mesh):
    rows = P(AXES, None)
    state = (rows, rows, rows, rows, P(None, AXES))
    direct = dict(mesh.shape) == {"wide": 16, "narrow": 2}
    return jax.shard_map(
        functools.partial(shards, direct),
        mesh=mesh,
        in_specs=(rows, rows, P(AXES), rows) + state * 3,
        out_specs=(rows, rows, rows, P()) + state * 5,
        check_vma=False,
    )
```

time: 220 us -> 203 us (0.923)
  Pallas kernels: 200 us -> 187 us
  local copies, waits for them, and re-layouts: 18.1 us -> 13.6 us
    pallas_call x3 -> x1, Pallas kernels: 196 us -> 183 us  [tables_call(): pl.pallas_call(functools.partial(tables_kernel, direct, names), out_shape...]
    unnamed x70 -> x56, local copies, waits for them, and re-layouts: 18.1 us -> 13.6 us
where the time goes in v2:
time: 203 us; the launch traced here: 202 us
  Pallas kernels  187 us (92%)
  local copies, waits for them, and re-layouts  13.6 us (7%)
    pallas_call x1, Pallas kernels, tables_call(): pl.pallas_call(functools.partial(tables_kernel, direct, names), out_shape...  183 us
    unnamed x56, local copies, waits for them, and re-layouts  13.6 us
    pallas_call x1, Pallas kernels, update(): pl.pallas_call(update_kernel, out_shape=[jax.ShapeDtypeStruct((rows, D),...  4.58 us

profile of v2, /device:TPU:0, one launch (start us, length us, event | category | flops | bytes accessed | tf_op | source)
XLA Modules:
  0.0 201.9 jit_solution(15249931965835600908)
XLA Ops:
  0.7 0.1 pad_add_fusion.place
  0.8 0.0 copy-start.2
  0.8 0.0 copy-start.3
  0.8 0.0 copy-start.4
  0.8 0.0 copy-start.5
  0.8 0.0 copy-start.6
  0.8 0.0 copy-start.7
  0.8 0.0 copy-start.9
  0.8 0.0 copy-start.10
  0.8 0.0 copy-start.11
  0.8 0.0 copy-start.12
  0.8 0.0 copy-start.16
  0.8 0.0 copy-start.17
  0.9 0.0 copy-start.20
  0.9 0.0 copy-start.21
  0.9 0.0 copy-start.22
  0.9 182.6 %tables.1 = (bf16[1536,512]{1,0:T(8,128)(2,1)}, f32[1536,512]{1,0:T(8,128)}, bf16[2352,512]{1,0:T(8,128)(2,1)}, f32[16,768]{1,0:T(8,128)}, f32[16,768]{1,0:T(8,1...) custom-call(s32[3]{0:T(128)} %refs_0_.1, ...), custom_call_target="tpu_custom_call" | custom-call | tf_op jit(solution)/shard_map/tables/pallas_call | solution.py:775
  183.5 0.0 copy-done.2
  183.6 0.0 copy-done.3
  183.6 0.0 copy-done.4
  183.6 0.0 copy-done.5
  183.6 0.0 copy-done.6
  183.6 0.0 copy-done.7
  183.6 0.0 copy-done.9
  183.6 0.0 copy-done.10
  183.6 0.0 copy-done.11
  183.6 0.0 copy-done.12
  183.6 0.0 copy-done.16
  183.7 0.0 copy-done.17
  183.7 0.0 copy-done.20
  183.7 0.0 copy-done.21
  183.7 0.0 copy-done.22
  183.7 0.0 copy-start
  183.7 1.7 copy-done
  185.4 0.0 copy-start.1
  185.4 1.7 copy-done.1
  187.1 0.0 copy-start.8
  187.1 0.9 copy-done.8
  187.9 0.0 copy-start.13
  187.9 0.8 copy-done.13
  188.8 0.0 copy-start.14
  188.8 0.8 copy-done.14
  189.6 0.0 copy-start.15
  189.6 0.8 copy-done.15
  190.4 0.0 copy-start.18
  190.4 0.7 copy-done.18
  191.1 0.0 copy-start.19
  191.1 0.7 copy-done.19
  191.8 0.0 copy-start.23
  191.8 0.7 copy-done.23
  192.5 0.0 copy-start.24
  192.5 0.7 copy-done.24
  193.2 0.0 copy-start.26
  193.2 4.6 %update.1 = (f32[2352,512]{1,0:T(8,128)}, f32[1,1]{1,0:T(1,128)}, f32[16,1536]{1,0:T(8,128)}, f32[16,512]{1,0:T(8,128)}, f32[16,1024]{1,0:T(8,128)}, /*index=5*/...) custom-call(s32[2]{0:T(128)S(1)} %pad_add_fusion.place, ...), custom_call_target="tpu_custom_call" | custom-call | tf_op jit(solution)/shard_map/update/pallas_call | solution.py:847
  197.8 0.0 copy-start.25
  197.8 0.0 copy-done.26
  197.8 1.1 copy.50
  198.9 1.3 copy-done.25
  200.2 1.7 copy.51
Async XLA Ops:
  0.8 182.8 %copy-start.2 = (f32[16,1536]{1,0:T(8,128)S(1)}, f32[16,1536]{1,0:T(8,128)}, u32[]{:S(2)}) copy-start(f32[16,1536]{1,0:T(8,128)} %w0.1) | copy-start | bytes 294916
  0.8 182.8 %copy-start.3 = (f32[16,1024]{1,0:T(8,128)S(1)}, f32[16,1024]{1,0:T(8,128)}, u32[]{:S(2)}) copy-start(f32[16,1024]{1,0:T(8,128)} %w2.1) | copy-start | bytes 196612
  0.8 182.8 %copy-start.4 = (f32[32,512]{1,0:T(8,128)S(1)}, f32[32,512]{1,0:T(8,128)}, u32[]{:S(2)}) copy-start(f32[32,512]{1,0:T(8,128)} %w3.1) | copy-start | bytes 196612
  0.8 182.8 %copy-start.5 = (f32[16,512]{1,0:T(8,128)S(1)}, f32[16,512]{1,0:T(8,128)}, u32[]{:S(2)}) copy-start(f32[16,512]{1,0:T(8,128)} %w1.1) | copy-start | bytes 98308
  0.8 182.8 %copy-start.6 = (f32[16,1536]{1,0:T(8,128)S(1)}, f32[16,1536]{1,0:T(8,128)}, u32[]{:S(2)}) copy-start(f32[16,1536]{1,0:T(8,128)} %f0.1) | copy-start | bytes 294916
  0.8 182.8 %copy-start.7 = (f32[16,1536]{1,0:T(8,128)S(1)}, f32[16,1536]{1,0:T(8,128)}, u32[]{:S(2)}) copy-start(f32[16,1536]{1,0:T(8,128)} %v0.1) | copy-start | bytes 294916
  0.8 182.8 %copy-start.9 = (f32[16,1024]{1,0:T(8,128)S(1)}, f32[16,1024]{1,0:T(8,128)}, u32[]{:S(2)}) copy-start(f32[16,1024]{1,0:T(8,128)} %f2.1) | copy-start | bytes 196612
  0.8 182.8 %copy-start.10 = (f32[32,512]{1,0:T(8,128)S(1)}, f32[32,512]{1,0:T(8,128)}, u32[]{:S(2)}) copy-start(f32[32,512]{1,0:T(8,128)} %f3.1) | copy-start | bytes 196612
  0.8 182.8 %copy-start.11 = (f32[16,1024]{1,0:T(8,128)S(1)}, f32[16,1024]{1,0:T(8,128)}, u32[]{:S(2)}) copy-start(f32[16,1024]{1,0:T(8,128)} %v2.1) | copy-start | bytes 196612
  0.8 182.8 %copy-start.12 = (f32[32,512]{1,0:T(8,128)S(1)}, f32[32,512]{1,0:T(8,128)}, u32[]{:S(2)}) copy-start(f32[32,512]{1,0:T(8,128)} %v3.1) | copy-start | bytes 196612
  0.8 182.8 %copy-start.16 = (f32[16,512]{1,0:T(8,128)S(1)}, f32[16,512]{1,0:T(8,128)}, u32[]{:S(2)}) copy-start(f32[16,512]{1,0:T(8,128)} %f1.1) | copy-start | bytes 98308
  0.8 182.8 %copy-start.17 = (f32[16,512]{1,0:T(8,128)S(1)}, f32[16,512]{1,0:T(8,128)}, u32[]{:S(2)}) copy-start(f32[16,512]{1,0:T(8,128)} %v1.1) | copy-start | bytes 98308
  0.9 182.8 %copy-start.20 = (f32[6,16]{1,0:T(8,128)S(1)}, f32[6,16]{1,0:T(8,128)}, u32[]{:S(2)}) copy-start(f32[6,16]{1,0:T(8,128)} %w4.1) | copy-start | bytes 1156
  0.9 182.8 %copy-start.21 = (f32[6,16]{1,0:T(8,128)S(1)}, f32[6,16]{1,0:T(8,128)}, u32[]{:S(2)}) copy-start(f32[6,16]{1,0:T(8,128)} %f4.1) | copy-start | bytes 1156
  0.9 182.8 %copy-start.22 = (f32[6,16]{1,0:T(8,128)S(1)}, f32[6,16]{1,0:T(8,128)}, u32[]{:S(2)}) copy-start(f32[6,16]{1,0:T(8,128)} %v4.1) | copy-start | bytes 1156
  183.7 1.7 copy-start
  185.4 1.7 copy-start.1
  187.1 0.9 copy-start.8
  187.9 0.8 copy-start.13
  188.8 0.8 copy-start.14
  189.6 0.8 copy-start.15
  190.4 0.7 copy-start.18
  191.1 0.7 copy-start.19
  191.8 0.7 copy-start.23
  192.5 0.7 copy-start.24
  193.2 4.6 %copy-start.26 = (bf16[1536,512]{1,0:T(8,128)(2,1)S(1)}, bf16[1536,512]{1,0:T(8,128)(2,1)}, u32[]{:S(2)}) copy-start(bf16[1536,512]{1,0:T(8,128)(2,1)} %get-tuple-element.134) | copy-start | bytes 4718596
  197.8 2.5 %copy-start.25 = (f32[1536,512]{1,0:T(8,128)S(1)}, f32[1536,512]{1,0:T(8,128)}, u32[]{:S(2)}) copy-start(f32[1536,512]{1,0:T(8,128)} %get-tuple-element.135) | copy-start | bytes 9437188

commit v3 on v2

v3 whole, which is shorter than its diff:
```python
import functools
import math

import jax
import jax.numpy as jnp
from jax import lax
from jax.experimental import pallas as pl
from jax.experimental.pallas import tpu as pltpu
from jax.sharding import PartitionSpec as P

f32 = jnp.float32
bf = jnp.bfloat16
MESH = pl.DeviceIdType.MESH
HEADS = 8
STEP = 10
EPS = 1e-05
NEG = -1000000000.0
CLIP_AT = 1.0
BETA_FIRST = 0.9
BETA_SECOND = 0.999
ADAM_EPS = 1e-08
RATE_MATRIX = 0.05
RATE_OUTPUT = 1.0
RATE_NORMS = 0.5
DECAY_RATE = 0.1
GC = math.sqrt(2 / math.pi)
GA = 0.044715
AXES = ("wide", "narrow")
VM = pl.BlockSpec(memory_space=pltpu.VMEM)


def dg(a, b, ca, cb):
    return lax.dot_general(a, b, (((ca,), (cb,)), ((), ())), preferred_element_type=f32)


class Place:
    def __init__(self):
        self.w = lax.axis_index("wide")
        self.c = lax.axis_index("narrow")
        self.x = lax.rem(self.w, 2)
        self.y = lax.rem(self.w // 2, 2)
        self.z = self.w // 4
        self.d = self.w * 2 + self.c
        self.to_x = (self.w + 1 - 2 * self.x, self.c)
        self.to_y = (self.w + 2 - 4 * self.y, self.c)
        self.sib = (self.w, 1 - self.c)

    def to_z(self, k):
        return (lax.rem(self.w + 4 * k, 16), self.c)

    def peer(self, k):
        d = lax.rem(self.d + k, 32)
        return (d // 2, lax.rem(d, 2))


def greet(me):
    bar = pltpu.get_barrier_semaphore()
    near = (me.sib, me.to_x, me.to_y, me.to_z(1), me.to_z(2), me.to_z(3))
    for dev in near:
        pl.semaphore_signal(bar, inc=1, device_id=dev, device_id_type=MESH)
    pl.semaphore_wait(bar, len(near))


def remote(src, dst, ss, rs, dev):
    return pltpu.make_async_remote_copy(
        src_ref=src, dst_ref=dst, send_sem=ss, recv_sem=rs, device_id=dev, device_id_type=MESH
    )


def mo(a, n):
    return pl.multiple_of(a, n)


class Gather:
    SLOTS = 35

    def __init__(self, me, g, ss, rs, split):
        self.me, self.g, self.ss, self.rs = me, g, ss, rs
        self.rows = g.shape[0] // 32
        n = g.shape[1]
        self.h = n // 2 if split else n
        self.split = split
        self.sent = []

    def ref(self, kz, pos, part=None, c=None):
        me = self.me
        z = lax.rem(me.z + 4 - kz, 4)
        y = me.y if pos in (0, 1) else 1 - me.y
        x = me.x if pos in (0, 2) else 1 - me.x
        d = z * 8 + y * 4 + x * 2 + (me.c if c is None else c)
        rows = pl.ds(mo(d * self.rows, self.rows), self.rows)
        if part is None:
            return self.g.at[rows]
        return self.g.at[rows, pl.ds(part * self.h, self.h)]

    def go(self, kz, pos, part, slot, dev):
        ref = self.ref(kz, pos, part)
        remote(ref, ref, self.ss.at[slot], self.rs.at[slot], dev).start()
        self.sent.append((kz, pos, part, slot))

    def got(self, slot, *key, **kw):
        ref = self.ref(*key, **kw)
        remote(ref, ref, self.ss.at[slot], self.rs.at[slot], self.me.sib).wait_recv()

    def start(self):
        me = self.me
        for k in (2, 1, 3):
            self.go(0, 0, None, k - 1, me.to_z(k))
        self.go(0, 0, None, 3, me.to_x)
        self.go(0, 0, None, 7, me.to_y)
        self.go(0, 0, None, 19, me.sib)

    def column(self):
        me = self.me
        for k in (1, 3, 2):
            self.got(k - 1, k, 0)
            self.go(k, 0, None, 3 + k, me.to_x)
            self.go(k, 0, None, 7 + k, me.to_y)
            self.go(k, 0, None, 19 + k, me.sib)

    def plane(self):
        me = self.me
        for k in (0, 1, 3, 2):
            self.got(3 + k, k, 1)
            self.go(k, 1, 0, 11 + k, me.to_y)
            self.go(k, 1, None, 23 + k, me.sib)
            self.got(7 + k, k, 2)
            if self.split:
                self.go(k, 2, 1, 15 + k, me.to_x)
            self.go(k, 2, None, 27 + k, me.sib)

    def corner(self):
        me = self.me
        for k in (0, 1, 3, 2):
            self.got(11 + k, k, 3, 0)
            if self.split:
                self.got(15 + k, k, 3, 1)
            self.go(k, 3, None, 31 + k, me.sib)

    def finish(self):
        for pos in range(4):
            for k in range(4):
                self.got(19 + 4 * pos + k, k, pos, c=1 - self.me.c)
        for kz, pos, part, slot in self.sent:
            ref = self.ref(kz, pos, part)
            remote(ref, ref, self.ss.at[slot], self.rs.at[slot], self.me.sib).wait_send()


def push_all(me, g, ss, rs):
    for k in range(1, 32):
        remote(g.at[me.d], g.at[me.d], ss.at[k], rs.at[k], me.peer(k)).start()


def push_done(me, g, ss, rs):
    for k in range(1, 32):
        remote(g.at[me.d], g.at[me.d], ss.at[k], rs.at[k], me.sib).wait_send()
        src = lax.rem(me.d + 32 - k, 32)
        remote(g.at[src], g.at[src], ss.at[k], rs.at[k], me.sib).wait_recv()


class Scatter:
    SLOTS = 8

    def __init__(self, me, g, out, bufs, sems):
        self.me, self.g, self.out, (self.ss, self.rs) = me, g, out, sems
        self.r0, self.r1a, self.r1b, self.r2a, self.r2b, self.s2, self.r3 = bufs
        self.s0, self.s1a, self.s1b = self.r0, self.r1a, self.r1b
        self.h = g.shape[-1] // 256 * 128

    @staticmethod
    def bufs(R, N):
        h = N // 256 * 128
        v = lambda *s: pltpu.VMEM(s, bf)
        return [
            v(4, 2, 2, R, N), v(4, 2, R, h), v(4, 2, R, N - h), v(4, R, h), v(4, R, N - h), v(4, R, N), v(3, R, N),
        ]

    def hop(self, slot):
        me, h = self.me, self.h
        n = self.g.shape[-1] - h
        if slot == 0:
            src, dst, dev = self.g.at[:, :, :, 1 - me.c], self.r0, me.sib
        elif slot == 1:
            src, dst, dev = self.s0.at[:, :, 1 - me.x, :, pl.ds(0, h)], self.r1a, me.to_x
        elif slot == 2:
            src, dst, dev = self.s0.at[:, 1 - me.y, :, :, pl.ds(h, n)], self.r1b, me.to_y
        elif slot == 3:
            src, dst, dev = self.s1a.at[:, 1 - me.y], self.r2a, me.to_y
        elif slot == 4:
            src, dst, dev = self.s1b.at[:, 1 - me.x], self.r2b, me.to_x
        else:
            k = slot - 4
            src, dst, dev = self.s2.at[lax.rem(me.z + k, 4)], self.r3.at[k - 1], me.to_z(k)
        return remote(src, dst, self.ss.at[slot], self.rs.at[slot], dev)

    def core(self):
        self.hop(0).start()

    def plane1(self):
        me = self.me
        self.hop(0).wait_recv()

        def add(i, _):
            k = (i // 4, lax.rem(i // 2, 2), lax.rem(i, 2))
            self.s0[k] = (self.g[k + (me.c,)].astype(f32) + self.r0[k].astype(f32)).astype(bf)
            return 0

        lax.fori_loop(0, 16, add, 0)
        self.hop(1).start()
        self.hop(2).start()

    def plane2(self):
        me, h = self.me, self.h
        n = self.g.shape[-1] - h
        self.hop(1).wait_recv()
        self.hop(2).wait_recv()

        def add(i, _):
            z, k = i // 2, lax.rem(i, 2)
            a = self.s0[z, k, me.x, :, pl.ds(0, h)].astype(f32) + self.r1a[z, k].astype(f32)
            self.s1a[z, k] = a.astype(bf)
            b = self.s0[z, me.y, k, :, pl.ds(h, n)].astype(f32) + self.r1b[z, k].astype(f32)
            self.s1b[z, k] = b.astype(bf)
            return 0

        lax.fori_loop(0, 8, add, 0)
        self.hop(3).start()
        self.hop(4).start()

    def column(self):
        me, h = self.me, self.h
        self.hop(3).wait_recv()
        self.hop(4).wait_recv()
        for z in range(4):
            self.s2[z, :, 0:h] = (self.s1a[z, me.y].astype(f32) + self.r2a[z].astype(f32)).astype(bf)
            self.s2[z, :, h:] = (self.s1b[z, me.x].astype(f32) + self.r2b[z].astype(f32)).astype(bf)
        for k in (2, 1, 3):
            self.hop(4 + k).start()

    def finish(self):
        acc = self.s2[self.me.z].astype(f32)
        for k in (1, 2, 3):
            self.hop(4 + k).wait_recv()
            acc += self.r3[k - 1].astype(f32)
        self.out[...] = acc
        for slot in range(8):
            self.hop(slot).wait_send()
        return jnp.sum(acc * acc)


class Sums:
    def __init__(self, me, tb, ss, rs, rows=0):
        self.me, self.tb, self.ss, self.rs, self.rows = me, tb, ss, rs, rows

    def hop(self, slot):
        me = self.me
        src, dst, dev = ((0, 1, me.sib), (2, 3, me.to_x), (4, 5, me.to_y))[slot] if slot < 3 else (
            6 + me.z, 6 + me.z, me.to_z(slot - 2)
        )
        return remote(self.tb.at[src], self.tb.at[dst], self.ss.at[slot], self.rs.at[slot], dev)

    def merge(self, dst, at, rows):
        n = len(at)
        parts = [self.tb[a] for a in at]
        total = parts[0] + parts[1] if n == 2 else (parts[0] + parts[1]) + (parts[2] + parts[3])
        if not self.rows:
            dst[...] = total
            return
        mean = total[6:7] / n
        off = [p[6:7] - mean for p in parts]
        squares = off[0] * off[0] + off[1] * off[1]
        if n == 4:
            squares += off[2] * off[2] + off[3] * off[3]
        dst[0:6] = total[0:6]
        dst[6:7] = mean
        dst[7:8] = total[7:8] + rows * squares

    def step(self, i):
        if i > 0:
            self.hop(i - 1).wait_recv()
            at = 2 * i if i < 3 else 6 + self.me.z
            self.merge(self.tb.at[at], (2 * i - 2, 2 * i - 1), self.rows * 2 ** (i - 1))
        for slot in (i,) if i < 3 else (3, 4, 5):
            self.hop(slot).start()

    def finish(self, dst):
        for k in (1, 2, 3):
            at = self.tb.at[6 + lax.rem(self.me.z + 4 - k, 4)]
            remote(at, at, self.ss.at[2 + k], self.rs.at[2 + k], self.me.sib).wait_recv()
        for slot in range(6):
            self.hop(slot).wait_send()
        self.merge(dst, (6, 7, 8, 9), self.rows * 8)


class Refs:
    pass


def tables_kernel(direct, names, *refs):
    r = Refs()
    for name, ref in zip(names, refs, strict=True):
        setattr(r, name, ref)
    t = pl.program_id(0)
    first = t == 0
    last = t == pl.num_programs(0) - 1
    T, D = r.tag.shape
    I = r.imglow.shape[0]
    NK = T + I
    hd = D // HEADS
    F = r.plow.shape[1]
    r.hidlow, r.rlow, r.hplow = (r.dqkv.at[:, i * D : (i + 1) * D] for i in range(3))
    r.act = r.dkvi.at[0:T]
    r.dqT = r.attT
    count = r.counts[t]
    half = HEADS // 4
    HC = D // 2
    if direct:
        me = Place()
        gat = [
            Gather(me, r.wq, r.gs.at[0], r.gs.at[1], True),
            Gather(me, r.wr, r.gs.at[2], r.gs.at[3], True),
            Gather(me, r.wd, r.gs.at[4], r.gs.at[5], True),
        ]
        sems = [(r.cs.at[2 * i], r.cs.at[2 * i + 1]) for i in range(7)]
        sq0 = Scatter(me, r.gq0, r.oq0, r.bq0, sems[0])
        sq1 = Scatter(me, r.gq1, r.oq1, r.bq1, sems[1])
        sr0 = Scatter(me, r.gr0, r.or0, r.br0, sems[2])
        sr1 = Scatter(me, r.gr1, r.or1, r.br1, sems[3])
        sd = Scatter(me, r.gd, r.od, r.bd, sems[4])
        sm = Sums(me, r.tb, *sems[5])
        ss = Sums(me, r.sb, *sems[6], rows=r.img.shape[0])
    wout_ref = r.wr.at[:, 0:D]
    wup_ref = r.wr.at[:, D : D + F]

    def when_last(*steps):
        @pl.when(last)
        def _():
            for step in steps:
                step()

    def clear():
        for ref in (r.aqkv, r.aout, r.aup, r.adn, r.terms):
            ref[...] = jnp.zeros_like(ref)

    def enter():
        img_in = pltpu.make_async_copy(r.img_hbm, r.img, r.isem)
        img_in.start()
        R, RD = r.pqkv.shape[0], r.pdn.shape[0]
        own = pl.ds(mo(me.d * R, R), R)
        r.wq[own, :] = r.pqkv[...].astype(bf)
        r.wr[own, pl.ds(0, D)] = r.pout[...].astype(bf)
        r.wr[own, pl.ds(D, F)] = r.pup[...].astype(bf)
        r.wd[pl.ds(mo(me.d * RD, RD), RD), :] = r.pdn[...].astype(bf)
        greet(me)
        for g in gat:
            g.start()
        cols = D // 32
        lane = lax.broadcasted_iota(jnp.int32, (cols, D), 1)
        unit = lax.broadcasted_iota(jnp.int32, (cols, D), 0)
        at = (lane == unit + cols * me.d).astype(bf)
        r.sb[0, 0:6, :] = dg(r.pnorm[...].astype(bf), at, 1, 0)
        img_in.wait()
        rows = r.img.shape[0]
        part = 112 if rows % 112 == 0 else I

        def over_rows(f):
            def step(i, acc):
                return acc + f(r.img[pl.ds(mo(i * part, 16), part), :].astype(f32))

            return jnp.sum(lax.fori_loop(0, rows // part, step, jnp.zeros((8, D), f32)), 0, keepdims=True)

        def fold(a):
            return jnp.sum(a.reshape(-1, 8, D), 0)

        mean_d = over_rows(fold) / rows
        m2 = over_rows(lambda a: fold((a - mean_d) * (a - mean_d)))
        r.sb[0, 6:7, :] = mean_d
        r.sb[0, 7:8, :] = m2
        ss.step(0)
        clear()
        ss.step(1)
        gat[0].column()
        ss.step(2)
        gat[0].plane()
        ss.step(3)
        gat[1].column()
        gat[2].column()
        gat[0].corner()
        ss.finish(r.gains)
        r.stats[0:1, :] = r.gains[6:7, :]
        r.stats[1:2, :] = lax.rsqrt(r.gains[7:8, :] / (rows * 32) + EPS)
        gat[0].finish()

    def gather_step(k):
        for g in gat[1:]:
            (g.plane, g.corner, g.finish)[k]()

    pl.when(first)(enter if direct else clear)

    img_ref = r.img.at[pl.ds(mo(t * I, 16), I)] if direct else r.img
    mean = r.stats[0:1, :]
    inv = r.stats[1:2, :]
    g1, b1, g2 = r.gains[0:1, :], r.gains[1:2, :], r.gains[2:3, :]
    b2, gb, bb = r.gains[3:4, :], r.gains[4:5, :], r.gains[5:6, :]
    img_parts = ((0, 256), (256, 256), (512, I - 512))

    for r0, rl in img_parts:
        img_hat = (img_ref[r0 : r0 + rl, :].astype(f32) - mean) * inv
        r.imglow[r0 : r0 + rl, :] = (img_hat * gb + bb).astype(bf)
    for r0 in range(0, T, 256):
        q = dg(r.tag[r0 : r0 + 256, :], r.wq[:, 0:D], 1, 0).astype(bf) * bf(1.0 / math.sqrt(hd))
        r.q[r0 : r0 + 256, :] = q
        r.qT[:, r0 : r0 + 256] = q.T
    key_parts = tuple((r0, 256) for r0 in range(0, T, 256)) + tuple((T + r0, rl) for r0, rl in img_parts)
    for j, dst in enumerate((r.kall, r.vall)):
        w = r.wq[:, (j + 1) * D : (j + 2) * D]
        for k0, kl in key_parts:
            rows = r.tag[k0 : k0 + kl, :] if k0 < T else r.imglow[k0 - T : k0 - T + kl, :]
            a = dg(rows, w, 1, 0).astype(bf)
            dst[k0 : k0 + kl, :] = a
            if j == 1:
                r.xT[:, k0 : k0 + kl] = a.T
    for ref, k0 in ((r.bias0, 0), (r.bias1, 256)):
        ji = k0 + lax.broadcasted_iota(jnp.int32, ref.shape, 0)
        ii = k0 + lax.broadcasted_iota(jnp.int32, ref.shape, 1)
        ref[...] = jnp.where((ji <= ii) & (ji < count), 3e38, NEG).astype(bf)

    if direct:
        pl.when(first)(functools.partial(gather_step, 0))

    chunks = [(0, 256, 0), (256, 256, 256), (512, 256, 0), (768, 256, 0), (1024, NK - 1024, 0)]
    nc = len(chunks)
    row64 = lax.broadcasted_iota(jnp.int32, (2 * hd, 1), 0)
    lane64 = lax.broadcasted_iota(jnp.int32, (1, 2 * hd), 1)

    def own_rows(a, b):
        return jnp.where((row64 < hd) if b == 0 else (row64 >= hd), a, jnp.zeros_like(a))

    def own_lanes(a, b):
        return jnp.where((lane64 < hd) if b == 0 else (lane64 >= hd), a, jnp.zeros_like(a))

    def fullq(a, q0, fill):
        if q0 == 0:
            return a
        return jnp.concatenate([jnp.full((a.shape[0], q0), fill, a.dtype), a], 1)

    def e_at(h, c):
        k0, kl, q0 = chunks[c]
        if q0:
            return r.e1.at[h]
        return r.e.at[h, 0:kl] if k0 == 0 else r.e.at[h, k0 - 256 : k0 - 256 + kl]

    def score(p, b, c, qz):
        k0, kl, q0 = chunks[c]
        ps = pl.ds(mo(p * 2 * hd, 2 * hd), 2 * hd)
        s = dg(r.kall[k0 : k0 + kl, ps], qz[:, q0:], 1, 0)
        if k0 < T:
            s = jnp.minimum(s, (r.bias1 if q0 else r.bias0)[...].astype(f32))
        r.s[k0 : k0 + kl, q0:] = s
        return fullq(jnp.max(s, 0, keepdims=True), q0, NEG)

    def query(p, b):
        return own_rows(r.qT[pl.ds(mo(p * 2 * hd, 2 * hd), 2 * hd), :], b)

    def weigh(p, b, c, m):
        k0, kl, q0 = chunks[c]
        e = jnp.exp(r.s[k0 : k0 + kl, q0:] - m[:, q0:])
        l = jnp.sum(e, 0, keepdims=True)
        e = e.astype(bf)
        e_at(2 * p + b, c)[...] = e
        o = dg(r.xT[pl.ds(mo(p * 2 * hd + b * hd, hd), hd), k0 : k0 + kl], e, 1, 0)
        return fullq(o, q0, 0.0), fullq(l, q0, 0.0)

    def head(p, b, m, following):
        qz = None if following is None else query(*following)
        m2 = None
        o = None
        for c in range(nc):
            oc, lc = weigh(p, b, c, m)
            o, l = (oc, lc) if o is None else (o + oc, l + lc)
            if following is not None:
                mc = score(*following, c, qz)
                m2 = mc if m2 is None else jnp.maximum(m2, mc)
        rl = 1.0 / l
        o = o * rl
        hs = pl.ds(mo(p * 2 * hd + b * hd, hd), hd)
        r.attT[hs, :] = o.astype(bf)
        r.rl[2 * p + b] = rl
        return m2

    def fwd_pair(p, m):
        m = head(p, 0, m, (p, 1))
        m = head(p, 1, m, (jnp.minimum(p + 1, HEADS // 2 - 1), 0))
        if direct:
            pl.when(first & (p == 1))(functools.partial(gather_step, 1))
            pl.when(first & (p == HEADS // 2 - 1))(functools.partial(gather_step, 2))
        return m

    qz = query(0, 0)
    m = None
    for c in range(nc):
        mc = score(0, 0, c, qz)
        m = mc if m is None else jnp.maximum(m, mc)
    lax.fori_loop(0, HEADS // 2, fwd_pair, m)

    RC = 256
    zero = jnp.zeros((1, D), f32)

    def rows_part(r0):
        rs = pl.ds(r0, RC)
        hp = r.tag[rs, :].astype(f32) + dg(r.attT[:, rs], wout_ref[...], 0, 0)
        yield
        c = hp - jnp.mean(hp, -1, keepdims=True)
        inv1 = lax.rsqrt(jnp.mean(c * c, -1, keepdims=True) + EPS)
        hat1 = c * inv1
        hidden = hat1 * g1 + b1
        hl = hidden.astype(bf)
        r.hidlow[rs, :] = hl
        yield
        pre = dg(hl, wup_ref[...], 1, 0)
        yield
        p2 = pre * pre
        th = jnp.tanh(GC * (pre + GA * (p2 * pre)))
        act = (0.5 * pre * (1.0 + th)).astype(bf)
        r.act[rs, :] = act
        gp = 0.5 * (1.0 + th) + 0.5 * pre * (1.0 - th * th) * (GC * (1.0 + 3 * GA * p2))
        yield
        resid = hidden + dg(act, r.wd[...], 1, 0)
        yield
        c = resid - jnp.mean(resid, -1, keepdims=True)
        inv2 = lax.rsqrt(jnp.mean(c * c, -1, keepdims=True) + EPS)
        hat2 = c * inv2
        r.mixed[rs, :] = (hat2 * g2 + b2).astype(bf)
        rows = r0 + lax.broadcasted_iota(jnp.int32, (RC, 1), 0)
        go = jnp.where(rows < count, r.cot[rs, :].astype(f32), 0.0)
        r.terms[2:3, :] += jnp.sum(go * hat2, 0, keepdims=True)
        r.terms[3:4, :] += jnp.sum(go, 0, keepdims=True)
        s = go * g2
        gr = inv2 * (s - jnp.mean(s, -1, keepdims=True) - hat2 * jnp.mean(s * hat2, -1, keepdims=True))
        rlow = gr.astype(bf)
        r.rlow[rs, :] = rlow
        yield
        gact = dg(rlow, r.wd[...], 1, 1)
        yield
        plow = (gact * gp).astype(bf)
        r.plow[rs, :] = plow
        yield
        gh = gr + dg(plow, wup_ref[...], 1, 1)
        yield
        r.terms[0:1, :] += jnp.sum(gh * hat1, 0, keepdims=True)
        r.terms[1:2, :] += jnp.sum(gh, 0, keepdims=True)
        s = gh * g1
        ghp = inv1 * (s - jnp.mean(s, -1, keepdims=True) - hat1 * jnp.mean(s * hat1, -1, keepdims=True))
        r.gtags[rs, :] = ghp
        hpl = ghp.astype(bf)
        r.hplow[rs, :] = hpl
        yield
        r.dOT[:, rs] = dg(hpl, wout_ref[...], 1, 1).astype(bf).T
        yield

    parts = [rows_part(r0) for r0 in range(0, T, RC)]
    for i in range(12 + len(parts) - 1):
        for j, part in enumerate(parts):
            if 0 <= i - j < 12:
                next(part, None)
    for h in range(HEADS):
        hs = slice(h * hd, (h + 1) * hd)
        d = r.dOT[hs, :].astype(f32) * r.rl[h]
        r.dOT[hs, :] = d.astype(bf)
        r.delta[h] = jnp.sum(d * r.attT[hs, :].astype(f32), 0, keepdims=True)
    r.dO[...] = r.dOT[...].T
    for k0, kl in key_parts:
        r.xT[:, k0 : k0 + kl] = r.kall[k0 : k0 + kl, :].T

    def put(dst, acc, r0, rn, c0, cn, add, col=None):
        rs = pl.ds(r0, rn)
        new = acc[rs, c0 : c0 + cn] + add
        acc[rs, c0 : c0 + cn] = new
        col = c0 if col is None else col
        low = new.astype(bf)
        if direct:
            R = dst.shape[4]
            nz = rn // (8 * R)
            dst[pl.ds(r0 // (8 * R), nz), :, :, :, :, col : col + cn] = low.reshape(nz, 2, 2, 2, R, cn)
        else:
            dst[rs, col : col + cn] = low

    for r0 in range(0, F, 256):
        put(r.gd, r.adn, r0, 256, 0, D, dg(r.act[:, r0 : r0 + 256], r.rlow[...], 0, 0))
    for r0 in range(0, D, 256):
        put(r.gr0, r.aout, r0, 256, 0, D, dg(r.attT[r0 : r0 + 256, :], r.hplow[...], 1, 0))
        for c0, cn, dst, col in ((0, 256, r.gr0, D), (256, 512, r.gr1, 0), (768, F - 768, r.gr1, 512)):
            put(dst, r.aup, r0, 256, c0, cn, dg(r.hidlow[:, r0 : r0 + 256], r.plow[:, c0 : c0 + cn], 0, 0), col)
    when_last(sd.core, sr0.core, sr1.core, sd.plane1) if direct else None

    def bwd_pair(p, _):
        p128 = mo(p * 2 * hd, 2 * hd)
        ps = pl.ds(p128, 2 * hd)
        dq = [None, None]
        ops = [(own_rows(r.dOT[ps, :], b), own_lanes(r.dO[:, ps], b), own_lanes(r.q[:, ps], b)) for b in range(2)]
        kc = pl.ds(mo(D + p128, 128), 2 * hd)
        vc = pl.ds(mo(2 * D + p128, 128), 2 * hd)
        for c in range(nc):
            k0, kl, q0 = chunks[c]
            ks = slice(k0, k0 + kl)
            dk = None
            for b in range(2):
                h = 2 * p + b
                hs = pl.ds(mo(p * 2 * hd + b * hd, hd), hd)
                dOz, dOl, ql = ops[b]
                dp = dg(r.vall[ks, ps], dOz[:, q0:], 1, 0)
                e = e_at(h, c)[...]
                ds = (e.astype(f32) * (dp - r.delta[h][:, q0:])).astype(bf)
                dvc = dg(e, dOl[q0:, :], 1, 0)
                dkc = dg(ds, ql[q0:, :], 1, 0)
                dqc = fullq(dg(r.xT[hs, ks], ds, 1, 0), q0, 0.0)
                dk, dv = (dkc, dvc) if dk is None else (dk + dkc, dv + dvc)
                dq[b] = dqc if dq[b] is None else dq[b] + dqc
            if k0 < T:
                r.dqkv[ks, kc] = dk.astype(bf)
                r.dqkv[ks, vc] = dv.astype(bf)
            else:
                si = slice(k0 - T, k0 - T + kl)
                r.dkvi[si, ps] = dk.astype(bf)
                r.dkvi[si, kc] = dv.astype(bf)
        for b in range(2):
            hs = pl.ds(mo(p * 2 * hd + b * hd, hd), hd)
            r.dqT[hs, :] = (dq[b] * (1.0 / math.sqrt(hd))).astype(bf)
        if direct:
            for k, steps in enumerate(
                ((sr0.plane1, sr1.plane1), (sd.plane2,), (sr1.plane2, sq0.plane1, sd.column), (sr0.column,))
            ):

                @pl.when(last & (p == k))
                def _():
                    for step in steps:
                        step()

        return 0

    for i, gq in enumerate((r.gq0, r.gq1)):
        lax.fori_loop(i * half, (i + 1) * half, bwd_pair, 0)
        hc = slice(i * HC, (i + 1) * HC)
        r.dqkv[:, hc] = r.dqT[hc, :].T
        for r0 in range(0, D, 256):
            rs = slice(r0, r0 + 256)
            x = r.tag[:, rs]
            put(gq, r.aqkv, r0, 256, i * HC, HC, dg(x, r.dqkv[:, hc], 0, 0), 0)
            for j in (1, 2):
                cs = slice(j * D + i * HC, j * D + (i + 1) * HC)
                ci = slice(cs.start - D, cs.stop - D)
                add = dg(x, r.dqkv[:, cs], 0, 0) + dg(r.imglow[:, rs], r.dkvi[:, ci], 0, 0)
                put(gq, r.aqkv, r0, 256, cs.start, HC, add, j * HC)
        if direct:
            when_last(*((sq0.core, sr0.plane2), (sq1.core,))[i])

    sg = jnp.zeros((1, D), f32)
    sb = sg
    for r0, rl in img_parts:
        rs = slice(r0, r0 + rl)
        gz = dg(r.dkvi[rs, :], r.wq[:, D:], 1, 1)
        r.gz[rs, :] = gz.astype(bf)
        hat = (img_ref[rs, :].astype(f32) - mean) * inv
        sg += jnp.sum(gz * hat, 0, keepdims=True)
        sb += jnp.sum(gz, 0, keepdims=True)
    r.terms[4:5, :] += sg
    r.terms[5:6, :] += sb
    if direct:

        @pl.when(last)
        def _():
            r.tb[0] = r.terms[...]
            sm.step(0)
            sq0.plane2()

    for r0 in range(0, T, 256):
        r.gtags[r0 : r0 + 256, :] += dg(r.dqkv[r0 : r0 + 256, :], r.wq[...], 1, 1)

    if direct:

        @pl.when(last)
        def _():
            sq1.plane1()
            sm.step(1)
            sr1.column()
            sq = sd.finish()
            sq += sr0.finish()
            sm.step(2)
            sq0.column()
            sq += sr1.finish()
            sq1.plane2()
            sm.step(3)
            sq += sq0.finish()
            sq1.column()
            sm.finish(r.small)
            tot = r.small[...]
            sq += sq1.finish()
            r.nb[me.d] = jnp.full((1, 128), sq, f32)
            push_all(me, r.nb, r.ps.at[0], r.ps.at[1])
            push_done(me, r.nb, r.ps.at[0], r.ps.at[1])
            r.nsq[...] = jnp.broadcast_to(jnp.sum(r.nb[...], 0) + jnp.sum(tot * tot), (8, 128))


def tables_call(direct, counts, tag, img, cot, params):
    n = counts.shape[0]
    T, I, D = tag.shape[0] // n, img.shape[0] // n, tag.shape[1]
    NK = T + I
    HC = D // 2
    V = lambda *s, d=bf: pltpu.VMEM(s, d)
    S = jax.ShapeDtypeStruct

    def row(a, b):
        return pl.BlockSpec((a, b), lambda t, *_: (t, 0))

    def whole(shape, **kw):
        return pl.BlockSpec(shape, lambda t, *_: (0,) * len(shape), **kw)

    one = dict(pipeline_mode=pl.Buffered(1))
    if direct:
        F = params[2].shape[1]
        R, RD = params[0].shape[0], params[3].shape[0]
        ins = [("tag", row(T, D)), ("img_hbm", pl.BlockSpec(memory_space=pl.ANY)), ("cot", row(T, D))]
        ins += [(k, whole(a.shape, **one)) for k, a in zip(("pqkv", "pout", "pup", "pdn", "pnorm"), params)]
    else:
        F = params[4].shape[0]
        ins = [("tag", row(T, D)), ("img", row(I, D)), ("cot", row(T, D))]
        ins += [(k, whole(a.shape, **one)) for k, a in zip(("stats", "gains", "wq", "wr", "wd"), params)]
    outs = [
        ("mixed", S((n * T, D), bf), row(T, D)),
        ("gtags", S((n * T, D), f32), row(T, D)),
        ("gz", S((n * I, D), bf), row(I, D)),
    ]
    scratch = [
        ("imglow", V(I, D)), ("kall", V(NK, D)), ("vall", V(NK, D)), ("xT", V(D, NK)),
        ("q", V(T, D)), ("qT", V(D, T)), ("bias0", V(256, T)), ("bias1", V(256, T - 256)), ("s", V(NK, T, d=f32)),
        ("e", V(HEADS, NK - 256, T)), ("e1", V(HEADS, 256, T - 256)), ("attT", V(D, T)),
        ("rl", V(HEADS, 1, T, d=f32)), ("plow", V(T, F)),
        ("dqkv", V(T, 3 * D)), ("dkvi", V(I, 2 * D)), ("dO", V(T, D)),
        ("dOT", V(D, T)), ("delta", V(HEADS, 1, T, d=f32)), ("aqkv", V(D, 3 * D, d=f32)), ("aout", V(D, D, d=f32)),
        ("aup", V(D, F, d=f32)), ("adn", V(F, D, d=f32)),
    ]
    if direct:
        outs += [
            ("oq0", S((R, 3 * HC), f32), None), ("oq1", S((R, 3 * HC), f32), None), ("or0", S((R, 3 * HC), f32), None),
            ("or1", S((R, D + F - 3 * HC), f32), None), ("od", S((RD, D), f32), None), ("small", S((8, D), f32), None), ("nsq", S((8, 128), f32), None),
            ("stats", S((2, D), f32), None), ("gains", S((8, D), f32), None),
        ]
        dims = (4, 2, 2, 2)
        dma = pltpu.SemaphoreType.DMA
        scratch += [
            ("img", V(n * I, D)), ("wq", V(D, 3 * D)), ("wr", V(D, D + F)), ("wd", V(F, D)), ("sb", V(10, 8, D, d=f32)),
            ("nb", V(32, 1, 128, d=f32)), ("terms", V(8, D, d=f32)), ("tb", V(10, 8, D, d=f32)),
            ("gq0", V(*dims, R, 3 * HC)), ("gq1", V(*dims, R, 3 * HC)), ("gr0", V(*dims, R, 3 * HC)),
            ("gr1", V(*dims, R, D + F - 3 * HC)), ("gd", V(*dims, RD, D)),
            ("bq0", Scatter.bufs(R, 3 * HC)), ("bq1", Scatter.bufs(R, 3 * HC)), ("br0", Scatter.bufs(R, 3 * HC)),
            ("br1", Scatter.bufs(R, D + F - 3 * HC)),
            ("bd", Scatter.bufs(RD, D)),
            ("isem", dma), ("gs", dma((6, Gather.SLOTS))), ("cs", dma((14, Scatter.SLOTS))), ("ps", dma((2, 32))),
        ]
        extra = dict(collective_id=0, has_side_effects=True)
    else:
        outs += [
            ("gq0", S((D, 3 * HC), bf), None), ("gq1", S((D, 3 * HC), bf), None), ("gr0", S((D, 3 * HC), bf), None),
            ("gr1", S((D, D + F - 3 * HC), bf), None),
            ("gd", S((F, D), bf), None), ("terms", S((8, D), f32), None),
        ]
        extra = {}
    names = ("counts",) + tuple(k for k, _ in ins) + tuple(k for k, _, _ in outs) + tuple(k for k, _ in scratch)
    return pl.pallas_call(
        functools.partial(tables_kernel, direct, names),
        out_shape=[s for _, s, _ in outs],
        grid_spec=pltpu.PrefetchScalarGridSpec(
            num_scalar_prefetch=1,
            grid=(n,),
            in_specs=[b for _, b in ins],
            out_specs=[whole(s.shape) if b is None else b for _, s, b in outs],
            scratch_shapes=[a for _, a in scratch],
        ),
        compiler_params=pltpu.CompilerParams(vmem_limit_bytes=63 * 2**20, **extra),
        name="tables",
    )(counts, tag, img, cot, *params)


def update_kernel(n_params, parts, place, gz_in, img_in, stats_ref, gains_ref, small_ref, nsq_ref, *refs):
    n_in = 5 + 3 * n_params
    n_out = 5 * n_params
    hbm_in, (mixed_in, gtags_in), refs = refs[:n_in], refs[n_in : n_in + 2], refs[n_in + 2 :]
    (mixed_out, gtags_out, gimg_out, norm_ref), refs = refs[:4], refs[4:]
    hbm_out, refs = refs[:n_out], refs[n_out:]
    ins, outs, refs = refs[:n_in], refs[n_in : n_in + n_out], refs[n_in + n_out :]
    mixed, gtags, gz, img, gimg, in_sem, out_sem, pass_sem, part_sem = refs
    rows, D = gz.shape
    copy = pltpu.make_async_copy

    def part(i):
        at = pl.ds(i * (rows // parts), rows // parts)
        return at, copy(gz_in.at[at], gz.at[at], part_sem.at[0, i]), copy(img_in.at[at], img.at[at], part_sem.at[1, i])

    def given(i):
        at = pl.ds(i * (rows // parts), rows // parts)
        return copy(gimg.at[at], gimg_out.at[at], part_sem.at[2, i])

    for i in range(parts):
        _, a, b = part(i)
        a.start()
        b.start()
    for i, (a, b) in enumerate(((gtags_in, gtags), (mixed_in, mixed))):
        copy(a, b, pass_sem.at[i]).start()
    for i, (a, b) in enumerate(zip(hbm_in, ins)):
        copy(a, b, in_sem.at[i]).start()

    total_rows = place[1].astype(f32)
    gb = gains_ref[4:5, :]
    k = stats_ref[1:2, :] * gb
    gsum = small_ref[4:5, :] / total_rows
    bsum = small_ref[5:6, :] / total_rows
    for i in range(parts):
        at, a, b = part(i)
        a.wait()
        b.wait()
        hat = (img[at, :].astype(f32) - stats_ref[0:1, :]) * stats_ref[1:2, :]
        gimg[at, :] = k * (gz[at, :].astype(f32) - bsum - hat * gsum)
        given(i).start()
    for i, (a, b, c) in enumerate(((gtags_in, gtags, gtags_out), (mixed_in, mixed, mixed_out))):
        copy(a, b, pass_sem.at[i]).wait()
        copy(b, c, pass_sem.at[2 + i]).start()

    for i, (a, b) in enumerate(zip(hbm_in, ins)):
        copy(a, b, in_sem.at[i]).wait()
    oq0, oq1, or0, or1, od = ins[:5]
    masters, firsts, seconds = (ins[5 + n_params * i : 5 + n_params * (i + 1)] for i in range(3))
    total_norm = jnp.sqrt(nsq_ref[0:1, 0:1])
    norm_ref[...] = total_norm
    factor = CLIP_AT / jnp.maximum(total_norm, CLIP_AT)
    cols = masters[4].shape[1]
    row = lax.broadcasted_iota(jnp.int32, (D, cols), 0)
    col = lax.broadcasted_iota(jnp.int32, (D, cols), 1)
    pick = (row == col + place[0] * cols).astype(f32)
    own = lax.dot_general(
        small_ref[...], pick, (((1,), (0,)), ((), ())), precision=lax.Precision.HIGHEST, preferred_element_type=f32
    )[0:6]
    hc = D // 2
    oq = [o[:, j * hc : (j + 1) * hc] for j in range(3) for o in (oq0, oq1)]
    grads = (jnp.concatenate(oq, 1), or0[:, 0:D], jnp.concatenate([or0[:, D:], or1[...]], 1), od[...], own)
    rates = (RATE_MATRIX, RATE_OUTPUT, RATE_MATRIX, RATE_MATRIX, RATE_NORMS)
    for i, (g, w, f, v) in enumerate(zip(grads, masters, firsts, seconds)):
        clip = g * factor
        moment = BETA_FIRST * f[...] + (1.0 - BETA_FIRST) * clip
        square = BETA_SECOND * v[...] + (1.0 - BETA_SECOND) * clip * clip
        u = (moment / (1.0 - BETA_FIRST**STEP)) / (jnp.sqrt(square / (1.0 - BETA_SECOND**STEP)) + ADAM_EPS)
        if i < 4:
            new = w[...] - rates[i] * (u + DECAY_RATE * w[...])
        else:
            new = w[...] - rates[i] * u
        for j, value in enumerate((clip, moment, square, new, new.astype(bf))):
            at = 5 * j + i
            outs[at][...] = value
            copy(outs[at], hbm_out[at], out_sem.at[at]).start()

    for i in range(n_out):
        copy(outs[i], hbm_out[i], out_sem.at[i]).wait()
    for i, (b, c) in enumerate(((gtags, gtags_out), (mixed, mixed_out))):
        copy(b, c, pass_sem.at[2 + i]).wait()
    for i in range(parts):
        given(i).wait()


def update(place, mixed, gtags, gz, img, stats, gains, small, nsq, owned, masters, firsts, seconds):
    rows = gz.shape[0]
    parts = 7 if rows % 112 == 0 else 3
    anywhere = pl.BlockSpec(memory_space=pl.ANY)
    windows = (stats, gains, small, nsq)
    manual = tuple(owned) + tuple(masters) + tuple(firsts) + tuple(seconds)
    shapes = [jax.ShapeDtypeStruct(m.shape, f32) for m in masters] * 4 + [jax.ShapeDtypeStruct(m.shape, bf) for m in masters]
    gimg = jax.ShapeDtypeStruct(gz.shape, f32)
    dma = pltpu.SemaphoreType.DMA
    passed = [jax.ShapeDtypeStruct(a.shape, a.dtype) for a in (mixed, gtags)]
    return pl.pallas_call(
        functools.partial(update_kernel, len(masters), parts),
        out_shape=passed + [gimg, jax.ShapeDtypeStruct((1, 1), f32)] + shapes,
        in_specs=[pl.BlockSpec(memory_space=pltpu.SMEM)] + [anywhere] * 2 + [VM] * 4 + [anywhere] * (len(manual) + 2),
        out_specs=[anywhere] * 3 + [VM] + [anywhere] * len(shapes),
        scratch_shapes=[pltpu.VMEM(a.shape, a.dtype) for a in manual + tuple(shapes) + tuple(passed) + (gz, img, gimg)]
        + [dma((len(manual),)), dma((len(shapes),)), dma((4,)), dma((3, parts))],
        compiler_params=pltpu.CompilerParams(vmem_limit_bytes=63 * 2**20),
        name="update",
    )(place, gz, img, *windows, *manual, mixed, gtags)


def gather_any(img, wqkv, wout, wup, wdn, norm):
    full = lambda a, axis: lax.all_gather(a.astype(bf), AXES, axis=axis, tiled=True)
    gr = jnp.concatenate([full(wout, 0), full(wup, 0)], 1)
    gains = jnp.concatenate([full(norm, 1).astype(f32), jnp.zeros((2, img.shape[1]), f32)], 0)
    values = img.astype(f32)
    total = img.shape[0] * lax.axis_size(AXES)
    mean = lax.psum(jnp.sum(values, 0), AXES) / total
    centred = values - mean
    spread = lax.psum(jnp.sum(centred * centred, 0), AXES) / total
    return full(wqkv, 0), gr, full(wdn, 0), jnp.stack([mean, lax.rsqrt(spread + EPS)]), gains


def scatter_any(gq0, gq1, gr0, gr1, gd, terms):
    part = lambda a: lax.psum_scatter(a.astype(f32), AXES, scatter_dimension=0, tiled=True)
    owned = [part(a) for a in (gq0, gq1, gr0, gr1, gd)]
    small = lax.psum(terms, AXES)
    local = sum(jnp.sum(a * a) for a in owned)
    nsq = lax.psum(local, AXES) + jnp.sum(small * small)
    return *owned, small, jnp.full((8, 128), nsq, f32)


def shards(direct, tag_inputs, image_inputs, tag_counts, cotangent, *params):
    masters, firsts, seconds = params[0:5], params[5:10], params[10:15]
    tables = tag_counts.shape[0]
    devices = lax.axis_size(AXES)
    total_rows = image_inputs.shape[0] * devices
    if direct:
        mixed, gtags, gz, *owned, small, nsq, stats, gains = tables_call(
            True, tag_counts, tag_inputs, image_inputs, cotangent, masters
        )
    else:
        wq, wr, wd, stats, gains = gather_any(image_inputs, *masters)
        mixed, gtags, gz, *sums = tables_call(
            False, tag_counts, tag_inputs, image_inputs, cotangent, (stats, gains, wq, wr, wd)
        )
        *owned, small, nsq = scatter_any(*sums)
    place = jnp.stack([lax.axis_index(AXES), jnp.int32(total_rows)])
    mixed, gtags, gimg, norm, *rest = update(
        place, mixed, gtags, gz, image_inputs, stats, gains, small, nsq, owned, masters, firsts, seconds
    )
    return (mixed, gtags, gimg, norm.reshape(()), *rest)


def solution(mesh):
    rows = P(AXES, None)
    state = (rows, rows, rows, rows, P(None, AXES))
    direct = dict(mesh.shape) == {"wide": 16, "narrow": 2}
    return jax.shard_map(
        functools.partial(shards, direct),
        mesh=mesh,
        in_specs=(rows, rows, P(AXES), rows) + state * 3,
        out_specs=(rows, rows, rows, P()) + state * 5,
        check_vma=False,
    )
```

time: 203 us -> 162 us (0.80)
  Pallas kernels: 187 us -> 160 us
  local copies, waits for them, and re-layouts: 13.6 us -> 0 us
    pallas_call x1, Pallas kernels: 183 us -> 150 us  [tables_call(): pl.pallas_call(functools.partial(tables_kernel, direct, names), out_shape...]
    unnamed x56 -> x0, local copies, waits for them, and re-layouts: 13.6 us -> none
    pallas_call x1, Pallas kernels: 4.58 us -> 10.1 us  [update(): pl.pallas_call(functools.partial(update_kernel, len(masters), parts), out...]
where the time goes in v3:
time: 162 us
  Pallas kernels  160 us (99%)
    pallas_call x1, Pallas kernels, tables_call(): pl.pallas_call(functools.partial(tables_kernel, direct, names), out_shape...  150 us
    pallas_call x1, Pallas kernels, update(): pl.pallas_call(functools.partial(update_kernel, len(masters), parts), out...  10.1 us

profile of v3, /device:TPU:0, one launch (start us, length us, event | category | flops | bytes accessed | tf_op | source)
XLA Modules:
  0.0 161.8 jit_solution(16957682922325037212)
XLA Ops:
  0.7 0.6 pad_add_fusion.place
  1.3 150.2 %tables.1 = (bf16[1536,512]{1,0:T(8,128)(2,1)}, f32[1536,512]{1,0:T(8,128)}, bf16[2352,512]{1,0:T(8,128)(2,1)}, f32[16,768]{1,0:T(8,128)}, f32[16,768]{1,0:T(8,1...) custom-call(s32[3]{0:T(128)} %refs_0_.1, ...), custom_call_target="tpu_custom_call" | custom-call | tf_op jit(solution)/shard_map/tables/pallas_call | solution.py:769
  151.5 10.1 %update.1 = (bf16[1536,512]{1,0:T(8,128)(2,1)}, f32[1536,512]{1,0:T(8,128)}, f32[2352,512]{1,0:T(8,128)}, f32[1,1]{1,0:T(1,128)}, f32[16,1536]{1,0:T(8,128)}, /*...) custom-call(s32[2]{0:T(128)} %pad_add_fusion.place, ...), custom_call_target="tpu_custom_call" | custom-call | tf_op jit(solution)/shard_map/update/pallas_call | solution.py:878

commit v4 on v3

--- a/solution.py
+++ b/solution.py
@@ -43,6 +43,7 @@
         self.d = self.w * 2 + self.c
         self.to_x = (self.w + 1 - 2 * self.x, self.c)
         self.to_y = (self.w + 2 - 4 * self.y, self.c)
+        self.to_d = (self.w + 3 - 2 * self.x - 4 * self.y, self.c)
         self.sib = (self.w, 1 - self.c)
 
     def to_z(self, k):
@@ -55,7 +56,7 @@
 
 def greet(me):
     bar = pltpu.get_barrier_semaphore()
-    near = (me.sib, me.to_x, me.to_y, me.to_z(1), me.to_z(2), me.to_z(3))
+    near = (me.sib, me.to_x, me.to_y, me.to_d, me.to_z(1), me.to_z(2), me.to_z(3))
     for dev in near:
         pl.semaphore_signal(bar, inc=1, device_id=dev, device_id_type=MESH)
     pl.semaphore_wait(bar, len(near))
@@ -72,31 +73,25 @@
 
 
 class Gather:
-    SLOTS = 35
-
-    def __init__(self, me, g, ss, rs, split):
+    SLOTS = 23
+
+    def __init__(self, me, g, ss, rs):
         self.me, self.g, self.ss, self.rs = me, g, ss, rs
-        self.rows = g.shape[0] // 32
-        n = g.shape[1]
-        self.h = n // 2 if split else n
-        self.split = split
+        self.h = g.shape[-1] // 2
         self.sent = []
 
-    def ref(self, kz, pos, part=None, c=None):
+    def ref(self, k, pos, part=None, c=None):
         me = self.me
-        z = lax.rem(me.z + 4 - kz, 4)
+        z = slice(None) if k is None else lax.rem(me.z + 4 - k, 4)
         y = me.y if pos in (0, 1) else 1 - me.y
         x = me.x if pos in (0, 2) else 1 - me.x
-        d = z * 8 + y * 4 + x * 2 + (me.c if c is None else c)
-        rows = pl.ds(mo(d * self.rows, self.rows), self.rows)
-        if part is None:
-            return self.g.at[rows]
-        return self.g.at[rows, pl.ds(part * self.h, self.h)]
-
-    def go(self, kz, pos, part, slot, dev):
-        ref = self.ref(kz, pos, part)
+        at = (z, y, x, me.c if c is None else c)
+        return self.g.at[at] if part is None else self.g.at[at + (slice(None), pl.ds(part * self.h, self.h))]
+
+    def go(self, k, pos, part, slot, dev):
+        ref = self.ref(k, pos, part)
         remote(ref, ref, self.ss.at[slot], self.rs.at[slot], dev).start()
-        self.sent.append((kz, pos, part, slot))
+        self.sent.append((k, pos, part, slot))
 
     def got(self, slot, *key, **kw):
         ref = self.ref(*key, **kw)
@@ -108,54 +103,44 @@
             self.go(0, 0, None, k - 1, me.to_z(k))
         self.go(0, 0, None, 3, me.to_x)
         self.go(0, 0, None, 7, me.to_y)
-        self.go(0, 0, None, 19, me.sib)
-
-    def column(self):
+
+    def share(self, pos):
+        self.go(None, pos, None, 19 + pos, self.me.sib)
+
+    def column(self, *ks):
         me = self.me
-        for k in (1, 3, 2):
+        for k in ks:
             self.got(k - 1, k, 0)
             self.go(k, 0, None, 3 + k, me.to_x)
             self.go(k, 0, None, 7 + k, me.to_y)
-            self.go(k, 0, None, 19 + k, me.sib)
-
-    def plane(self):
+
+    def plane(self, *ks):
         me = self.me
-        for k in (0, 1, 3, 2):
+        for k in ks:
             self.got(3 + k, k, 1)
             self.go(k, 1, 0, 11 + k, me.to_y)
-            self.go(k, 1, None, 23 + k, me.sib)
             self.got(7 + k, k, 2)
-            if self.split:
-                self.go(k, 2, 1, 15 + k, me.to_x)
-            self.go(k, 2, None, 27 + k, me.sib)
-
-    def corner(self):
-        me = self.me
-        for k in (0, 1, 3, 2):
+            self.go(k, 2, 1, 15 + k, me.to_x)
+
+    def corner(self, *ks):
+        for k in ks:
             self.got(11 + k, k, 3, 0)
-            if self.split:
-                self.got(15 + k, k, 3, 1)
-            self.go(k, 3, None, 31 + k, me.sib)
+            self.got(15 + k, k, 3, 1)
 
     def finish(self):
         for pos in range(4):
-            for k in range(4):
-                self.got(19 + 4 * pos + k, k, pos, c=1 - self.me.c)
-        for kz, pos, part, slot in self.sent:
-            ref = self.ref(kz, pos, part)
+            self.got(19 + pos, None, pos, c=1 - self.me.c)
+        for k, pos, part, slot in self.sent:
+            ref = self.ref(k, pos, part)
             remote(ref, ref, self.ss.at[slot], self.rs.at[slot], self.me.sib).wait_send()
 
 
 def push_all(me, g, ss, rs):
     for k in range(1, 32):
-        remote(g.at[me.d], g.at[me.d], ss.at[k], rs.at[k], me.peer(k)).start()
-
-
-def push_done(me, g, ss, rs):
-    for k in range(1, 32):
-        remote(g.at[me.d], g.at[me.d], ss.at[k], rs.at[k], me.sib).wait_send()
-        src = lax.rem(me.d + 32 - k, 32)
-        remote(g.at[src], g.at[src], ss.at[k], rs.at[k], me.sib).wait_recv()
+        remote(g.at[me.d], g.at[me.d], ss, rs, me.peer(k)).start()
+    all_of = remote(g.at[pl.ds(0, 31)], g.at[pl.ds(0, 31)], ss, rs, me.sib)
+    all_of.wait_send()
+    all_of.wait_recv()
 
 
 class Scatter:
@@ -176,8 +161,10 @@
         ]
 
     def hop(self, slot):
-        me, h = self.me, self.h
-        n = self.g.shape[-1] - h
+        me = self.me
+        if slot in (1, 2):
+            h = self.h
+            n = self.g.shape[-1] - h
         if slot == 0:
             src, dst, dev = self.g.at[:, :, :, 1 - me.c], self.r0, me.sib
         elif slot == 1:
@@ -196,16 +183,17 @@
     def core(self):
         self.hop(0).start()
 
-    def plane1(self):
+    slots = tuple(range(8))
+
+    def first_sum(self):
         me = self.me
         self.hop(0).wait_recv()
 
-        def add(i, _):
-            k = (i // 4, lax.rem(i // 2, 2), lax.rem(i, 2))
-            self.s0[k] = (self.g[k + (me.c,)].astype(f32) + self.r0[k].astype(f32)).astype(bf)
-            return 0
-
-        lax.fori_loop(0, 16, add, 0)
+        for z in range(4):
+            self.s0[z] = self.g[z, :, :, me.c] + self.r0[z]
+
+    def plane1(self):
+        self.first_sum()
         self.hop(1).start()
         self.hop(2).start()
 
@@ -215,15 +203,9 @@
         self.hop(1).wait_recv()
         self.hop(2).wait_recv()
 
-        def add(i, _):
-            z, k = i // 2, lax.rem(i, 2)
-            a = self.s0[z, k, me.x, :, pl.ds(0, h)].astype(f32) + self.r1a[z, k].astype(f32)
-            self.s1a[z, k] = a.astype(bf)
-            b = self.s0[z, me.y, k, :, pl.ds(h, n)].astype(f32) + self.r1b[z, k].astype(f32)
-            self.s1b[z, k] = b.astype(bf)
-            return 0
-
-        lax.fori_loop(0, 8, add, 0)
+        for z in range(4):
+            self.s1a[z] = self.s0[z, :, me.x, :, pl.ds(0, h)] + self.r1a[z]
+            self.s1b[z] = self.s0[z, me.y, :, :, pl.ds(h, n)] + self.r1b[z]
         self.hop(3).start()
         self.hop(4).start()
 
@@ -232,8 +214,8 @@
         self.hop(3).wait_recv()
         self.hop(4).wait_recv()
         for z in range(4):
-            self.s2[z, :, 0:h] = (self.s1a[z, me.y].astype(f32) + self.r2a[z].astype(f32)).astype(bf)
-            self.s2[z, :, h:] = (self.s1b[z, me.x].astype(f32) + self.r2b[z].astype(f32)).astype(bf)
+            self.s2[z, :, 0:h] = self.s1a[z, me.y] + self.r2a[z]
+            self.s2[z, :, h:] = self.s1b[z, me.x] + self.r2b[z]
         for k in (2, 1, 3):
             self.hop(4 + k).start()
 
@@ -243,9 +225,49 @@
             self.hop(4 + k).wait_recv()
             acc += self.r3[k - 1].astype(f32)
         self.out[...] = acc
-        for slot in range(8):
+        for slot in self.slots:
             self.hop(slot).wait_send()
         return jnp.sum(acc * acc)
+
+
+class ScatterPlane(Scatter):
+    def __init__(self, me, g, out, bufs, sems):
+        self.me, self.g, self.out, (self.ss, self.rs) = me, g, out, sems
+        self.r0, self.rp, self.s2, self.r3 = bufs
+        self.s0 = self.r0
+
+    @staticmethod
+    def bufs(R, N):
+        v = lambda *s: pltpu.VMEM(s, bf)
+        return [v(4, 2, 2, R, N), v(3, 4, R, N), v(4, R, N), v(3, R, N)]
+
+    def hop(self, slot):
+        me = self.me
+        if slot in (0, 5, 6, 7):
+            return Scatter.hop(self, slot)
+        y = me.y if slot == 1 else 1 - me.y
+        x = me.x if slot == 2 else 1 - me.x
+        dev = (me.to_x, me.to_y, me.to_d)[slot - 1]
+        return remote(self.s0.at[:, y, x], self.rp.at[slot - 1], self.ss.at[slot], self.rs.at[slot], dev)
+
+    def plane1(self):
+        self.first_sum()
+        for slot in (3, 1, 2):
+            self.hop(slot).start()
+
+    def column(self):
+        me = self.me
+        for slot in (1, 2, 3):
+            self.hop(slot).wait_recv()
+        for z in range(4):
+            total = self.s0[z, me.y, me.x].astype(f32)
+            for i in range(3):
+                total += self.rp[i, z].astype(f32)
+            self.s2[z] = total.astype(bf)
+        for k in (2, 1, 3):
+            self.hop(4 + k).start()
+
+    slots = (0, 1, 2, 3, 5, 6, 7)
 
 
 class Sums:
@@ -254,10 +276,23 @@
 
     def hop(self, slot):
         me = self.me
-        src, dst, dev = ((0, 1, me.sib), (2, 3, me.to_x), (4, 5, me.to_y))[slot] if slot < 3 else (
-            6 + me.z, 6 + me.z, me.to_z(slot - 2)
-        )
+        if slot == 0:
+            src, dst, dev = 0, 1, me.sib
+        elif slot < 4:
+            src = dst = 2 + me.y * 2 + me.x
+            dev = (me.to_x, me.to_y, me.to_d)[slot - 1]
+        else:
+            src = dst = 6 + me.z
+            dev = me.to_z(slot - 3)
         return remote(self.tb.at[src], self.tb.at[dst], self.ss.at[slot], self.rs.at[slot], dev)
+
+    def arrived(self, slot):
+        me = self.me
+        y = me.y if slot == 1 else 1 - me.y
+        x = me.x if slot == 2 else 1 - me.x
+        at = 1 if slot == 0 else 2 + y * 2 + x if slot < 4 else 6 + lax.rem(me.z + 7 - slot, 4)
+        at = self.tb.at[at]
+        remote(at, at, self.ss.at[slot], self.rs.at[slot], me.sib).wait_recv()
 
     def merge(self, dst, at, rows):
         n = len(at)
@@ -276,18 +311,21 @@
         dst[7:8] = total[7:8] + rows * squares
 
     def step(self, i):
-        if i > 0:
-            self.hop(i - 1).wait_recv()
-            at = 2 * i if i < 3 else 6 + self.me.z
-            self.merge(self.tb.at[at], (2 * i - 2, 2 * i - 1), self.rows * 2 ** (i - 1))
-        for slot in (i,) if i < 3 else (3, 4, 5):
+        me = self.me
+        if i == 1:
+            self.arrived(0)
+            self.merge(self.tb.at[2 + me.y * 2 + me.x], (0, 1), self.rows)
+        if i == 2:
+            for slot in (1, 2, 3):
+                self.arrived(slot)
+            self.merge(self.tb.at[6 + me.z], (2, 3, 4, 5), self.rows * 2)
+        for slot in ((0,), (3, 1, 2), (4, 5, 6))[i]:
             self.hop(slot).start()
 
     def finish(self, dst):
-        for k in (1, 2, 3):
-            at = self.tb.at[6 + lax.rem(self.me.z + 4 - k, 4)]
-            remote(at, at, self.ss.at[2 + k], self.rs.at[2 + k], self.me.sib).wait_recv()
-        for slot in range(6):
+        for slot in (4, 5, 6):
+            self.arrived(slot)
+        for slot in range(7):
             self.hop(slot).wait_send()
         self.merge(dst, (6, 7, 8, 9), self.rows * 8)
 
@@ -312,25 +350,38 @@
     r.act = r.dkvi.at[0:T]
     r.dqT = r.attT
     count = r.counts[t]
-    half = HEADS // 4
     HC = D // 2
     if direct:
         me = Place()
-        gat = [
-            Gather(me, r.wq, r.gs.at[0], r.gs.at[1], True),
-            Gather(me, r.wr, r.gs.at[2], r.gs.at[3], True),
-            Gather(me, r.wd, r.gs.at[4], r.gs.at[5], True),
-        ]
-        sems = [(r.cs.at[2 * i], r.cs.at[2 * i + 1]) for i in range(7)]
+        gq, gw = Gather(me, r.wq, r.gs.at[0], r.gs.at[1]), Gather(me, r.ww, r.gs.at[2], r.gs.at[3])
+        sems = [(r.cs.at[2 * i], r.cs.at[2 * i + 1]) for i in range(8)]
         sq0 = Scatter(me, r.gq0, r.oq0, r.bq0, sems[0])
         sq1 = Scatter(me, r.gq1, r.oq1, r.bq1, sems[1])
+        sq2 = ScatterPlane(me, r.gq2, r.oq2, r.bq2, sems[7])
         sr0 = Scatter(me, r.gr0, r.or0, r.br0, sems[2])
         sr1 = Scatter(me, r.gr1, r.or1, r.br1, sems[3])
         sd = Scatter(me, r.gd, r.od, r.bd, sems[4])
         sm = Sums(me, r.tb, *sems[5])
         ss = Sums(me, r.sb, *sems[6], rows=r.img.shape[0])
-    wout_ref = r.wr.at[:, 0:D]
-    wup_ref = r.wr.at[:, D : D + F]
+    def cols(ref, a, b):
+        if not direct:
+            return ref[:, a:b]
+        return ref[:, :, :, :, :, a:b].reshape(D, b - a)
+
+    def w_qkv(a, b):
+        return cols(r.wq, a, b)
+
+    def w_out():
+        return cols(r.ww if direct else r.wr, 0, D)
+
+    def w_up():
+        return cols(r.ww if direct else r.wr, D, D + F)
+
+    def w_down():
+        if not direct:
+            return r.wd[...]
+        halves = [r.ww[:, :, :, :, :, a : a + D] for a in (D + F, 2 * D + F)]
+        return jnp.stack(halves, 4).reshape(F, D)
 
     def when_last(*steps):
         @pl.when(last)
@@ -346,18 +397,22 @@
         img_in = pltpu.make_async_copy(r.img_hbm, r.img, r.isem)
         img_in.start()
         R, RD = r.pqkv.shape[0], r.pdn.shape[0]
-        own = pl.ds(mo(me.d * R, R), R)
-        r.wq[own, :] = r.pqkv[...].astype(bf)
-        r.wr[own, pl.ds(0, D)] = r.pout[...].astype(bf)
-        r.wr[own, pl.ds(D, F)] = r.pup[...].astype(bf)
-        r.wd[pl.ds(mo(me.d * RD, RD), RD), :] = r.pdn[...].astype(bf)
+        own = (me.z, me.y, me.x, me.c)
+        r.wq[own + (slice(None), pl.ds(0, D))] = r.pqkv[:, 0:D].astype(bf)
+        for p in range(HEADS // 2):
+            for j in (0, 1):
+                at = (j + 1) * D + p * 2 * hd
+                to = pl.ds(D + (2 * p + j) * 2 * hd, 2 * hd)
+                r.wq[own + (slice(None), to)] = r.pqkv[:, at : at + 2 * hd].astype(bf)
         greet(me)
-        for g in gat:
-            g.start()
-        cols = D // 32
-        lane = lax.broadcasted_iota(jnp.int32, (cols, D), 1)
-        unit = lax.broadcasted_iota(jnp.int32, (cols, D), 0)
-        at = (lane == unit + cols * me.d).astype(bf)
+        gq.start()
+        for at, part in ((0, r.pout[...]), (D, r.pup[...]), (D + F, r.pdn[0:R, :]), (2 * D + F, r.pdn[R:RD, :])):
+            r.ww[own + (slice(None), pl.ds(at, part.shape[1]))] = part.astype(bf)
+        gw.start()
+        share = D // 32
+        lane = lax.broadcasted_iota(jnp.int32, (share, D), 1)
+        unit = lax.broadcasted_iota(jnp.int32, (share, D), 0)
+        at = (lane == unit + share * me.d).astype(bf)
         r.sb[0, 0:6, :] = dg(r.pnorm[...].astype(bf), at, 1, 0)
         img_in.wait()
         rows = r.img.shape[0]
@@ -379,21 +434,39 @@
         ss.step(0)
         clear()
         ss.step(1)
-        gat[0].column()
+        gq.column(1, 3, 2)
+        gq.share(0)
         ss.step(2)
-        gat[0].plane()
-        ss.step(3)
-        gat[1].column()
-        gat[2].column()
-        gat[0].corner()
+        gq.plane(0, 1, 3, 2)
+        gq.share(1)
+        gq.share(2)
+        gw.plane(0)
+        gw.column(1)
+        gq.corner(0, 1, 3, 2)
+        gq.share(3)
+        gw.column(3)
         ss.finish(r.gains)
         r.stats[0:1, :] = r.gains[6:7, :]
         r.stats[1:2, :] = lax.rsqrt(r.gains[7:8, :] / (rows * 32) + EPS)
-        gat[0].finish()
+        gq.finish()
+
+    def gather_column():
+        gw.column(2)
+        gw.share(0)
 
     def gather_step(k):
-        for g in gat[1:]:
-            (g.plane, g.corner, g.finish)[k]()
+        if k == 0:
+            gw.plane(1, 3)
+        if k == 1:
+            gw.plane(2)
+            gw.share(1)
+            gw.share(2)
+        if k == 2:
+            gw.corner(0, 1, 3)
+        if k == 3:
+            gw.corner(2)
+            gw.share(3)
+            gw.finish()
 
     pl.when(first)(enter if direct else clear)
 
@@ -408,27 +481,26 @@
         img_hat = (img_ref[r0 : r0 + rl, :].astype(f32) - mean) * inv
         r.imglow[r0 : r0 + rl, :] = (img_hat * gb + bb).astype(bf)
     for r0 in range(0, T, 256):
-        q = dg(r.tag[r0 : r0 + 256, :], r.wq[:, 0:D], 1, 0).astype(bf) * bf(1.0 / math.sqrt(hd))
+        q = dg(r.tag[r0 : r0 + 256, :], w_qkv(0, D), 1, 0).astype(bf) * bf(1.0 / math.sqrt(hd))
         r.q[r0 : r0 + 256, :] = q
         r.qT[:, r0 : r0 + 256] = q.T
     key_parts = tuple((r0, 256) for r0 in range(0, T, 256)) + tuple((T + r0, rl) for r0, rl in img_parts)
-    for j, dst in enumerate((r.kall, r.vall)):
-        w = r.wq[:, (j + 1) * D : (j + 2) * D]
-        for k0, kl in key_parts:
-            rows = r.tag[k0 : k0 + kl, :] if k0 < T else r.imglow[k0 - T : k0 - T + kl, :]
-            a = dg(rows, w, 1, 0).astype(bf)
-            dst[k0 : k0 + kl, :] = a
-            if j == 1:
-                r.xT[:, k0 : k0 + kl] = a.T
+    for k0, kl in key_parts:
+        if direct and k0 == T:
+            pl.when(first)(gather_column)
+        rows = r.tag[k0 : k0 + kl, :] if k0 < T else r.imglow[k0 - T : k0 - T + kl, :]
+        for p in range(HEADS // 2):
+            a = dg(rows, w_qkv(D + p * 4 * hd, D + (p + 1) * 4 * hd), 1, 0).astype(bf)
+            ps = slice(p * 2 * hd, (p + 1) * 2 * hd)
+            r.kall[k0 : k0 + kl, ps] = a[:, 0 : 2 * hd]
+            r.vall[k0 : k0 + kl, ps] = a[:, 2 * hd :]
+            r.xT[ps, k0 : k0 + kl] = a[:, 2 * hd :].T
     for ref, k0 in ((r.bias0, 0), (r.bias1, 256)):
         ji = k0 + lax.broadcasted_iota(jnp.int32, ref.shape, 0)
         ii = k0 + lax.broadcasted_iota(jnp.int32, ref.shape, 1)
         ref[...] = jnp.where((ji <= ii) & (ji < count), 3e38, NEG).astype(bf)
 
-    if direct:
-        pl.when(first)(functools.partial(gather_step, 0))
-
-    chunks = [(0, 256, 0), (256, 256, 256), (512, 256, 0), (768, 256, 0), (1024, NK - 1024, 0)]
+    chunks = [(512, 400, 0), (0, 256, 0), (256, 256, 256), (912, NK - 912, 0)]
     nc = len(chunks)
     row64 = lax.broadcasted_iota(jnp.int32, (2 * hd, 1), 0)
     lane64 = lax.broadcasted_iota(jnp.int32, (1, 2 * hd), 1)
@@ -488,27 +560,34 @@
         r.rl[2 * p + b] = rl
         return m2
 
-    def fwd_pair(p, m):
+    def fwd_pair(hooks, p, m):
         m = head(p, 0, m, (p, 1))
         m = head(p, 1, m, (jnp.minimum(p + 1, HEADS // 2 - 1), 0))
-        if direct:
-            pl.when(first & (p == 1))(functools.partial(gather_step, 1))
-            pl.when(first & (p == HEADS // 2 - 1))(functools.partial(gather_step, 2))
+        if hooks:
+            for k in range(HEADS // 2):
+                pl.when(p == k)(functools.partial(gather_step, k))
         return m
 
-    qz = query(0, 0)
-    m = None
-    for c in range(nc):
-        mc = score(0, 0, c, qz)
-        m = mc if m is None else jnp.maximum(m, mc)
-    lax.fori_loop(0, HEADS // 2, fwd_pair, m)
+    def forward(hooks):
+        qz = query(0, 0)
+        m = None
+        for c in range(nc):
+            mc = score(0, 0, c, qz)
+            m = mc if m is None else jnp.maximum(m, mc)
+        lax.fori_loop(0, HEADS // 2, functools.partial(fwd_pair, hooks), m)
+
+    if direct:
+        pl.when(first)(functools.partial(forward, True))
+        pl.when(jnp.logical_not(first))(functools.partial(forward, False))
+    else:
+        forward(False)
 
     RC = 256
     zero = jnp.zeros((1, D), f32)
 
     def rows_part(r0):
         rs = pl.ds(r0, RC)
-        hp = r.tag[rs, :].astype(f32) + dg(r.attT[:, rs], wout_ref[...], 0, 0)
+        hp = r.tag[rs, :].astype(f32) + dg(r.attT[:, rs], w_out(), 0, 0)
         yield
         c = hp - jnp.mean(hp, -1, keepdims=True)
         inv1 = lax.rsqrt(jnp.mean(c * c, -1, keepdims=True) + EPS)
@@ -517,7 +596,7 @@
         hl = hidden.astype(bf)
         r.hidlow[rs, :] = hl
         yield
-        pre = dg(hl, wup_ref[...], 1, 0)
+        pre = dg(hl, w_up(), 1, 0)
         yield
         p2 = pre * pre
         th = jnp.tanh(GC * (pre + GA * (p2 * pre)))
@@ -525,7 +604,7 @@
         r.act[rs, :] = act
         gp = 0.5 * (1.0 + th) + 0.5 * pre * (1.0 - th * th) * (GC * (1.0 + 3 * GA * p2))
         yield
-        resid = hidden + dg(act, r.wd[...], 1, 0)
+        resid = hidden + dg(act, w_down(), 1, 0)
         yield
         c = resid - jnp.mean(resid, -1, keepdims=True)
         inv2 = lax.rsqrt(jnp.mean(c * c, -1, keepdims=True) + EPS)
@@ -540,22 +619,22 @@
         rlow = gr.astype(bf)
         r.rlow[rs, :] = rlow
         yield
-        gact = dg(rlow, r.wd[...], 1, 1)
+        gact = dg(rlow, w_down(), 1, 1)
         yield
         plow = (gact * gp).astype(bf)
         r.plow[rs, :] = plow
         yield
-        gh = gr + dg(plow, wup_ref[...], 1, 1)
+        gh = gr + dg(plow, w_up(), 1, 1)
         yield
         r.terms[0:1, :] += jnp.sum(gh * hat1, 0, keepdims=True)
         r.terms[1:2, :] += jnp.sum(gh, 0, keepdims=True)
         s = gh * g1
         ghp = inv1 * (s - jnp.mean(s, -1, keepdims=True) - hat1 * jnp.mean(s * hat1, -1, keepdims=True))
-        r.gtags[rs, :] = ghp
+        r.ghp[rs, :] = ghp
         hpl = ghp.astype(bf)
         r.hplow[rs, :] = hpl
         yield
-        r.dOT[:, rs] = dg(hpl, wout_ref[...], 1, 1).astype(bf).T
+        r.dOT[:, rs] = dg(hpl, w_out(), 1, 1).astype(bf).T
         yield
 
     parts = [rows_part(r0) for r0 in range(0, T, RC)]
@@ -591,15 +670,15 @@
         put(r.gr0, r.aout, r0, 256, 0, D, dg(r.attT[r0 : r0 + 256, :], r.hplow[...], 1, 0))
         for c0, cn, dst, col in ((0, 256, r.gr0, D), (256, 512, r.gr1, 0), (768, F - 768, r.gr1, 512)):
             put(dst, r.aup, r0, 256, c0, cn, dg(r.hidlow[:, r0 : r0 + 256], r.plow[:, c0 : c0 + cn], 0, 0), col)
-    when_last(sd.core, sr0.core, sr1.core, sd.plane1) if direct else None
-
-    def bwd_pair(p, _):
+    when_last(sr0.core, sr1.core, sd.core) if direct else None
+
+    def bwd_pair(hooks, p, _):
         p128 = mo(p * 2 * hd, 2 * hd)
         ps = pl.ds(p128, 2 * hd)
         dq = [None, None]
         ops = [(own_rows(r.dOT[ps, :], b), own_lanes(r.dO[:, ps], b), own_lanes(r.q[:, ps], b)) for b in range(2)]
-        kc = pl.ds(mo(D + p128, 128), 2 * hd)
-        vc = pl.ds(mo(2 * D + p128, 128), 2 * hd)
+        tc = pl.ds(mo(D + 2 * p128, 256), 4 * hd)
+        ic = pl.ds(mo(2 * p128, 256), 4 * hd)
         for c in range(nc):
             k0, kl, q0 = chunks[c]
             ks = slice(k0, k0 + kl)
@@ -616,49 +695,71 @@
                 dqc = fullq(dg(r.xT[hs, ks], ds, 1, 0), q0, 0.0)
                 dk, dv = (dkc, dvc) if dk is None else (dk + dkc, dv + dvc)
                 dq[b] = dqc if dq[b] is None else dq[b] + dqc
+            dkv = jnp.concatenate([dk.astype(bf), dv.astype(bf)], 1)
             if k0 < T:
-                r.dqkv[ks, kc] = dk.astype(bf)
-                r.dqkv[ks, vc] = dv.astype(bf)
+                r.dqkv[ks, tc] = dkv
             else:
-                si = slice(k0 - T, k0 - T + kl)
-                r.dkvi[si, ps] = dk.astype(bf)
-                r.dkvi[si, kc] = dv.astype(bf)
+                r.dkvi[k0 - T : k0 - T + kl, ic] = dkv
+            if hooks and c == 1:
+                at_pair(p, halfway)
         for b in range(2):
             hs = pl.ds(mo(p * 2 * hd + b * hd, hd), hd)
             r.dqT[hs, :] = (dq[b] * (1.0 / math.sqrt(hd))).astype(bf)
-        if direct:
-            for k, steps in enumerate(
-                ((sr0.plane1, sr1.plane1), (sd.plane2,), (sr1.plane2, sq0.plane1, sd.column), (sr0.column,))
-            ):
-
-                @pl.when(last & (p == k))
+        if hooks:
+            at_pair(p, after)
+        for i in range(3):
+
+            @pl.when(p == i + 1)
+            def _():
+                qkv_piece(i)
+                if hooks:
+                    (sq0, sq1, sq2)[i].core()
+
+        return 0
+
+    if direct:
+        halfway = ((sr0.plane1,), (sd.plane1,), (sr1.plane2,), (sd.plane2, sr0.column, sq1.plane1))
+        after = ((sr1.plane1,), (sr0.plane2,), (sq0.plane1,), (sr1.column,))
+
+    def at_pair(p, todo):
+        for k, steps in enumerate(todo):
+            if steps:
+
+                @pl.when(p == k)
                 def _():
                     for step in steps:
                         step()
 
-        return 0
-
-    for i, gq in enumerate((r.gq0, r.gq1)):
-        lax.fori_loop(i * half, (i + 1) * half, bwd_pair, 0)
-        hc = slice(i * HC, (i + 1) * HC)
-        r.dqkv[:, hc] = r.dqT[hc, :].T
+    def qkv_piece(i):
+        gq = (r.gq0, r.gq1, r.gq2)[i]
+        a, b = ((0, 2), (2, 3), (3, 4))[i]
+        qc = slice(a * 2 * hd, b * 2 * hd)
+        kc = slice(a * 4 * hd, b * 4 * hd)
+        tc = slice(D + kc.start, D + kc.stop)
+        n = qc.stop - qc.start
+        r.dqkv[:, qc] = r.dqT[qc, :].T
         for r0 in range(0, D, 256):
             rs = slice(r0, r0 + 256)
             x = r.tag[:, rs]
-            put(gq, r.aqkv, r0, 256, i * HC, HC, dg(x, r.dqkv[:, hc], 0, 0), 0)
-            for j in (1, 2):
-                cs = slice(j * D + i * HC, j * D + (i + 1) * HC)
-                ci = slice(cs.start - D, cs.stop - D)
-                add = dg(x, r.dqkv[:, cs], 0, 0) + dg(r.imglow[:, rs], r.dkvi[:, ci], 0, 0)
-                put(gq, r.aqkv, r0, 256, cs.start, HC, add, j * HC)
-        if direct:
-            when_last(*((sq0.core, sr0.plane2), (sq1.core,))[i])
+            put(gq, r.aqkv, r0, 256, qc.start, n, dg(x, r.dqkv[:, qc], 0, 0), 0)
+            add = dg(x, r.dqkv[:, tc], 0, 0) + dg(r.imglow[:, rs], r.dkvi[:, kc], 0, 0)
+            put(gq, r.aqkv, r0, 256, tc.start, 2 * n, add, n)
+
+    def backward(hooks):
+        lax.fori_loop(0, HEADS // 2, functools.partial(bwd_pair, hooks), 0)
+
+    if direct:
+        pl.when(last)(functools.partial(backward, True))
+        pl.when(jnp.logical_not(last))(functools.partial(backward, False))
+    else:
+        backward(False)
+
 
     sg = jnp.zeros((1, D), f32)
     sb = sg
     for r0, rl in img_parts:
         rs = slice(r0, r0 + rl)
-        gz = dg(r.dkvi[rs, :], r.wq[:, D:], 1, 1)
+        gz = dg(r.dkvi[rs, :], w_qkv(D, 3 * D), 1, 1)
         r.gz[rs, :] = gz.astype(bf)
         hat = (img_ref[rs, :].astype(f32) - mean) * inv
         sg += jnp.sum(gz * hat, 0, keepdims=True)
@@ -674,30 +775,32 @@
             sq0.plane2()
 
     for r0 in range(0, T, 256):
-        r.gtags[r0 : r0 + 256, :] += dg(r.dqkv[r0 : r0 + 256, :], r.wq[...], 1, 1)
+        total = r.ghp[r0 : r0 + 256, :] + dg(r.dqkv[r0 : r0 + 256, :], w_qkv(0, 3 * D), 1, 1)
+        r.gtags[r0 : r0 + 256, :] = total.astype(bf)
 
     if direct:
 
         @pl.when(last)
         def _():
-            sq1.plane1()
             sm.step(1)
-            sr1.column()
-            sq = sd.finish()
-            sq += sr0.finish()
+            sq2.plane1()
+            sd.column()
+            sq = sr0.finish()
+            sq1.plane2()
+            sq += sr1.finish()
             sm.step(2)
             sq0.column()
-            sq += sr1.finish()
-            sq1.plane2()
-            sm.step(3)
+            sq2.column()
+            sq1.column()
+            sq += sd.finish()
             sq += sq0.finish()
-            sq1.column()
             sm.finish(r.small)
+            sq += sq1.finish()
             tot = r.small[...]
-            sq += sq1.finish()
+            r.small[6:7, :] = jnp.full((1, D), me.d, jnp.int32).astype(f32)
+            sq += sq2.finish()
             r.nb[me.d] = jnp.full((1, 128), sq, f32)
             push_all(me, r.nb, r.ps.at[0], r.ps.at[1])
-            push_done(me, r.nb, r.ps.at[0], r.ps.at[1])
             r.nsq[...] = jnp.broadcast_to(jnp.sum(r.nb[...], 0) + jnp.sum(tot * tot), (8, 128))
 
 
@@ -727,40 +830,40 @@
         ins += [(k, whole(a.shape, **one)) for k, a in zip(("stats", "gains", "wq", "wr", "wd"), params)]
     outs = [
         ("mixed", S((n * T, D), bf), row(T, D)),
-        ("gtags", S((n * T, D), f32), row(T, D)),
+        ("gtags", S((n * T, D), bf), row(T, D)),
         ("gz", S((n * I, D), bf), row(I, D)),
     ]
     scratch = [
         ("imglow", V(I, D)), ("kall", V(NK, D)), ("vall", V(NK, D)), ("xT", V(D, NK)),
         ("q", V(T, D)), ("qT", V(D, T)), ("bias0", V(256, T)), ("bias1", V(256, T - 256)), ("s", V(NK, T, d=f32)),
         ("e", V(HEADS, NK - 256, T)), ("e1", V(HEADS, 256, T - 256)), ("attT", V(D, T)),
-        ("rl", V(HEADS, 1, T, d=f32)), ("plow", V(T, F)),
+        ("rl", V(HEADS, 1, T, d=f32)), ("plow", V(T, F)), ("ghp", V(T, D, d=f32)),
         ("dqkv", V(T, 3 * D)), ("dkvi", V(I, 2 * D)), ("dO", V(T, D)),
         ("dOT", V(D, T)), ("delta", V(HEADS, 1, T, d=f32)), ("aqkv", V(D, 3 * D, d=f32)), ("aout", V(D, D, d=f32)),
         ("aup", V(D, F, d=f32)), ("adn", V(F, D, d=f32)),
     ]
     if direct:
         outs += [
-            ("oq0", S((R, 3 * HC), f32), None), ("oq1", S((R, 3 * HC), f32), None), ("or0", S((R, 3 * HC), f32), None),
+            ("oq0", S((R, 3 * HC), f32), None), ("oq1", S((R, 3 * HC // 2), f32), None), ("oq2", S((R, 3 * HC // 2), f32), None), ("or0", S((R, 3 * HC), f32), None),
             ("or1", S((R, D + F - 3 * HC), f32), None), ("od", S((RD, D), f32), None), ("small", S((8, D), f32), None), ("nsq", S((8, 128), f32), None),
             ("stats", S((2, D), f32), None), ("gains", S((8, D), f32), None),
         ]
         dims = (4, 2, 2, 2)
         dma = pltpu.SemaphoreType.DMA
         scratch += [
-            ("img", V(n * I, D)), ("wq", V(D, 3 * D)), ("wr", V(D, D + F)), ("wd", V(F, D)), ("sb", V(10, 8, D, d=f32)),
+            ("img", V(n * I, D)), ("wq", V(*dims, R, 3 * D)), ("ww", V(*dims, R, 3 * D + F)), ("sb", V(10, 8, D, d=f32)),
             ("nb", V(32, 1, 128, d=f32)), ("terms", V(8, D, d=f32)), ("tb", V(10, 8, D, d=f32)),
-            ("gq0", V(*dims, R, 3 * HC)), ("gq1", V(*dims, R, 3 * HC)), ("gr0", V(*dims, R, 3 * HC)),
+            ("gq0", V(*dims, R, 3 * HC)), ("gq1", V(*dims, R, 3 * HC // 2)), ("gq2", V(*dims, R, 3 * HC // 2)), ("gr0", V(*dims, R, 3 * HC)),
             ("gr1", V(*dims, R, D + F - 3 * HC)), ("gd", V(*dims, RD, D)),
-            ("bq0", Scatter.bufs(R, 3 * HC)), ("bq1", Scatter.bufs(R, 3 * HC)), ("br0", Scatter.bufs(R, 3 * HC)),
+            ("bq0", Scatter.bufs(R, 3 * HC)), ("bq1", Scatter.bufs(R, 3 * HC // 2)), ("bq2", ScatterPlane.bufs(R, 3 * HC // 2)), ("br0", Scatter.bufs(R, 3 * HC)),
             ("br1", Scatter.bufs(R, D + F - 3 * HC)),
             ("bd", Scatter.bufs(RD, D)),
-            ("isem", dma), ("gs", dma((6, Gather.SLOTS))), ("cs", dma((14, Scatter.SLOTS))), ("ps", dma((2, 32))),
+            ("isem", dma), ("gs", dma((4, Gather.SLOTS))), ("cs", dma((16, Scatter.SLOTS))), ("ps", dma((2,))),
         ]
         extra = dict(collective_id=0, has_side_effects=True)
     else:
         outs += [
-            ("gq0", S((D, 3 * HC), bf), None), ("gq1", S((D, 3 * HC), bf), None), ("gr0", S((D, 3 * HC), bf), None),
+            ("gq0", S((D, 3 * HC), bf), None), ("gq1", S((D, 3 * HC // 2), bf), None), ("gq2", S((D, 3 * HC // 2), bf), None), ("gr0", S((D, 3 * HC), bf), None),
             ("gr1", S((D, D + F - 3 * HC), bf), None),
             ("gd", S((F, D), bf), None), ("terms", S((8, D), f32), None),
         ]
@@ -776,19 +879,19 @@
             out_specs=[whole(s.shape) if b is None else b for _, s, b in outs],
             scratch_shapes=[a for _, a in scratch],
         ),
-        compiler_params=pltpu.CompilerParams(vmem_limit_bytes=63 * 2**20, **extra),
+        compiler_params=pltpu.CompilerParams(vmem_limit_bytes=255 * 2**18, **extra),
         name="tables",
     )(counts, tag, img, cot, *params)
 
 
-def update_kernel(n_params, parts, place, gz_in, img_in, stats_ref, gains_ref, small_ref, nsq_ref, *refs):
-    n_in = 5 + 3 * n_params
+def update_kernel(n_params, parts, total_rows, gz_in, img_in, stats_ref, gains_ref, small_ref, nsq_ref, *refs):
+    n_in = 6 + 3 * n_params
     n_out = 5 * n_params
     hbm_in, (mixed_in, gtags_in), refs = refs[:n_in], refs[n_in : n_in + 2], refs[n_in + 2 :]
     (mixed_out, gtags_out, gimg_out, norm_ref), refs = refs[:4], refs[4:]
     hbm_out, refs = refs[:n_out], refs[n_out:]
     ins, outs, refs = refs[:n_in], refs[n_in : n_in + n_out], refs[n_in + n_out :]
-    mixed, gtags, gz, img, gimg, in_sem, out_sem, pass_sem, part_sem = refs
+    mixed, gtags_low, gtags, gz, img, gimg, in_sem, out_sem, pass_sem, part_sem = refs
     rows, D = gz.shape
     copy = pltpu.make_async_copy
 
@@ -804,12 +907,11 @@
         _, a, b = part(i)
         a.start()
         b.start()
-    for i, (a, b) in enumerate(((gtags_in, gtags), (mixed_in, mixed))):
+    for i, (a, b) in enumerate(((gtags_in, gtags_low), (mixed_in, mixed))):
         copy(a, b, pass_sem.at[i]).start()
     for i, (a, b) in enumerate(zip(hbm_in, ins)):
         copy(a, b, in_sem.at[i]).start()
 
-    total_rows = place[1].astype(f32)
     gb = gains_ref[4:5, :]
     k = stats_ref[1:2, :] * gb
     gsum = small_ref[4:5, :] / total_rows
@@ -821,26 +923,32 @@
         hat = (img[at, :].astype(f32) - stats_ref[0:1, :]) * stats_ref[1:2, :]
         gimg[at, :] = k * (gz[at, :].astype(f32) - bsum - hat * gsum)
         given(i).start()
-    for i, (a, b, c) in enumerate(((gtags_in, gtags, gtags_out), (mixed_in, mixed, mixed_out))):
-        copy(a, b, pass_sem.at[i]).wait()
-        copy(b, c, pass_sem.at[2 + i]).start()
+    copy(mixed_in, mixed, pass_sem.at[1]).wait()
+    copy(mixed, mixed_out, pass_sem.at[3]).start()
+    copy(gtags_in, gtags_low, pass_sem.at[0]).wait()
+    gtags[...] = gtags_low[...].astype(f32)
+    copy(gtags, gtags_out, pass_sem.at[2]).start()
 
     for i, (a, b) in enumerate(zip(hbm_in, ins)):
         copy(a, b, in_sem.at[i]).wait()
-    oq0, oq1, or0, or1, od = ins[:5]
-    masters, firsts, seconds = (ins[5 + n_params * i : 5 + n_params * (i + 1)] for i in range(3))
+    oq0, oq1, oq2, or0, or1, od = ins[:6]
+    masters, firsts, seconds = (ins[6 + n_params * i : 6 + n_params * (i + 1)] for i in range(3))
     total_norm = jnp.sqrt(nsq_ref[0:1, 0:1])
     norm_ref[...] = total_norm
     factor = CLIP_AT / jnp.maximum(total_norm, CLIP_AT)
     cols = masters[4].shape[1]
     row = lax.broadcasted_iota(jnp.int32, (D, cols), 0)
     col = lax.broadcasted_iota(jnp.int32, (D, cols), 1)
-    pick = (row == col + place[0] * cols).astype(f32)
+    first = small_ref[6:7, 0:cols].astype(jnp.int32) * cols
+    pick = (row == col + first).astype(f32)
     own = lax.dot_general(
         small_ref[...], pick, (((1,), (0,)), ((), ())), precision=lax.Precision.HIGHEST, preferred_element_type=f32
     )[0:6]
-    hc = D // 2
-    oq = [o[:, j * hc : (j + 1) * hc] for j in range(3) for o in (oq0, oq1)]
+    pc = D // 4
+    oq = [oq0[:, 0 : 2 * pc], oq1[:, 0:pc], oq2[:, 0:pc]]
+    for j in (0, 1):
+        oq += [oq0[:, (2 + j) * pc : (3 + j) * pc], oq0[:, (4 + j) * pc : (5 + j) * pc]]
+        oq += [o[:, (1 + j) * pc : (2 + j) * pc] for o in (oq1, oq2)]
     grads = (jnp.concatenate(oq, 1), or0[:, 0:D], jnp.concatenate([or0[:, D:], or1[...]], 1), od[...], own)
     rates = (RATE_MATRIX, RATE_OUTPUT, RATE_MATRIX, RATE_MATRIX, RATE_NORMS)
     for i, (g, w, f, v) in enumerate(zip(grads, masters, firsts, seconds)):
@@ -865,7 +973,7 @@
         given(i).wait()
 
 
-def update(place, mixed, gtags, gz, img, stats, gains, small, nsq, owned, masters, firsts, seconds):
+def update(total_rows, mixed, gtags, gz, img, stats, gains, small, nsq, owned, masters, firsts, seconds):
     rows = gz.shape[0]
     parts = 7 if rows % 112 == 0 else 3
     anywhere = pl.BlockSpec(memory_space=pl.ANY)
@@ -874,17 +982,17 @@
     shapes = [jax.ShapeDtypeStruct(m.shape, f32) for m in masters] * 4 + [jax.ShapeDtypeStruct(m.shape, bf) for m in masters]
     gimg = jax.ShapeDtypeStruct(gz.shape, f32)
     dma = pltpu.SemaphoreType.DMA
-    passed = [jax.ShapeDtypeStruct(a.shape, a.dtype) for a in (mixed, gtags)]
+    passed = [jax.ShapeDtypeStruct(mixed.shape, bf), jax.ShapeDtypeStruct(gtags.shape, f32)]
     return pl.pallas_call(
-        functools.partial(update_kernel, len(masters), parts),
+        functools.partial(update_kernel, len(masters), parts, total_rows),
         out_shape=passed + [gimg, jax.ShapeDtypeStruct((1, 1), f32)] + shapes,
-        in_specs=[pl.BlockSpec(memory_space=pltpu.SMEM)] + [anywhere] * 2 + [VM] * 4 + [anywhere] * (len(manual) + 2),
+        in_specs=[anywhere] * 2 + [VM] * 4 + [anywhere] * (len(manual) + 2),
         out_specs=[anywhere] * 3 + [VM] + [anywhere] * len(shapes),
-        scratch_shapes=[pltpu.VMEM(a.shape, a.dtype) for a in manual + tuple(shapes) + tuple(passed) + (gz, img, gimg)]
+        scratch_shapes=[pltpu.VMEM(a.shape, a.dtype) for a in manual + tuple(shapes) + (mixed, gtags, passed[1], gz, img, gimg)]
         + [dma((len(manual),)), dma((len(shapes),)), dma((4,)), dma((3, parts))],
         compiler_params=pltpu.CompilerParams(vmem_limit_bytes=63 * 2**20),
         name="update",
-    )(place, gz, img, *windows, *manual, mixed, gtags)
+    )(gz, img, *windows, *manual, mixed, gtags)
 
 
 def gather_any(img, wqkv, wout, wup, wdn, norm):
@@ -896,15 +1004,19 @@
     mean = lax.psum(jnp.sum(values, 0), AXES) / total
     centred = values - mean
     spread = lax.psum(jnp.sum(centred * centred, 0), AXES) / total
-    return full(wqkv, 0), gr, full(wdn, 0), jnp.stack([mean, lax.rsqrt(spread + EPS)]), gains
-
-
-def scatter_any(gq0, gq1, gr0, gr1, gd, terms):
+    D = img.shape[1]
+    wq = full(wqkv, 0)
+    kv = [wq[:, D:].reshape(D, 2, HEADS // 2, -1)[:, j, p] for p in range(HEADS // 2) for j in (0, 1)]
+    return jnp.concatenate([wq[:, 0:D]] + kv, 1), gr, full(wdn, 0), jnp.stack([mean, lax.rsqrt(spread + EPS)]), gains
+
+
+def scatter_any(gq0, gq1, gq2, gr0, gr1, gd, terms):
     part = lambda a: lax.psum_scatter(a.astype(f32), AXES, scatter_dimension=0, tiled=True)
-    owned = [part(a) for a in (gq0, gq1, gr0, gr1, gd)]
+    owned = [part(a) for a in (gq0, gq1, gq2, gr0, gr1, gd)]
     small = lax.psum(terms, AXES)
     local = sum(jnp.sum(a * a) for a in owned)
     nsq = lax.psum(local, AXES) + jnp.sum(small * small)
+    small = small.at[6].set(lax.axis_index(AXES).astype(f32))
     return *owned, small, jnp.full((8, 128), nsq, f32)
 
 
@@ -923,9 +1035,8 @@
             False, tag_counts, tag_inputs, image_inputs, cotangent, (stats, gains, wq, wr, wd)
         )
         *owned, small, nsq = scatter_any(*sums)
-    place = jnp.stack([lax.axis_index(AXES), jnp.int32(total_rows)])
     mixed, gtags, gimg, norm, *rest = update(
-        place, mixed, gtags, gz, image_inputs, stats, gains, small, nsq, owned, masters, firsts, seconds
+        total_rows, mixed, gtags, gz, image_inputs, stats, gains, small, nsq, owned, masters, firsts, seconds
     )
     return (mixed, gtags, gimg, norm.reshape(()), *rest)
 

time: 162 us -> 152 us (0.938)
  Pallas kernels: 160 us -> 151 us
    pallas_call x1, Pallas kernels: 150 us -> 141 us  [tables_call(): pl.pallas_call(functools.partial(tables_kernel, direct, names), out_shape...]
where the time goes in v4:
time: 152 us; the launch traced here: 151 us
  Pallas kernels  151 us (99%)
    pallas_call x1, Pallas kernels, tables_call(): pl.pallas_call(functools.partial(tables_kernel, direct, names), out_shape...  141 us
    pallas_call x1, Pallas kernels, update(): pl.pallas_call(functools.partial(update_kernel, len(masters), parts, tota...  9.75 us

profile of v4, /device:TPU:0, one launch (start us, length us, event | category | flops | bytes accessed | tf_op | source)
XLA Modules:
  0.0 151.5 jit_solution(12996273766850365395)
XLA Ops:
  0.7 140.9 %tables.1 = (bf16[1536,512]{1,0:T(8,128)(2,1)}, bf16[1536,512]{1,0:T(8,128)(2,1)}, bf16[2352,512]{1,0:T(8,128)(2,1)}, f32[16,768]{1,0:T(8,128)}, f32[16,384]{1,0...) custom-call(s32[3]{0:T(128)} %refs_0_.1, ...), custom_call_target="tpu_custom_call" | custom-call | tf_op jit(solution)/shard_map/tables/pallas_call | solution.py:872
  141.6 9.8 %update.1 = (bf16[1536,512]{1,0:T(8,128)(2,1)}, f32[1536,512]{1,0:T(8,128)}, f32[2352,512]{1,0:T(8,128)}, f32[1,1]{1,0:T(1,128)}, f32[16,1536]{1,0:T(8,128)}, /*...) custom-call(bf16[2352,512]{1,0:T(8,128)(2,1)} %get-tuple-element.71., ...), custom_call_target="tpu_custom_call" | custom-call | tf_op jit(solution)/shard_map/update/pallas_call | solution.py:986

commit v5 on v4

--- a/solution.py
+++ b/solution.py
@@ -346,7 +346,7 @@
     NK = T + I
     hd = D // HEADS
     F = r.plow.shape[1]
-    r.hidlow, r.rlow, r.hplow = (r.dqkv.at[:, i * D : (i + 1) * D] for i in range(3))
+    r.hidlow, r.rlow = (r.dqkv.at[:, i * D : (i + 1) * D] for i in range(2))
     r.act = r.dkvi.at[0:T]
     r.dqT = r.attT
     count = r.counts[t]
@@ -630,7 +630,6 @@
         r.terms[1:2, :] += jnp.sum(gh, 0, keepdims=True)
         s = gh * g1
         ghp = inv1 * (s - jnp.mean(s, -1, keepdims=True) - hat1 * jnp.mean(s * hat1, -1, keepdims=True))
-        r.ghp[rs, :] = ghp
         hpl = ghp.astype(bf)
         r.hplow[rs, :] = hpl
         yield
@@ -682,18 +681,14 @@
         for c in range(nc):
             k0, kl, q0 = chunks[c]
             ks = slice(k0, k0 + kl)
-            dk = None
+            dps = [dg(r.vall[ks, ps], ops[b][0][:, q0:], 1, 0) for b in range(2)]
+            es = [e_at(2 * p + b, c)[...] for b in range(2)]
+            dv = dg(es[0], ops[0][1][q0:, :], 1, 0) + dg(es[1], ops[1][1][q0:, :], 1, 0)
+            dss = [(es[b].astype(f32) * (dps[b] - r.delta[2 * p + b][:, q0:])).astype(bf) for b in range(2)]
+            dk = dg(dss[0], ops[0][2][q0:, :], 1, 0) + dg(dss[1], ops[1][2][q0:, :], 1, 0)
             for b in range(2):
-                h = 2 * p + b
                 hs = pl.ds(mo(p * 2 * hd + b * hd, hd), hd)
-                dOz, dOl, ql = ops[b]
-                dp = dg(r.vall[ks, ps], dOz[:, q0:], 1, 0)
-                e = e_at(h, c)[...]
-                ds = (e.astype(f32) * (dp - r.delta[h][:, q0:])).astype(bf)
-                dvc = dg(e, dOl[q0:, :], 1, 0)
-                dkc = dg(ds, ql[q0:, :], 1, 0)
-                dqc = fullq(dg(r.xT[hs, ks], ds, 1, 0), q0, 0.0)
-                dk, dv = (dkc, dvc) if dk is None else (dk + dkc, dv + dvc)
+                dqc = fullq(dg(r.xT[hs, ks], dss[b], 1, 0), q0, 0.0)
                 dq[b] = dqc if dq[b] is None else dq[b] + dqc
             dkv = jnp.concatenate([dk.astype(bf), dv.astype(bf)], 1)
             if k0 < T:
@@ -775,7 +770,7 @@
             sq0.plane2()
 
     for r0 in range(0, T, 256):
-        total = r.ghp[r0 : r0 + 256, :] + dg(r.dqkv[r0 : r0 + 256, :], w_qkv(0, 3 * D), 1, 1)
+        total = r.hplow[r0 : r0 + 256, :].astype(f32) + dg(r.dqkv[r0 : r0 + 256, :], w_qkv(0, 3 * D), 1, 1)
         r.gtags[r0 : r0 + 256, :] = total.astype(bf)
 
     if direct:
@@ -837,7 +832,7 @@
         ("imglow", V(I, D)), ("kall", V(NK, D)), ("vall", V(NK, D)), ("xT", V(D, NK)),
         ("q", V(T, D)), ("qT", V(D, T)), ("bias0", V(256, T)), ("bias1", V(256, T - 256)), ("s", V(NK, T, d=f32)),
         ("e", V(HEADS, NK - 256, T)), ("e1", V(HEADS, 256, T - 256)), ("attT", V(D, T)),
-        ("rl", V(HEADS, 1, T, d=f32)), ("plow", V(T, F)), ("ghp", V(T, D, d=f32)),
+        ("rl", V(HEADS, 1, T, d=f32)), ("plow", V(T, F)), ("hplow", V(T, D)),
         ("dqkv", V(T, 3 * D)), ("dkvi", V(I, 2 * D)), ("dO", V(T, D)),
         ("dOT", V(D, T)), ("delta", V(HEADS, 1, T, d=f32)), ("aqkv", V(D, 3 * D, d=f32)), ("aout", V(D, D, d=f32)),
         ("aup", V(D, F, d=f32)), ("adn", V(F, D, d=f32)),

time: 152 us -> 149 us (0.980)
  Pallas kernels: 151 us -> 148 us
    pallas_call x1, Pallas kernels: 141 us -> 138 us  [tables_call(): pl.pallas_call(functools.partial(tables_kernel, direct, names), out_shape...]
where the time goes in v5:
time: 149 us
  Pallas kernels  148 us (99%)
    pallas_call x1, Pallas kernels, tables_call(): pl.pallas_call(functools.partial(tables_kernel, direct, names), out_shape...  138 us
    pallas_call x1, Pallas kernels, update(): pl.pallas_call(functools.partial(update_kernel, len(masters), parts, tota...  9.75 us

profile of v5, /device:TPU:0, one launch (start us, length us, event | category | flops | bytes accessed | tf_op | source)
XLA Modules:
  0.0 148.7 jit_solution(7105297703668608634)
XLA Ops:
  0.7 138.1 %tables.1 = (bf16[1536,512]{1,0:T(8,128)(2,1)}, bf16[1536,512]{1,0:T(8,128)(2,1)}, bf16[2352,512]{1,0:T(8,128)(2,1)}, f32[16,768]{1,0:T(8,128)}, f32[16,384]{1,0...) custom-call(s32[3]{0:T(128)} %refs_0_.1, ...), custom_call_target="tpu_custom_call" | custom-call | tf_op jit(solution)/shard_map/tables/pallas_call | solution.py:867
  138.8 9.8 %update.1 = (bf16[1536,512]{1,0:T(8,128)(2,1)}, f32[1536,512]{1,0:T(8,128)}, f32[2352,512]{1,0:T(8,128)}, f32[1,1]{1,0:T(1,128)}, f32[16,1536]{1,0:T(8,128)}, /*...) custom-call(bf16[2352,512]{1,0:T(8,128)(2,1)} %get-tuple-element.71., ...), custom_call_target="tpu_custom_call" | custom-call | tf_op jit(solution)/shard_map/update/pallas_call | solution.py:981
